TPU v7x, 32 devices: a whole 2x2x4 slice. The times are simulated.
32 devices in a mesh: tgt: 8 (over y, x, core), src: 4 (over z).
Axes of the slice: x: 2, y: 2, z: 4, core: 2. Of those that a mesh axis runs over, the one named last changes fastest.
Arguments:
- incident: bfloat16 [128, 8, 2048], P(None, None, 'tgt'), may hold values from -6 to 6
- past_density: bfloat16 [76, 8, 2048], P(None, None, 'src'), may hold values from -6 to 6
- kernels: bfloat16 [8, 2048, 2048], P(None, 'src', 'tgt'), may hold values from -0.0625 to 0.0625
- lag_offset: int32 [8, 4, 12], P('tgt', 'src'), may hold values from 0 to 11, each once within a row
- lag_counts: int32 [8, 4], P('tgt', 'src'), may hold values from 2 to 8, as said below
- couplings: float32 [2, 2048, 256], P(None, 'tgt'), may hold values from -0.86 to 0.01
- inverse: float32 [2048, 256], P('tgt'), may hold values from -0.02 to 1.06
Outputs:
- densities: float32 [128, 8, 2048], P(None, None, 'tgt')
Inputs may be any that keep to these rules, and one draw needn't show every extreme that they name: `lag_counts`: each tile has between 2 and 8 nonzero retarded lags; in every draw some tile has 8.
All inputs are finite; a program needn't handle non-finite values.
Results may differ from a plain program's by a relative error of at most 0.0014.
Values may be sent and summed in bfloat16 or wider, within the bound.
No kernel may reach another device: no remote copies, remote signals or barrier semaphores. Data moves between devices by JAX's collectives and lax.ppermute only.
A program may use at most 64 MiB of HBM per device.

v0:
```python
import math

import jax
import jax.numpy as jnp
from jax import lax
from jax.sharding import PartitionSpec as P

BLOCK_STEPS = 64
BLOCKS = 2
HIST = 76
COUPLINGS = 2


precise = lax.Precision.HIGHEST


def spread(array, axis, root):
    mine = lax.axis_index(axis) == root
    return lax.psum(jnp.where(mine, array, jnp.zeros_like(array)), axis)


def far_partial(
    kernels, offsets, history, first_step, start_slot, end_slot, kernel_base, partial_sum
):
    column_size = history.shape[2]

    def add_slot(slot_index, running):
        lag_value = BLOCK_STEPS + offsets[slot_index]
        window = lax.dynamic_slice_in_dim(history, first_step - lag_value + HIST, BLOCK_STEPS, 0)
        kernel_block = lax.dynamic_index_in_dim(
            kernels, slot_index - kernel_base, 0, keepdims=False
        )
        return running + jnp.dot(
            window.reshape(-1, column_size), kernel_block, preferred_element_type=jnp.float32
        )

    return lax.fori_loop(start_slot, end_slot, add_slot, partial_sum)


def impulse_table(couplings, inverse, inner_steps):
    entries = [inverse]
    for delay_index in range(1, inner_steps):
        summed = jnp.zeros_like(inverse)
        for shift_lag in range(1, min(delay_index, COUPLINGS) + 1):
            summed = summed + jnp.dot(
                entries[delay_index - shift_lag], couplings[shift_lag - 1], precision=precise
            )
        entries.append(-jnp.dot(summed, inverse, precision=precise))
    return entries


def self_response(driving, earlier_steps, couplings, responses, inner_steps):
    row_size = driving.shape[2]
    load_count = driving.shape[1]
    grouped = driving.reshape(BLOCK_STEPS // inner_steps, inner_steps, load_count, row_size)

    def advance(earlier, driving_group):
        padded = jnp.concatenate(
            [earlier, jnp.zeros((inner_steps, load_count, row_size), jnp.float32)], 0
        )
        adjusted = driving_group
        for shift_lag in range(1, COUPLINGS + 1):
            lagged = padded[COUPLINGS - shift_lag : COUPLINGS - shift_lag + inner_steps]
            adjusted = adjusted - jnp.dot(
                lagged.reshape(-1, row_size), couplings[shift_lag - 1], precision=precise
            ).reshape(adjusted.shape)
        solved = jnp.zeros_like(adjusted)
        for delay_index in range(inner_steps):
            shifted = jnp.concatenate(
                [
                    jnp.zeros((delay_index, load_count, row_size), jnp.float32),
                    adjusted[: inner_steps - delay_index],
                ],
                0,
            )
            solved = solved + jnp.dot(
                shifted.reshape(-1, row_size), responses[delay_index], precision=precise
            ).reshape(adjusted.shape)
        return (solved[inner_steps - COUPLINGS :], solved)

    earlier_steps, solved_all = lax.scan(advance, earlier_steps, grouped)
    return (earlier_steps, solved_all.reshape(BLOCK_STEPS, load_count, row_size))


def local(incident, past_density, kernels, lag_offset, lag_counts, couplings, inverse):
    row_size = incident.shape[2]
    load_count = incident.shape[1]
    column_size = past_density.shape[2]
    ratio_groups = column_size // row_size
    source_count = lax.axis_size("src")
    repeats = max(source_count // load_count, 1)
    share = max(load_count // source_count, 1)
    target = lax.axis_index("tgt")
    source = lax.axis_index("src")
    load_start = source * share % load_count
    offsets = lag_offset[0, 0]
    own_count = lag_counts[0, 0]
    inner_steps = math.gcd(BLOCK_STEPS, 8)
    responses = impulse_table(couplings, inverse, inner_steps)
    recent_piece = lax.dynamic_slice_in_dim(
        past_density[HIST - COUPLINGS :], target * row_size - source * column_size, row_size, 2
    )
    earlier_steps = spread(recent_piece, "src", target // ratio_groups).astype(jnp.float32)
    earlier_steps = lax.dynamic_slice_in_dim(earlier_steps, load_start, share, 1)
    history = past_density
    produced = []
    for block_index in range(BLOCKS):
        first_step = block_index * BLOCK_STEPS
        partial_sum = jnp.zeros((BLOCK_STEPS * load_count, row_size), jnp.float32)
        partial_sum = far_partial(
            kernels, offsets, history, first_step, jnp.int32(0), own_count, 0, partial_sum
        )
        incident_block = incident[first_step : first_step + BLOCK_STEPS].astype(jnp.float32)
        term = jnp.tile(partial_sum.reshape(BLOCK_STEPS, load_count, row_size), (1, repeats, 1))
        far_share = lax.psum_scatter(term, "src", scatter_dimension=1, tiled=True)
        driving = lax.dynamic_slice_in_dim(incident_block, load_start, share, 1) - far_share
        earlier_steps, solved_share = self_response(
            driving, earlier_steps, couplings, responses, inner_steps
        )
        every_load = lax.all_gather(solved_share, "src", axis=1, tiled=True)
        fresh_block = every_load[:, :load_count]
        produced.append(fresh_block)
        if block_index + 1 < BLOCKS:
            rounded = fresh_block.astype(jnp.bfloat16)
            gathered = lax.all_gather(rounded, "tgt", axis=2, tiled=True)
            columns = lax.dynamic_slice_in_dim(gathered, source * column_size, column_size, 2)
            history = jnp.concatenate([history, columns], 0)
    return jnp.concatenate(produced, 0)


def solution(mesh):
    return jax.shard_map(
        local,
        mesh=mesh,
        in_specs=(
            P(None, None, "tgt"),
            P(None, None, "src"),
            P(None, "src", "tgt"),
            P("tgt", "src", None),
            P("tgt", "src"),
            P(None, "tgt", None),
            P("tgt", None),
        ),
        out_specs=P(None, None, "tgt"),
        check_vma=False,
    )
```

profile of v0, /device:TPU:0, one launch (start us, length us, event | category | flops | bytes accessed | tf_op | source)
XLA Modules:
  0.0 224.8 jit_solution(2054293282193091544)
XLA Ops:
  6.6 16.8 %while.48 = (s32[]{:T(128)}, f32[512,256]{1,0:T(8,128)S(1)}, s32[]{:T(128)}, s32[12]{0:T(128)}, bf16[76,8,512]{2,1,0:T(8,128)(2,1)}, /*index=5*/bf16[8,512,256]{...) while((s32[]{:T(128)}, f32[512,256]{1,0:T(8,128)S(1)}, ...), condition=%wide.region_2.3_spmd, body=%wide.region_1.2_spmd.sunk | while | flops 134348816 | bytes 1835270 | solution.py:37
  7.3 1.3 dynamic_slice.100
  9.2 1.4 convolution_add_fusion.36
  11.3 1.3 dynamic_slice.100
  13.3 1.4 convolution_add_fusion.36
  15.3 1.3 dynamic_slice.100
  17.3 1.4 convolution_add_fusion.36
  19.4 1.3 dynamic_slice.100
  21.3 1.4 convolution_add_fusion.36
  23.4 1.0 copy.27
  25.2 0.7 fusion.101
  25.9 27.7 %psum.7 = bf16[2,8,256]{2,0,1:T(2,128)(2,1)S(1)} all-reduce(bf16[2,8,256]{2,0,1:T(2,128)(2,1)S(1)} %broadcast_select_fusion), channel_id=1, replica_groups=mesh['tgt'=8,'src'=4] {'src'}, use_global_device_ids=true, to_apply=%region_0.1 | all-reduce | flops 4096 | bytes 16384 | tf_op jit(solution)/shard_map/psum | solution.py:19
  61.5 2.5 %reduce-scatter.3.cloned.1.call-done = f32[64,2,256]{2,0,1:T(8,128)} async-done(((f32[64,8,256]{2,0,1:T(8,128)}), f32[64,2,256]{2,0,1:T(8,128)}) %reduce-scatter.3.cloned.1.call-update) | async-done | bytes 131088 | tf_op jit(solution)/shard_map/reduce_scatter | solution.py:115
  64.1 0.9 subtract_bitcast_fusion.1
  65.0 19.1 %while.49 = (s32[]{:T(128)}, f32[2,2,256]{2,0,1:T(2,128)S(1)}, f32[8,8,2,256]{3,1,0,2:T(8,128)S(1)}, f32[8,8,2,256]{3,1,0,2:T(8,128)S(1)}, f32[2,256,256]{2,1,0:...) while((s32[]{:T(128)}, f32[2,2,256]{2,0,1:T(2,128)S(1)}, ...), condition=%wide.region_5.6_spmd, body=%wide.region_4.5_spmd.sunk | while | flops 125865984 | bytes 3080333 | solution.py:81
  84.1 15.9 %all_gather.9 = f32[64,8,256]{2,0,1:T(8,128)S(1)} all-gather(f32[64,2,256]{2,0,1:T(8,128)S(1)} %bitcast.262), channel_id=1, replica_groups=mesh['tgt'=8,'src'=4] {'src'}, dimensions={1}, use_global_device_ids=true | all-gather | bytes 655360 | tf_op jit(solution)/shard_map/all_gather | solution.py:120
  100.0 0.8 copy-done.3
  101.6 26.1 %all-gather.2.cloned.1.call-done = bf16[64,8,2048]{2,0,1:T(8,128)(2,1)} async-done(((bf16[64,8,256]{2,0,1:T(8,128)(2,1)}), bf16[64,8,2048]{2,0,1:T(8,128)(2,1)}) %all-gather.2.cloned.1.call-update) | async-done | bytes 2097168 | tf_op jit(solution)/shard_map/all_gather | solution.py:125
  127.7 1.1 constant_dynamic-slice_fusion
  129.1 1.1 pad_maximum_fusion
  130.3 14.2 %while.50 = (s32[]{:T(128)}, f32[512,256]{1,0:T(8,128)S(1)}, s32[]{:T(128)}, s32[12]{0:T(128)S(1)}, bf16[140,8,512]{2,1,0:T(8,128)(2,1)}, /*index=5*/bf16[8,512,...) while((s32[]{:T(128)}, f32[512,256]{1,0:T(8,128)S(1)}, ...), condition=%wide.region_7.8_spmd, body=%wide.region_6.7_spmd.sunk | while | flops 134348816 | bytes 1835258 | solution.py:37
  132.2 1.4 convolution_add_fusion.43
  135.6 1.4 convolution_add_fusion.43
  138.9 1.4 convolution_add_fusion.43
  142.3 1.4 convolution_add_fusion.43
  144.5 1.0 copy.32
  145.5 1.0 constant_dynamic-slice_fusion.1
  146.5 34.1 %reduce-scatter.5.cloned.1.call-done = f32[64,2,256]{2,0,1:T(8,128)} async-done(((f32[64,8,256]{2,0,1:T(8,128)}), f32[64,2,256]{2,0,1:T(8,128)}) %reduce-scatter.5.cloned.1.call-update) | async-done | bytes 131088 | tf_op jit(solution)/shard_map/reduce_scatter | solution.py:115
  180.6 0.9 subtract_bitcast_fusion
  181.6 19.1 %while.51 = (s32[]{:T(128)}, f32[2,2,256]{2,0,1:T(2,128)S(1)}, f32[8,8,2,256]{3,1,0,2:T(8,128)S(1)}, f32[8,8,2,256]{3,1,0,2:T(8,128)S(1)}, f32[2,256,256]{2,1,0:...) while((s32[]{:T(128)}, f32[2,2,256]{2,0,1:T(2,128)S(1)}, ...), condition=%wide.region_10.11_spmd, body=%wide.region_9.10_spmd.sunk | while | flops 125865984 | bytes 3080333 | solution.py:81
  200.7 15.9 %all_gather.11 = f32[64,8,256]{2,0,1:T(8,128)S(1)} all-gather(f32[64,2,256]{2,0,1:T(8,128)S(1)} %bitcast.261), channel_id=1, replica_groups=mesh['tgt'=8,'src'=4] {'src'}, dimensions={1}, use_global_device_ids=true | all-gather | bytes 655360 | tf_op jit(solution)/shard_map/all_gather | solution.py:120
  216.6 1.6 copy.35
  (295 shorter events, 48.0 us)
Async XLA Ops:
  6.5 57.5 %reduce-scatter.3.cloned.1.call-start = ((), (), s32[]{:S(2)}) async-start(), calls=%async_computation.2 | async-start | bytes 655360 | tf_op jit(solution)/shard_map/reduce_scatter | solution.py:115
  6.6 18.6 %copy-start.5 = (bf16[128,8,256]{2,1,0:T(8,128)(2,1)S(1)}, bf16[128,8,256]{2,1,0:T(8,128)(2,1)}, u32[]{:S(2)}) copy-start(bf16[128,8,256]{2,1,0:T(8,128)(2,1)} %param.15) | copy-start | bytes 1572868
  23.4 30.3 %copy-start = (f32[2,256,256]{2,1,0:T(8,128)S(1)}, f32[2,256,256]{2,1,0:T(8,128)}, u32[]{:S(2)}) copy-start(f32[2,256,256]{2,1,0:T(8,128)} %param.20) | copy-start | bytes 1572868
  23.4 30.3 %copy-start.1 = (f32[256,256]{1,0:T(8,128)S(1)}, f32[256,256]{1,0:T(8,128)}, u32[]{:S(2)}) copy-start(f32[256,256]{1,0:T(8,128)} %param.21) | copy-start | bytes 786436
  24.4 103.4 %all-gather.2.cloned.1.call-start = ((), (), s32[]{:S(2)}) async-start(), calls=%async_computation.3 | async-start | bytes 2359296 | tf_op jit(solution)/shard_map/all_gather | solution.py:125
  84.1 45.1 %copy-start.2 = (bf16[76,8,512]{2,1,0:T(8,128)(2,1)S(1)}, bf16[76,8,512]{2,1,0:T(8,128)(2,1)}, u32[]{:S(2)}) copy-start(bf16[76,8,512]{2,1,0:T(8,128)(2,1)} %get-tuple-element.878) | copy-start | bytes 1867780
  100.0 0.8 copy-start.3
  101.6 79.1 %reduce-scatter.5.cloned.1.call-start = ((), (), s32[]{:S(2)}) async-start(), calls=%async_computation.4 | async-start | bytes 655360 | tf_op jit(solution)/shard_map/reduce_scatter | solution.py:115
  128.8 1.5 copy-start.6
  181.6 35.0 %copy-start.4 = (f32[64,8,256]{2,0,1:T(8,128)S(1)}, f32[64,8,256]{2,0,1:T(8,128)}, u32[]{:S(2)}) copy-start(f32[64,8,256]{2,0,1:T(8,128)} %copy-done.3) | copy-start | bytes 1572868
Sparse Core Ops, SparseCore 0:
  24.5 39.5 reduce-scatter.2
  101.7 26.0 all-gather.1
  145.6 34.9 reduce-scatter.4
where the time goes:
time: 226 us; the launch traced here: 225 us
  waiting for transfers between devices  62.8 us (28%)
  blocking collectives  59.5 us (26%)
  matrix products  52.7 us (23%)
  local copies, waits for them, and re-layouts  17.8 us (8%)
  loops' own time  14.5 us (6%)
  between operations  13.5 us (6%)
  other arithmetic  3.8 us (2%)
    reduce_scatter x2, waiting for transfers between devices, local(): far_share = lax.psum_scatter(term, 'src', scatter_dimension=1, tiled=True)  36.6 us
    all_gather x2, blocking collectives, local(): every_load = lax.all_gather(solved_share, 'src', axis=1, tiled=True)  31.8 us
    psum x1, blocking collectives, spread(): return lax.psum(jnp.where(mine, array, jnp.zeros_like(array)), axis)  27.7 us
    dot_general x128, matrix products, advance(): jnp.dot(shifted.reshape(-1, row_size), responses[delay_index], precision=...  27.1 us
    all_gather x1, waiting for transfers between devices, local(): gathered = lax.all_gather(rounded, 'tgt', axis=2, tiled=True)  26.1 us
    another operation x2, loops' own time, far_partial(): return lax.fori_loop(start_slot, end_slot, add_slot, partial_sum)  12.2 us
    dot_general x8, matrix products, add_slot(): jnp.dot(window.reshape(-1, column_size), kernel_block, preferred_element_...  11.3 us
    dynamic_slice x8, local copies, waits for them, and re-layouts, add_slot(): lag_value = BLOCK_STEPS + offsets[slot_index]  7.45 us
  transfers between devices with their start and end apart: 3, of which 3 were waited for; matrix products, arithmetic and copies ran while one was open for 5% of the time, Pallas kernels for 0%

commit v1 on v0

v1 whole, which is shorter than its diff:
```python
import functools

import jax
import jax.numpy as jnp
from jax import lax
from jax.experimental import pallas as pl
from jax.experimental.pallas import tpu as pltpu
from jax.sharding import PartitionSpec as P

F32 = jnp.float32
BF16 = jnp.bfloat16
LANES = 128
SUBLANES = 8
VMEM = pl.BlockSpec(memory_space=pltpu.VMEM)
SMEM = pl.BlockSpec(memory_space=pltpu.SMEM)
ANY = pl.BlockSpec(memory_space=pl.ANY)


def partner(index, shift, count):
    if count & (count - 1) == 0:
        return index ^ shift
    return (index + shift) % count


def sender(index, shift, count):
    if count & (count - 1) == 0:
        return index ^ shift
    return (index - shift) % count


def split(value):
    high = value.astype(BF16)
    return high, (value - high.astype(F32)).astype(BF16)


def dot3(value, high, low):
    rows = value.shape[0]
    value_high, value_low = split(value)
    both = jnp.dot(
        jnp.concatenate([value_high, value_low], 0), high, preferred_element_type=F32
    )
    cross = jnp.dot(value_high, low, preferred_element_type=F32)
    return both[:rows] + (both[rows:] + cross)


def sum_slots(ints, window_of, kernels, kernel_buffer, sems, total, span):
    count = ints[0]
    slots = kernel_buffer.shape[0]

    def fetch(slot):
        return pltpu.make_async_copy(
            kernels.at[slot], kernel_buffer.at[slot], sems.at[slot]
        )

    total[...] = jnp.zeros_like(total)

    def add(slot, carry):
        fetch(slot).wait()
        window = window_of(span - ints[1 + slot])
        total[...] += jnp.dot(
            window, kernel_buffer[slot], preferred_element_type=F32
        )
        return carry

    lax.fori_loop(0, count, add, 0)


def start_slots(ints, kernels, kernel_buffer, sems):
    for slot in range(kernel_buffer.shape[0]):

        @pl.when(slot < ints[0])
        def _():
            pltpu.make_async_copy(
                kernels.at[slot], kernel_buffer.at[slot], sems.at[slot]
            ).start()


def split_loads(total, strided, by_load, loads, steps):
    groups = strided.shape[0]
    for group in range(groups):
        strided[group] = total[:, group * LANES : (group + 1) * LANES]
    for load in range(loads):
        for group in range(groups):
            by_load[load, :, group * LANES : (group + 1) * LANES] = strided[
                group, pl.ds(load, steps, stride=loads), :
            ]


def write_chunks(ints, base, by_load, outs, share, steps):
    for index, out in enumerate(outs):
        first = ints[base + index]
        for item in range(share):
            out[item * steps : (item + 1) * steps] = by_load[first + item]


def far_first_kernel(
    slots, span, couplings, share, ints, past, kernels, *refs
):
    (*outs, kernel_buffer, total, strided, by_load, sems) = refs
    steps = past.shape[0] - span
    loads, columns = past.shape[1:]
    rows = total.shape[1]
    start_slots(ints, kernels, kernel_buffer, sems)

    def window_of(start):
        return past[pl.ds(start, steps)].reshape(steps * loads, columns)

    sum_slots(ints, window_of, kernels, kernel_buffer, sems, total, span)
    split_loads(total, strided, by_load, loads, steps)
    base = 1 + slots
    write_chunks(ints, base, by_load, outs, share, steps)
    holds = ints[base + len(outs)] > 0
    at = pl.multiple_of(ints[base + len(outs) + 1] * rows, LANES)
    recent = past[past.shape[0] - couplings :, :, pl.ds(at, rows)].astype(F32)
    recent = jnp.where(holds, recent, jnp.zeros_like(recent))
    for step in range(couplings):
        for group in range(rows // LANES):
            strided[group, step * loads : (step + 1) * loads] = recent[
                step, :, group * LANES : (group + 1) * LANES
            ]
    for index, out in enumerate(outs):
        first = ints[base + index]
        out[share * steps :] = jnp.zeros_like(out[share * steps :])
        for item in range(share):
            for step in range(couplings):
                row = share * steps + item * couplings + step
                for group in range(rows // LANES):
                    out[row : row + 1, group * LANES : (group + 1) * LANES] = strided[
                        group, pl.ds(step * loads + first + item, 1), :
                    ]


def far_next_kernel(slots, span, share, ratio, ints, past, kernels, *refs):
    chunk_count = len(refs) - 8
    half = chunk_count
    (*rest, kernel_buffer, total, strided, by_load, stage, history, sems, past_sem) = refs
    sources = (len(rest)) // 2
    chunks, outs = rest[:sources], rest[sources:]
    loads, columns = past.shape[1:]
    rows = total.shape[1]
    steps = history.shape[0] - span
    start_slots(ints, kernels, kernel_buffer, sems)
    tail = pltpu.make_async_copy(
        past.at[pl.ds(steps, span)], history.at[pl.ds(0, span)], past_sem
    )
    tail.start()
    base = 1 + slots + len(outs)
    for index, chunk in enumerate(chunks):
        first = ints[base + index]
        for part in range(ratio):
            for item in range(share):
                stage[first + item, :, part * rows : (part + 1) * rows] = chunk[
                    part, item * steps : (item + 1) * steps
                ].astype(F32)
    groups = columns // LANES
    for group in range(groups):
        for load in range(loads):
            strided[group, pl.ds(load, steps, stride=loads), :] = stage[
                load, :, group * LANES : (group + 1) * LANES
            ]
    for group in range(groups):
        history[span:, :, group * LANES : (group + 1) * LANES] = (
            strided[group].reshape(steps, loads, LANES).astype(BF16)
        )
    tail.wait()

    def window_of(start):
        return history[pl.ds(start, steps)].reshape(steps * loads, columns)

    sum_slots(ints, window_of, kernels, kernel_buffer, sems, total, span)
    split_loads(total, strided.at[pl.ds(0, rows // LANES)], by_load, loads, steps)
    write_chunks(ints, 1 + slots, by_load, outs, share, steps)


def prepare_kernel(levels, couplings, inverse, *refs):
    (
        inverse_high,
        inverse_low,
        coupling_high,
        coupling_low,
        first_high,
        first_low,
        *powers,
        matrix,
    ) = refs
    count, rows, _ = couplings.shape
    high, low = split(inverse[...])
    inverse_high[...] = high
    inverse_low[...] = low
    matrix[...] = jnp.zeros_like(matrix)
    identity = (
        lax.broadcasted_iota(jnp.int32, (rows, rows), 0)
        == lax.broadcasted_iota(jnp.int32, (rows, rows), 1)
    ).astype(F32)
    for lag in range(count):
        coupling_high[lag], coupling_low[lag] = split(couplings[lag])
        matrix[lag * rows : (lag + 1) * rows, :rows] = -dot3(couplings[lag], high, low)
        if lag + 1 < count:
            matrix[
                lag * rows : (lag + 1) * rows, (lag + 1) * rows : (lag + 2) * rows
            ] = identity
    first_high[...], first_low[...] = split(matrix[:rows, :rows])
    power_high, power_low = split(matrix[...])
    for level in range(1, levels):
        wide = powers[2 * (level - 1)].shape[1]
        product = dot3(matrix[...], power_high[:, :wide], power_low[:, :wide])
        power_high, power_low = split(product)
        powers[2 * (level - 1)][...] = power_high
        powers[2 * (level - 1) + 1][...] = power_low
        if level + 1 < levels:
            matrix[...] = product


def solve_kernel(steps, share, levels, parts, packed, *refs):
    partials, refs = refs[:parts], refs[parts:]
    (
        driving,
        earlier,
        inverse_high,
        inverse_low,
        coupling_high,
        coupling_low,
        first_high,
        first_low,
        *powers,
    ) = refs[: 8 + 2 * (levels - 1)]
    solved, rounded, state = refs[8 + 2 * (levels - 1) :]
    count, rows, _ = coupling_high.shape
    size = share * steps
    far = partials[0][...]
    for partial in partials[1:]:
        far = far + partial[...]
    adjusted = driving[...].astype(F32) - far[:size]
    row_of = lax.broadcasted_iota(jnp.int32, (size, 1), 0)
    padded = -(-share // SUBLANES) * SUBLANES
    known = far[size:] if packed else earlier[...]

    def back(lag):
        pieces = [
            known[item * count + count - lag : item * count + count - lag + 1]
            for item in range(share)
        ]
        pieces.append(jnp.zeros((padded - share, rows), F32))
        return jnp.concatenate(pieces, 0)

    for step in range(count):
        pull = None
        for lag in range(step + 1, count + 1):
            term = dot3(back(lag - step), coupling_high[lag - 1], coupling_low[lag - 1])
            pull = term if pull is None else pull + term
        for item in range(share):
            adjusted = adjusted - jnp.where(
                row_of == item * steps + step, pull[item : item + 1], 0.0
            )
    within = row_of % steps
    driven = dot3(adjusted, inverse_high[...], inverse_low[...])

    def delayed(value, delay):
        return jnp.where(within >= delay, pltpu.roll(value, delay, 0), 0.0)

    columns = [driven + delayed(dot3(driven, first_high[...], first_low[...]), 1)]
    if count > 1:
        columns.append(delayed(driven, 1))
    columns += [jnp.zeros_like(driven)] * (count - 2)
    total = jnp.concatenate(columns, 1)
    for level in range(1, levels):
        high, low = powers[2 * (level - 1)], powers[2 * (level - 1) + 1]
        wide = high.shape[1]
        total = total[:, :wide] + delayed(dot3(total, high[...], low[...]), 2**level)
    result = total[:, :rows]
    solved[...] = result
    rounded[...] = result.astype(BF16)
    state[...] = jnp.zeros_like(state)
    for item in range(share):
        state[item * count : (item + 1) * count] = result[
            (item + 1) * steps - count : (item + 1) * steps
        ]


def spread_kernel(steps, share, ints, *refs):
    (*chunks, out, by_load, strided) = refs
    loads, rows = out.shape[1:]
    for index, chunk in enumerate(chunks):
        first = ints[index]
        for item in range(share):
            by_load[first + item] = chunk[item * steps : (item + 1) * steps]
    for group in range(rows // LANES):
        for load in range(loads):
            strided[group, pl.ds(load, steps, stride=loads), :] = by_load[
                load, :, group * LANES : (group + 1) * LANES
            ]
    for group in range(rows // LANES):
        out[:, :, group * LANES : (group + 1) * LANES] = strided[group].reshape(
            steps, loads, LANES
        )


def landing(plane, sources):
    shares = sorted(range(sources), key=lambda z: (-abs(z - plane), z))
    if sources & (sources - 1) == 0:
        chips = sorted(range(sources), key=lambda e: (bin(e ^ plane).count("1"), e))
    else:
        chips = sorted(range(sources), key=lambda e: (abs(e - plane), e))
    where = [0] * sources
    for one, chip in zip(shares, chips):
        where[one] = chip
    return where


def local(incident, past_density, kernels, lag_offset, lag_counts, couplings, inverse):
    all_steps, loads, rows = incident.shape
    columns = past_density.shape[2]
    slots = kernels.shape[0]
    span = lag_offset.shape[2]
    steps = past_density.shape[0] - span
    blocks = all_steps // steps
    count = couplings.shape[0]
    levels = steps.bit_length() - 1
    ratio = columns // rows
    sources = lax.axis_size("src")
    targets = lax.axis_size("tgt")
    target = lax.axis_index("tgt")
    source = lax.axis_index("src")
    share = max(loads // sources, 1)
    size = share * steps
    groups = rows // LANES
    pad = -(-share * count // SUBLANES) * SUBLANES

    def first_load(member):
        return member * share % loads

    peers = [partner(source, k, sources) for k in range(sources)]
    owners = [sender(source, k, sources) for k in range(sources)]
    wanted = [first_load(member) for member in peers]
    offsets = lag_offset[0, 0, :slots]
    scalars = [lag_counts[0, 0]] + [offsets[slot] for slot in range(slots)]
    holds = (source == target // ratio).astype(jnp.int32)
    ints = jnp.stack(scalars + wanted + [holds, target % ratio]).astype(jnp.int32)

    table = [landing(plane, sources) for plane in range(sources)]
    inverse_table = [
        [table[plane].index(chip) for chip in range(sources)] for plane in range(sources)
    ]
    chip = target // ratio
    back_table = jnp.array(inverse_table, jnp.int32)
    arrived = [
        first_load(back_table[source, sender(chip, k, sources)]) for k in range(sources)
    ]
    ints_next = jnp.stack(scalars + wanted + arrived).astype(jnp.int32)
    ints_spread = jnp.stack([first_load(member) for member in owners]).astype(jnp.int32)

    vector = functools.partial(pltpu.CompilerParams, vmem_limit_bytes=32 * 1024 * 1024)
    far_scratch = [
        pltpu.VMEM(kernels.shape, BF16),
        pltpu.VMEM((steps * loads, rows), F32),
    ]

    def trade(value, axis_shift):
        pairs = [(i, partner(i, axis_shift, sources)) for i in range(sources)]
        return lax.ppermute(value, "src", pairs)

    prepared = pl.pallas_call(
        functools.partial(prepare_kernel, levels),
        out_shape=[jax.ShapeDtypeStruct((rows, rows), BF16)] * 2
        + [jax.ShapeDtypeStruct((count, rows, rows), BF16)] * 2
        + [jax.ShapeDtypeStruct((rows, rows), BF16)] * 2
        + [jax.ShapeDtypeStruct((count * rows, count * rows), BF16)] * (2 * (levels - 2))
        + [jax.ShapeDtypeStruct((count * rows, rows), BF16)] * 2,
        in_specs=[VMEM, VMEM],
        out_specs=[VMEM] * (6 + 2 * (levels - 1)),
        scratch_shapes=[pltpu.VMEM((count * rows, count * rows), F32)],
        compiler_params=vector(),
        cost_estimate=pl.CostEstimate(
            flops=6 * levels * (count * rows) ** 3, bytes_accessed=8 * 2**20, transcendentals=0
        ),
        name="prepare",
    )(couplings, inverse)

    def solve(partials, driving, earlier, packed):
        operands = [*partials, driving, earlier, *prepared]
        return pl.pallas_call(
            functools.partial(solve_kernel, steps, share, levels, len(partials), packed),
            out_shape=[
                jax.ShapeDtypeStruct((size, rows), F32),
                jax.ShapeDtypeStruct((size, rows), BF16),
                jax.ShapeDtypeStruct((pad, rows), F32),
            ],
            in_specs=[VMEM] * len(operands),
            out_specs=[VMEM] * 3,
            compiler_params=vector(),
            name="solve",
        )(*operands)

    def spread(chunks):
        return pl.pallas_call(
            functools.partial(spread_kernel, steps, share),
            out_shape=jax.ShapeDtypeStruct((steps, loads, rows), F32),
            in_specs=[SMEM] + [VMEM] * sources,
            out_specs=VMEM,
            scratch_shapes=[
                pltpu.VMEM((loads, steps, rows), F32),
                pltpu.VMEM((groups, steps * loads, LANES), F32),
            ],
            compiler_params=vector(),
            name="spread",
        )(ints_spread, *chunks)

    own_incident = lax.dynamic_slice_in_dim(incident, first_load(source), share, 1)
    own_incident = own_incident.reshape(blocks, steps, share, rows)
    own_incident = own_incident.transpose(0, 2, 1, 3).reshape(blocks, size, rows)

    partials = pl.pallas_call(
        functools.partial(far_first_kernel, slots, span, count, share),
        out_shape=[jax.ShapeDtypeStruct((size + pad, rows), F32)] * sources,
        in_specs=[SMEM, VMEM, ANY],
        out_specs=[VMEM] * sources,
        scratch_shapes=far_scratch
        + [
            pltpu.VMEM((groups, steps * loads, LANES), F32),
            pltpu.VMEM((loads, steps, rows), F32),
            pltpu.SemaphoreType.DMA((slots,)),
        ],
        compiler_params=vector(),
        name="far_first",
    )(ints, past_density, kernels)

    state = jnp.zeros((pad, rows), F32)
    produced = []
    for block in range(blocks):
        if block > 0:
            moves = [
                (
                    (one * ratio + part) * sources + z,
                    (table[one][z] * ratio + part) * sources + one,
                )
                for one in range(sources)
                for part in range(ratio)
                for z in range(sources)
            ]
            landed = lax.ppermute(rounded, ("tgt", "src"), moves)
            around = [landed]
            for k in range(1, sources):
                pairs = [
                    (e * ratio + part, partner(e, k, sources) * ratio + part)
                    for e in range(sources)
                    for part in range(ratio)
                ]
                around.append(lax.ppermute(landed, "tgt", pairs))
            held = jnp.stack(around)
            parts = [held]
            for turn in range(1, ratio):
                pairs = [
                    (e * ratio + part, e * ratio + (part + turn) % ratio)
                    for e in range(sources)
                    for part in range(ratio)
                ]
                parts.append(lax.ppermute(held, "tgt", pairs))
            every = jnp.stack(parts, 1)
            order = (target % ratio - jnp.arange(ratio)) % ratio
            every = every[:, order]
            partials = pl.pallas_call(
                functools.partial(far_next_kernel, slots, span, share, ratio),
                out_shape=[jax.ShapeDtypeStruct((size, rows), F32)] * sources,
                in_specs=[SMEM, ANY, ANY] + [VMEM] * sources,
                out_specs=[VMEM] * sources,
                scratch_shapes=far_scratch
                + [
                    pltpu.VMEM((columns // LANES, steps * loads, LANES), F32),
                    pltpu.VMEM((loads, steps, rows), F32),
                    pltpu.VMEM((loads, steps, columns), F32),
                    pltpu.VMEM((span + steps, loads, columns), BF16),
                    pltpu.SemaphoreType.DMA((slots,)),
                    pltpu.SemaphoreType.DMA,
                ],
                compiler_params=vector(),
                name="far_next",
            )(ints_next, past_density, kernels, *[every[k] for k in range(sources)])
        received = [partials[0]] + [trade(partials[k], k) for k in range(1, sources)]
        solved, rounded, state = solve(received, own_incident[block], state, block == 0)
        chunks = [solved] + [trade(solved, k) for k in range(1, sources)]
        produced.append(spread(chunks))
    return jnp.concatenate(produced, 0)


def solution(mesh):
    return jax.shard_map(
        local,
        mesh=mesh,
        in_specs=(
            P(None, None, "tgt"),
            P(None, None, "src"),
            P(None, "src", "tgt"),
            P("tgt", "src", None),
            P("tgt", "src"),
            P(None, "tgt", None),
            P("tgt", None),
        ),
        out_specs=P(None, None, "tgt"),
        check_vma=False,
    )
```

time: 226 us -> 108 us (0.48)
  blocking collectives: 59.5 us -> 0 us
  matrix products: 52.7 us -> 0 us
  waiting for transfers between devices: 62.8 us -> 25.7 us
  starting transfers between devices: 0.09 us -> 33.7 us
  Pallas kernels: 0 us -> 16.3 us
  loops' own time: 14.5 us -> 0 us
  between operations: 13.5 us -> 3.86 us
  local copies, waits for them, and re-layouts: 17.8 us -> 26.8 us
  other arithmetic: 3.8 us -> 1.23 us
    dot_general x188 -> x0, matrix products: 52.7 us -> none  [the longest x128 27.1 us: advance(): jnp.dot(shifted.reshape(-1, row_size), responses[delay_index], precision=...]
    reduce_scatter x2 -> x0, waiting for transfers between devices: 36.6 us -> none  [local(): far_share = lax.psum_scatter(term, 'src', scatter_dimension=1, tiled=True)]
    ppermute x0 -> x17, starting transfers between devices: none -> 33.7 us  [the longest x12 25 us: trade(): return lax.ppermute(value, 'src', pairs)]
    all_gather x2 -> x0, blocking collectives: 31.8 us -> none  [local(): every_load = lax.all_gather(solved_share, 'src', axis=1, tiled=True)]
    psum x1 -> x0, blocking collectives: 27.7 us -> none  [spread(): return lax.psum(jnp.where(mine, array, jnp.zeros_like(array)), axis)]
    all_gather x1 -> x0, waiting for transfers between devices: 26.1 us -> none  [local(): gathered = lax.all_gather(rounded, 'tgt', axis=2, tiled=True)]
    ppermute x0 -> x17, waiting for transfers between devices: none -> 25.7 us  [the longest x12 19.5 us: trade(): return lax.ppermute(value, 'src', pairs)]
    pallas_call x0 -> x7, Pallas kernels: none -> 16.3 us  [the longest x2 5.25 us: solve(): pl.pallas_call(functools.partial(solve_kernel, steps, share, levels, len(...]
  transfers between devices with their start and end apart: 3 -> 17, of which waited for: 3 -> 8; matrix products, arithmetic and copies ran while one was open for 5% -> 6% of each run, Pallas kernels for 0% -> 8%
where the time goes in v1:
time: 108 us
  starting transfers between devices  33.7 us (31%)
  local copies, waits for them, and re-layouts  26.8 us (25%)
  waiting for transfers between devices  25.7 us (24%)
  Pallas kernels  16.3 us (15%)
  between operations  3.86 us (4%)
  other arithmetic  1.23 us (1%)
    ppermute x12, starting transfers between devices, trade(): return lax.ppermute(value, 'src', pairs)  25 us
    ppermute x12, waiting for transfers between devices, trade(): return lax.ppermute(value, 'src', pairs)  19.5 us
    unnamed x83, local copies, waits for them, and re-layouts  8.86 us
    ppermute x3, starting transfers between devices, local(): around.append(lax.ppermute(landed, 'tgt', pairs))  5.45 us
    pallas_call x2, Pallas kernels, solve(): pl.pallas_call(functools.partial(solve_kernel, steps, share, levels, len(...  5.25 us
    another operation x1, local copies, waits for them, and re-layouts, local(): ints_next = jnp.stack(scalars + wanted + arrived).astype(jnp.int32)  5.08 us
    another operation x1, local copies, waits for them, and re-layouts, local(): jnp.stack(scalars + wanted + [holds, target % ratio]).astype(jnp.int32)  5.08 us
    pallas_call x1, Pallas kernels, local(): pl.pallas_call(functools.partial(prepare_kernel, levels), out_shape=[jax....  4.78 us
  transfers between devices with their start and end apart: 17, of which 8 were waited for; matrix products, arithmetic and copies ran while one was open for 6% of the time, Pallas kernels for 8%

profile of v1, /device:TPU:0, one launch (start us, length us, event | category | flops | bytes accessed | tf_op | source)
XLA Modules:
  0.0 107.7 jit_solution(859849484874226232)
XLA Ops:
  0.7 1.6 %fusion.5 = (s32[1,1,1]{2,1,0:T(1,128)}, s32[1,1,1]{2,1,0:T(1,128)}, s32[1,1,1]{2,1,0:T(1,128)}, s32[1,1,1]{2,1,0:T(1,128)}, s32[1,1,1]{2,1,0:T(1,128)}, /*index...) fusion(s32[1,1,12]{2,1,0:T(1,128)} %param.11), kind=kLoop, calls=%fused_computation.21 | loop fusion | bytes 64 | tf_op jit(solution)/shard_map/slice | solution.py:336
  2.4 5.1 %stack.82.ints = s32[15]{0:T(128)S(1)} concatenate(s32[1]{0:T(128)} %bitcast.48, s32[1]{0:T(128)} %bitcast.5, s32[1]{0:T(128)} %bitcast.6, s32[1]{0:T(128)} %bitcast.7, s32[1]{0:T(128)} %bitcast.8, s32[1]{0:T(128)} %bitcast.9, s32[1]{0:T(128)} %bitcast.10, s32[1]{0:T(128)} %bitcast.11, s32[1]{0:T(128)} %bitcast.12, s32[1]{0:T(128)} %bitcast, s32[1]{0:T(128)} %bitcast.1, ...), dimensions={0} | concatenate | bytes 120 | tf_op jit(solution)/shard_map/stack | solution.py:338
  7.5 1.6 %copy-done.1 = bf16[8,512,256]{2,1,0:T(8,128)(2,1)S(1)} copy-done((bf16[8,512,256]{2,1,0:T(8,128)(2,1)S(1)}, bf16[8,512,256]{2,1,0:T(8,128)(2,1)}, u32[]{:S(2)}) %copy-start.1) | copy-done | bytes 2097176
  9.0 1.1 copy-done.3
  10.1 2.2 %far_first.1 = (f32[136,256]{1,0:T(8,128)S(1)}, f32[136,256]{1,0:T(8,128)S(1)}, f32[136,256]{1,0:T(8,128)S(1)}, f32[136,256]{1,0:T(8,128)S(1)}) custom-call(s32[15]{0:T(128)S(1)} %stack.82.ints, bf16[76,8,512]{2,1,0:T(8,128)(2,1)S(1)} %copy-done.3, bf16[8,512,256]{2,1,0:T(8,128)(2,1)S(1)} %copy-done.1), custom_call_target="tpu_custom_call" | custom-call | tf_op jit(solution)/shard_map/far_first/pallas_call | solution.py:412
  12.3 3.1 %collective-permute-start = (f32[136,256]{1,0:T(8,128)S(1)}, f32[136,256]{1,0:T(8,128)S(1)}, u32[]{:S(2)}, u32[]{:S(2)}) collective-permute-start(f32[136,256]{1,0:T(8,128)S(1)} %get-tuple-element.34), channel_id=1, source_target_pairs={{0,1},{1,0},{2,3},{3,2},{4,5},{5,4},{6,7},{7,6},{8,9},{9,8},{10,11... | collective-permute-start | bytes 417800 | tf_op jit(solution)/shard_map/ppermute | solution.py:360
  15.4 2.0 %collective-permute-start.1 = (f32[136,256]{1,0:T(8,128)S(1)}, f32[136,256]{1,0:T(8,128)S(1)}, u32[]{:S(2)}, u32[]{:S(2)}) collective-permute-start(f32[136,256]{1,0:T(8,128)S(1)} %get-tuple-element.35), channel_id=1, source_target_pairs={{0,2},{1,3},{2,0},{3,1},{4,6},{5,7},{6,4},{7,5},{8,10},{9,11},{10,... | collective-permute-start | bytes 417800 | tf_op jit(solution)/shard_map/ppermute | solution.py:360
  18.0 4.8 %prepare.1 = (bf16[256,256]{1,0:T(8,128)(2,1)S(1)}, bf16[256,256]{1,0:T(8,128)(2,1)S(1)}, bf16[2,256,256]{2,1,0:T(8,128)(2,1)S(1)}, bf16[2,256,256]{2,1,0:T(8,12...) custom-call(f32[2,256,256]{2,1,0:T(8,128)S(1)} %copy-done.38, ...), custom_call_target="tpu_custom_call" | custom-call | flops 4831838208 | bytes 8388608 | tf_op jit(solution)/shard_map/prepare/pallas_call | solution.py:362
  23.8 4.0 %collective-permute-done.2.refs_3_ = f32[136,256]{1,0:T(8,128)S(1)} collective-permute-done((f32[136,256]{1,0:T(8,128)S(1)}, f32[136,256]{1,0:T(8,128)S(1)}, u32[]{:S(2)}, u32[]{:S(2)}) %collective-permute-start.2) | collective-permute-done | bytes 139296 | tf_op jit(solution)/shard_map/ppermute | solution.py:360
  27.8 2.3 %solve.2 = (f32[128,256]{1,0:T(8,128)S(1)}, bf16[128,256]{1,0:T(8,128)(2,1)S(1)}, f32[8,256]{1,0:T(8,128)S(1)}) custom-call(f32[136,256]{1,0:T(8,128)S(1)} %get-tuple-element.33.refs_0_, f32[136,256]{1,0:T(8,128)S(1)} %collective-permute-done.refs_1_, f32[136,256]{1,0:T(8,128)S(1)} %collective-permute-done.1.refs_2_, ...), custom_call_target="tpu_custom_call" | custom-call | tf_op jit(solution)/shard_map/solve/pallas_call | solution.py:381
  30.9 3.2 %collective-permute-start.6 = (bf16[128,256]{1,0:T(8,128)(2,1)S(1)}, bf16[128,256]{1,0:T(8,128)(2,1)S(1)}, u32[]{:S(2)}, u32[]{:S(2)}) collective-permute-start(bf16[128,256]{1,0:T(8,128)(2,1)S(1)} %get-tuple-element.54), channel_id=1, source_target_pairs={{0,24},{1,16},{2,8},{3,0},{4,28},{5,20},{6,12},{7,4},{8,1},{9,17},... | collective-permute-start | bytes 196616 | tf_op jit(solution)/shard_map/ppermute | solution.py:440
  34.1 2.9 %collective-permute-done.6 = bf16[128,256]{1,0:T(8,128)(2,1)S(1)} collective-permute-done((bf16[128,256]{1,0:T(8,128)(2,1)S(1)}, bf16[128,256]{1,0:T(8,128)(2,1)S(1)}, u32[]{:S(2)}, u32[]{:S(2)}) %collective-permute-start.6) | collective-permute-done | bytes 65568 | tf_op jit(solution)/shard_map/ppermute | solution.py:440
  37.0 2.3 %collective-permute-start.9 = (bf16[128,256]{1,0:T(8,128)(2,1)S(1)}, bf16[128,256]{1,0:T(8,128)(2,1)S(1)}, u32[]{:S(2)}, u32[]{:S(2)}) collective-permute-start(bf16[128,256]{1,0:T(8,128)(2,1)S(1)} %collective-permute-done.6), channel_id=1, source_target_pairs={{0,24},{4,28},{8,16},{12,20},{16,8},{20,12},{24,0},{28,4},{1,25},{... | collective-permute-start | bytes 196616 | tf_op jit(solution)/shard_map/ppermute | solution.py:448
  39.2 2.2 %collective-permute-start.8 = (bf16[128,256]{1,0:T(8,128)(2,1)S(1)}, bf16[128,256]{1,0:T(8,128)(2,1)S(1)}, u32[]{:S(2)}, u32[]{:S(2)}) collective-permute-start(bf16[128,256]{1,0:T(8,128)(2,1)S(1)} %collective-permute-done.6), channel_id=1, source_target_pairs={{0,16},{4,20},{8,24},{12,28},{16,0},{20,4},{24,8},{28,12},{1,17},{... | collective-permute-start | bytes 196616 | tf_op jit(solution)/shard_map/ppermute | solution.py:448
  41.5 1.0 collective-permute-start.7
  42.4 1.3 %collective-permute-done.8 = bf16[128,256]{1,0:T(8,128)(2,1)S(1)} collective-permute-done((bf16[128,256]{1,0:T(8,128)(2,1)S(1)}, bf16[128,256]{1,0:T(8,128)(2,1)S(1)}, u32[]{:S(2)}, u32[]{:S(2)}) %collective-permute-start.8) | collective-permute-done | bytes 65568 | tf_op jit(solution)/shard_map/ppermute | solution.py:448
  43.7 2.0 %collective-permute-done.7 = bf16[128,256]{1,0:T(8,128)(2,1)S(1)} collective-permute-done((bf16[128,256]{1,0:T(8,128)(2,1)S(1)}, bf16[128,256]{1,0:T(8,128)(2,1)S(1)}, u32[]{:S(2)}, u32[]{:S(2)}) %collective-permute-start.7) | collective-permute-done | bytes 65568 | tf_op jit(solution)/shard_map/ppermute | solution.py:448
  49.0 5.1 %stack.87.ints = s32[17]{0:T(128)S(1)} concatenate(s32[1]{0:T(128)} %bitcast.49, s32[1]{0:T(128)} %bitcast.5, s32[1]{0:T(128)} %bitcast.6, s32[1]{0:T(128)} %bitcast.7, s32[1]{0:T(128)} %bitcast.8, s32[1]{0:T(128)} %bitcast.9, s32[1]{0:T(128)} %bitcast.10, s32[1]{0:T(128)} %bitcast.11, s32[1]{0:T(128)} %bitcast.12, s32[1]{0:T(128)} %bitcast, s32[1]{0:T(128)} %bitcast.1, ...), dimensions={0} | concatenate | bytes 136 | tf_op jit(solution)/shard_map/stack | solution.py:349
  55.1 2.6 %gather_fusion = bf16[2,4,128,256]{3,2,1,0:T(8,128)(2,1)} fusion(bf16[4,2,128,256]{3,2,1,0:T(8,128)(2,1)} %copy.10, s32[1024]{0:T(1024)S(1)} %pad_clamp_fusion), kind=kCustom, calls=%fused_computation | custom fusion | bytes 1048584 | tf_op jit(solution)/shard_map/gather | solution.py:460
  57.7 1.1 %copy.14 = bf16[2,4,128,256]{3,2,0,1:T(8,128)(2,1)S(1)} copy(bf16[2,4,128,256]{3,2,1,0:T(8,128)(2,1)} %gather_fusion) | data formatting | bytes 1048576 | tf_op jit(solution)/shard_map/gather | solution.py:460
  58.9 2.7 %far_next.1 = (f32[128,256]{1,0:T(8,128)S(1)}, f32[128,256]{1,0:T(8,128)S(1)}, f32[128,256]{1,0:T(8,128)S(1)}, f32[128,256]{1,0:T(8,128)S(1)}) custom-call(s32[17]{0:T(128)S(1)} %stack.87.ints, bf16[76,8,512]{2,1,0:T(8,128)(2,1)S(1)} %copy-done.4, bf16[8,512,256]{2,1,0:T(8,128)(2,1)S(1)} %copy-done.2, bf16[2,128,256]{2,1,0:T(8,128)(2,1)S(1)} %get-tuple-element.64.refs_0_, ...), custom_call_target="tpu_custom_call" | custom-call | tf_op jit(solution)/shard_map/far_next/pallas_call | solution.py:461
  61.6 0.9 collective-permute-start.11
  63.3 2.7 %collective-permute-start.13 = (f32[128,256]{1,0:T(8,128)S(1)}, f32[128,256]{1,0:T(8,128)S(1)}, u32[]{:S(2)}, u32[]{:S(2)}) collective-permute-start(f32[128,256]{1,0:T(8,128)S(1)} %get-tuple-element.58), channel_id=1, source_target_pairs={{0,3},{1,2},{2,1},{3,0},{4,7},{5,6},{6,5},{7,4},{8,11},{9,10},{10,... | collective-permute-start | bytes 393224 | tf_op jit(solution)/shard_map/ppermute | solution.py:360
  66.1 1.6 %collective-permute-start.4 = (f32[128,256]{1,0:T(8,128)}, f32[128,256]{1,0:T(8,128)S(1)}, u32[]{:S(2)}, u32[]{:S(2)}) collective-permute-start(f32[128,256]{1,0:T(8,128)} %copy-done.36), channel_id=1, source_target_pairs={{0,2},{1,3},{2,0},{3,1},{4,6},{5,7},{6,4},{7,5},{8,10},{9,11},{10,... | collective-permute-start | bytes 393224 | tf_op jit(solution)/shard_map/ppermute | solution.py:360
  68.6 1.8 %collective-permute-start.5 = (f32[128,256]{1,0:T(8,128)}, f32[128,256]{1,0:T(8,128)S(1)}, u32[]{:S(2)}, u32[]{:S(2)}) collective-permute-start(f32[128,256]{1,0:T(8,128)} %copy-done.36), channel_id=1, source_target_pairs={{0,3},{1,2},{2,1},{3,0},{4,7},{5,6},{6,5},{7,4},{8,11},{9,10},{10,... | collective-permute-start | bytes 393224 | tf_op jit(solution)/shard_map/ppermute | solution.py:360
  70.5 4.8 %collective-permute-done.12.refs_2_ = f32[128,256]{1,0:T(8,128)S(1)} collective-permute-done((f32[128,256]{1,0:T(8,128)S(1)}, f32[128,256]{1,0:T(8,128)S(1)}, u32[]{:S(2)}, u32[]{:S(2)}) %collective-permute-start.12) | collective-permute-done | bytes 131104 | tf_op jit(solution)/shard_map/ppermute | solution.py:360
  80.8 2.9 %solve.3 = (f32[128,256]{1,0:T(8,128)S(1)}, bf16[128,256]{1,0:T(8,128)(2,1)}, f32[8,256]{1,0:T(8,128)}) custom-call(f32[128,256]{1,0:T(8,128)S(1)} %get-tuple-element.55.refs_0_, f32[128,256]{1,0:T(8,128)S(1)} %collective-permute-done.11.refs_1_, f32[128,256]{1,0:T(8,128)S(1)} %collective-permute-done.12.refs_2_, ...), custom_call_target="tpu_custom_call" | custom-call | tf_op jit(solution)/shard_map/solve/pallas_call | solution.py:381
  83.8 9.2 %collective-permute-start.14 = (f32[128,256]{1,0:T(8,128)S(1)}, f32[128,256]{1,0:T(8,128)S(1)}, u32[]{:S(2)}, u32[]{:S(2)}) collective-permute-start(f32[128,256]{1,0:T(8,128)S(1)} %get-tuple-element.60.refs_0_), channel_id=1, source_target_pairs={{0,1},{1,0},{2,3},{3,2},{4,5},{5,4},{6,7},{7,6},{8,9},{9,8},{10,11... | collective-permute-start | bytes 393224 | tf_op jit(solution)/shard_map/ppermute | solution.py:360
  93.0 2.4 %collective-permute-start.16 = (f32[128,256]{1,0:T(8,128)S(1)}, f32[128,256]{1,0:T(8,128)S(1)}, u32[]{:S(2)}, u32[]{:S(2)}) collective-permute-start(f32[128,256]{1,0:T(8,128)S(1)} %get-tuple-element.60.refs_0_), channel_id=1, source_target_pairs={{0,3},{1,2},{2,1},{3,0},{4,7},{5,6},{6,5},{7,4},{8,11},{9,10},{10,... | collective-permute-start | bytes 393224 | tf_op jit(solution)/shard_map/ppermute | solution.py:360
  96.2 2.4 %collective-permute-done.14.refs_1_ = f32[128,256]{1,0:T(8,128)S(1)} collective-permute-done((f32[128,256]{1,0:T(8,128)S(1)}, f32[128,256]{1,0:T(8,128)S(1)}, u32[]{:S(2)}, u32[]{:S(2)}) %collective-permute-start.14) | collective-permute-done | bytes 131104 | tf_op jit(solution)/shard_map/ppermute | solution.py:360
  98.6 7.3 %collective-permute-done.15.refs_2_ = f32[128,256]{1,0:T(8,128)S(1)} collective-permute-done((f32[128,256]{1,0:T(8,128)S(1)}, f32[128,256]{1,0:T(8,128)S(1)}, u32[]{:S(2)}, u32[]{:S(2)}) %collective-permute-start.15) | collective-permute-done | bytes 131104 | tf_op jit(solution)/shard_map/ppermute | solution.py:360
  106.6 1.0 pad_maximum_fusion
  (109 shorter events, 12.6 us)
Async XLA Ops:
  0.0 17.8 %copy-start = (bf16[128,8,256]{2,1,0:T(8,128)(2,1)S(1)}, bf16[128,8,256]{2,1,0:T(8,128)(2,1)}, u32[]{:S(2)}) copy-start(bf16[128,8,256]{2,1,0:T(8,128)(2,1)} %param.8) | copy-start | bytes 1572868
  10.1 7.9 %copy-start.38 = (f32[2,256,256]{2,1,0:T(8,128)S(1)}, f32[2,256,256]{2,1,0:T(8,128)}, u32[]{:S(2)}) copy-start(f32[2,256,256]{2,1,0:T(8,128)} %couplings.1) | copy-start | bytes 1572868
  10.1 7.9 %copy-start.39 = (f32[256,256]{1,0:T(8,128)S(1)}, f32[256,256]{1,0:T(8,128)}, u32[]{:S(2)}) copy-start(f32[256,256]{1,0:T(8,128)} %inverse.1) | copy-start | bytes 786436
  12.3 11.5 %collective-permute-start = (f32[136,256]{1,0:T(8,128)S(1)}, f32[136,256]{1,0:T(8,128)S(1)}, u32[]{:S(2)}, u32[]{:S(2)}) collective-permute-start(f32[136,256]{1,0:T(8,128)S(1)} %get-tuple-element.34), channel_id=1, source_target_pairs={{0,1},{1,0},{2,3},{3,2},{4,5},{5,4},{6,7},{7,6},{8,9},{9,8},{10,11... | collective-permute-start | bytes 417800 | tf_op jit(solution)/shard_map/ppermute | solution.py:360
  15.4 8.4 %collective-permute-start.1 = (f32[136,256]{1,0:T(8,128)S(1)}, f32[136,256]{1,0:T(8,128)S(1)}, u32[]{:S(2)}, u32[]{:S(2)}) collective-permute-start(f32[136,256]{1,0:T(8,128)S(1)} %get-tuple-element.35), channel_id=1, source_target_pairs={{0,2},{1,3},{2,0},{3,1},{4,6},{5,7},{6,4},{7,5},{8,10},{9,11},{10,... | collective-permute-start | bytes 417800 | tf_op jit(solution)/shard_map/ppermute | solution.py:360
  17.3 10.4 %collective-permute-start.2 = (f32[136,256]{1,0:T(8,128)S(1)}, f32[136,256]{1,0:T(8,128)S(1)}, u32[]{:S(2)}, u32[]{:S(2)}) collective-permute-start(f32[136,256]{1,0:T(8,128)S(1)} %get-tuple-element.36), channel_id=1, source_target_pairs={{0,3},{1,2},{2,1},{3,0},{4,7},{5,6},{6,5},{7,4},{8,11},{9,10},{10,... | collective-permute-start | bytes 417800 | tf_op jit(solution)/shard_map/ppermute | solution.py:360
  27.8 18.1 %copy-start.40 = (s32[4,4]{1,0:T(4,128)S(1)}, s32[4,4]{1,0:T(4,128)}, u32[]{:S(2)}) copy-start(s32[4,4]{1,0:T(4,128)} %constant.110.clone) | copy-start | bytes 196
  30.9 6.1 %collective-permute-start.6 = (bf16[128,256]{1,0:T(8,128)(2,1)S(1)}, bf16[128,256]{1,0:T(8,128)(2,1)S(1)}, u32[]{:S(2)}, u32[]{:S(2)}) collective-permute-start(bf16[128,256]{1,0:T(8,128)(2,1)S(1)} %get-tuple-element.54), channel_id=1, source_target_pairs={{0,24},{1,16},{2,8},{3,0},{4,28},{5,20},{6,12},{7,4},{8,1},{9,17},... | collective-permute-start | bytes 196616 | tf_op jit(solution)/shard_map/ppermute | solution.py:440
  37.0 5.5 %collective-permute-start.9 = (bf16[128,256]{1,0:T(8,128)(2,1)S(1)}, bf16[128,256]{1,0:T(8,128)(2,1)S(1)}, u32[]{:S(2)}, u32[]{:S(2)}) collective-permute-start(bf16[128,256]{1,0:T(8,128)(2,1)S(1)} %collective-permute-done.6), channel_id=1, source_target_pairs={{0,24},{4,28},{8,16},{12,20},{16,8},{20,12},{24,0},{28,4},{1,25},{... | collective-permute-start | bytes 196616 | tf_op jit(solution)/shard_map/ppermute | solution.py:448
  39.2 4.5 %collective-permute-start.8 = (bf16[128,256]{1,0:T(8,128)(2,1)S(1)}, bf16[128,256]{1,0:T(8,128)(2,1)S(1)}, u32[]{:S(2)}, u32[]{:S(2)}) collective-permute-start(bf16[128,256]{1,0:T(8,128)(2,1)S(1)} %collective-permute-done.6), channel_id=1, source_target_pairs={{0,16},{4,20},{8,24},{12,28},{16,0},{20,4},{24,8},{28,12},{1,17},{... | collective-permute-start | bytes 196616 | tf_op jit(solution)/shard_map/ppermute | solution.py:448
  41.5 4.3 %collective-permute-start.7 = (bf16[128,256]{1,0:T(8,128)(2,1)S(1)}, bf16[128,256]{1,0:T(8,128)(2,1)S(1)}, u32[]{:S(2)}, u32[]{:S(2)}) collective-permute-start(bf16[128,256]{1,0:T(8,128)(2,1)S(1)} %collective-permute-done.6), channel_id=1, source_target_pairs={{0,8},{4,12},{8,0},{12,4},{16,24},{20,28},{24,16},{28,20},{1,9},{5... | collective-permute-start | bytes 196616 | tf_op jit(solution)/shard_map/ppermute | solution.py:448
  45.8 8.4 %collective-permute-start.10 = (bf16[4,128,256]{2,1,0:T(8,128)(2,1)S(1)}, bf16[4,128,256]{2,1,0:T(8,128)(2,1)S(1)}, u32[]{:S(2)}, u32[]{:S(2)}) collective-permute-start(bf16[4,128,256]{2,1,0:T(8,128)(2,1)S(1)} %get-tuple-element.66), channel_id=1, source_target_pairs={{0,4},{4,0},{8,12},{12,8},{16,20},{20,16},{24,28},{28,24},{1,5},{5... | collective-permute-start | bytes 786440 | tf_op jit(solution)/shard_map/ppermute | solution.py:457
  57.7 17.7 %copy-start.22 = (bf16[2,256,256]{2,1,0:T(8,128)(2,1)S(1)}, bf16[2,256,256]{2,1,0:T(8,128)(2,1)}, u32[]{:S(2)}) copy-start(bf16[2,256,256]{2,1,0:T(8,128)(2,1)} %copy-done.21) | copy-start | bytes 786436
  57.7 17.7 %copy-start.24 = (bf16[512,256]{1,0:T(8,128)(2,1)S(1)}, bf16[512,256]{1,0:T(8,128)(2,1)}, u32[]{:S(2)}) copy-start(bf16[512,256]{1,0:T(8,128)(2,1)} %copy-done.23) | copy-start | bytes 786436
  58.8 16.5 %copy-start.6 = (bf16[512,512]{1,0:T(8,128)(2,1)S(1)}, bf16[512,512]{1,0:T(8,128)(2,1)}, u32[]{:S(2)}) copy-start(bf16[512,512]{1,0:T(8,128)(2,1)} %copy-done.5) | copy-start | bytes 1572868
  58.8 16.5 %copy-start.8 = (bf16[512,512]{1,0:T(8,128)(2,1)S(1)}, bf16[512,512]{1,0:T(8,128)(2,1)}, u32[]{:S(2)}) copy-start(bf16[512,512]{1,0:T(8,128)(2,1)} %copy-done.7) | copy-start | bytes 1572868
  58.8 16.5 %copy-start.10 = (bf16[512,512]{1,0:T(8,128)(2,1)S(1)}, bf16[512,512]{1,0:T(8,128)(2,1)}, u32[]{:S(2)}) copy-start(bf16[512,512]{1,0:T(8,128)(2,1)} %copy-done.9) | copy-start | bytes 1572868
  58.8 16.5 %copy-start.12 = (bf16[512,512]{1,0:T(8,128)(2,1)S(1)}, bf16[512,512]{1,0:T(8,128)(2,1)}, u32[]{:S(2)}) copy-start(bf16[512,512]{1,0:T(8,128)(2,1)} %copy-done.11) | copy-start | bytes 1572868
  58.8 16.5 %copy-start.14 = (bf16[512,512]{1,0:T(8,128)(2,1)S(1)}, bf16[512,512]{1,0:T(8,128)(2,1)}, u32[]{:S(2)}) copy-start(bf16[512,512]{1,0:T(8,128)(2,1)} %copy-done.13) | copy-start | bytes 1572868
  58.8 16.5 %copy-start.16 = (bf16[512,512]{1,0:T(8,128)(2,1)S(1)}, bf16[512,512]{1,0:T(8,128)(2,1)}, u32[]{:S(2)}) copy-start(bf16[512,512]{1,0:T(8,128)(2,1)} %copy-done.15) | copy-start | bytes 1572868
  58.9 16.5 %copy-start.18 = (bf16[512,512]{1,0:T(8,128)(2,1)S(1)}, bf16[512,512]{1,0:T(8,128)(2,1)}, u32[]{:S(2)}) copy-start(bf16[512,512]{1,0:T(8,128)(2,1)} %copy-done.17) | copy-start | bytes 1572868
  58.9 16.5 %copy-start.20 = (bf16[512,512]{1,0:T(8,128)(2,1)S(1)}, bf16[512,512]{1,0:T(8,128)(2,1)}, u32[]{:S(2)}) copy-start(bf16[512,512]{1,0:T(8,128)(2,1)} %copy-done.19) | copy-start | bytes 1572868
  61.6 7.0 %collective-permute-start.11 = (f32[128,256]{1,0:T(8,128)S(1)}, f32[128,256]{1,0:T(8,128)S(1)}, u32[]{:S(2)}, u32[]{:S(2)}) collective-permute-start(f32[128,256]{1,0:T(8,128)S(1)} %get-tuple-element.56), channel_id=1, source_target_pairs={{0,1},{1,0},{2,3},{3,2},{4,5},{5,4},{6,7},{7,6},{8,9},{9,8},{10,11... | collective-permute-start | bytes 393224 | tf_op jit(solution)/shard_map/ppermute | solution.py:360
  62.6 12.7 %collective-permute-start.12 = (f32[128,256]{1,0:T(8,128)S(1)}, f32[128,256]{1,0:T(8,128)S(1)}, u32[]{:S(2)}, u32[]{:S(2)}) collective-permute-start(f32[128,256]{1,0:T(8,128)S(1)} %get-tuple-element.57), channel_id=1, source_target_pairs={{0,2},{1,3},{2,0},{3,1},{4,6},{5,7},{6,4},{7,5},{8,10},{9,11},{10,... | collective-permute-start | bytes 393224 | tf_op jit(solution)/shard_map/ppermute | solution.py:360
  63.3 12.0 %collective-permute-start.13 = (f32[128,256]{1,0:T(8,128)S(1)}, f32[128,256]{1,0:T(8,128)S(1)}, u32[]{:S(2)}, u32[]{:S(2)}) collective-permute-start(f32[128,256]{1,0:T(8,128)S(1)} %get-tuple-element.58), channel_id=1, source_target_pairs={{0,3},{1,2},{2,1},{3,0},{4,7},{5,6},{6,5},{7,4},{8,11},{9,10},{10,... | collective-permute-start | bytes 393224 | tf_op jit(solution)/shard_map/ppermute | solution.py:360
  66.1 26.9 %collective-permute-start.3 = (f32[128,256]{1,0:T(8,128)}, f32[128,256]{1,0:T(8,128)S(1)}, u32[]{:S(2)}, u32[]{:S(2)}) collective-permute-start(f32[128,256]{1,0:T(8,128)} %copy-done.36), channel_id=1, source_target_pairs={{0,1},{1,0},{2,3},{3,2},{4,5},{5,4},{6,7},{7,6},{8,9},{9,8},{10,11... | collective-permute-start | bytes 393224 | tf_op jit(solution)/shard_map/ppermute | solution.py:360
  66.1 29.3 %collective-permute-start.4 = (f32[128,256]{1,0:T(8,128)}, f32[128,256]{1,0:T(8,128)S(1)}, u32[]{:S(2)}, u32[]{:S(2)}) collective-permute-start(f32[128,256]{1,0:T(8,128)} %copy-done.36), channel_id=1, source_target_pairs={{0,2},{1,3},{2,0},{3,1},{4,6},{5,7},{6,4},{7,5},{8,10},{9,11},{10,... | collective-permute-start | bytes 393224 | tf_op jit(solution)/shard_map/ppermute | solution.py:360
  68.6 26.8 %collective-permute-start.5 = (f32[128,256]{1,0:T(8,128)}, f32[128,256]{1,0:T(8,128)S(1)}, u32[]{:S(2)}, u32[]{:S(2)}) collective-permute-start(f32[128,256]{1,0:T(8,128)} %copy-done.36), channel_id=1, source_target_pairs={{0,3},{1,2},{2,1},{3,0},{4,7},{5,6},{6,5},{7,4},{8,11},{9,10},{10,... | collective-permute-start | bytes 393224 | tf_op jit(solution)/shard_map/ppermute | solution.py:360
  80.8 14.6 %copy-start.37 = (f32[128,256]{1,0:T(8,128)S(1)}, f32[128,256]{1,0:T(8,128)}, u32[]{:S(2)}) copy-start(f32[128,256]{1,0:T(8,128)} %copy-done.36) | copy-start | bytes 393220
  83.8 14.8 %collective-permute-start.14 = (f32[128,256]{1,0:T(8,128)S(1)}, f32[128,256]{1,0:T(8,128)S(1)}, u32[]{:S(2)}, u32[]{:S(2)}) collective-permute-start(f32[128,256]{1,0:T(8,128)S(1)} %get-tuple-element.60.refs_0_), channel_id=1, source_target_pairs={{0,1},{1,0},{2,3},{3,2},{4,5},{5,4},{6,7},{7,6},{8,9},{9,8},{10,11... | collective-permute-start | bytes 393224 | tf_op jit(solution)/shard_map/ppermute | solution.py:360
  93.0 12.9 %collective-permute-start.15 = (f32[128,256]{1,0:T(8,128)S(1)}, f32[128,256]{1,0:T(8,128)S(1)}, u32[]{:S(2)}, u32[]{:S(2)}) collective-permute-start(f32[128,256]{1,0:T(8,128)S(1)} %get-tuple-element.60.refs_0_), channel_id=1, source_target_pairs={{0,2},{1,3},{2,0},{3,1},{4,6},{5,7},{6,4},{7,5},{8,10},{9,11},{10,... | collective-permute-start | bytes 393224 | tf_op jit(solution)/shard_map/ppermute | solution.py:360
  93.0 12.9 %collective-permute-start.16 = (f32[128,256]{1,0:T(8,128)S(1)}, f32[128,256]{1,0:T(8,128)S(1)}, u32[]{:S(2)}, u32[]{:S(2)}) collective-permute-start(f32[128,256]{1,0:T(8,128)S(1)} %get-tuple-element.60.refs_0_), channel_id=1, source_target_pairs={{0,3},{1,2},{2,1},{3,0},{4,7},{5,6},{6,5},{7,4},{8,11},{9,10},{10,... | collective-permute-start | bytes 393224 | tf_op jit(solution)/shard_map/ppermute | solution.py:360
  (26 other events, 127.7 us)

commit v2 on v1

v2 whole, which is shorter than its diff:
```python
import functools

import jax
import jax.numpy as jnp
from jax import lax
from jax.experimental import pallas as pl
from jax.experimental.pallas import tpu as pltpu
from jax.sharding import PartitionSpec as P

F32 = jnp.float32
BF16 = jnp.bfloat16
LANES = 128
SUBLANES = 8
VMEM = pl.BlockSpec(memory_space=pltpu.VMEM)
SMEM = pl.BlockSpec(memory_space=pltpu.SMEM)
HBM = pl.BlockSpec(memory_space=pltpu.HBM)


def partner(index, shift, count):
    if count & (count - 1) == 0:
        return index ^ shift
    return (index + shift) % count


def sender(index, shift, count):
    if count & (count - 1) == 0:
        return index ^ shift
    return (index - shift) % count


def split(value):
    high = value.astype(BF16)
    return high, (value - high.astype(F32)).astype(BF16)


def dot3(value, high, low):
    rows = value.shape[0]
    value_high, value_low = split(value)
    both = jnp.dot(
        jnp.concatenate([value_high, value_low], 0), high, preferred_element_type=F32
    )
    cross = jnp.dot(value_high, low, preferred_element_type=F32)
    return both[:rows] + (both[rows:] + cross)


HEADROOM = 13.0
SMALLEST = 2.0**-100


def scaled(chunk):
    largest = jnp.max(jnp.max(jnp.abs(chunk), axis=0, keepdims=True), axis=1, keepdims=True)
    power = jnp.floor(jnp.log2(jnp.maximum(largest, SMALLEST)))
    return chunk * jnp.exp2(HEADROOM - power), power


def unscaled(packed, size, row):
    return packed[:size] * jnp.exp2(packed[row : row + 1] - HEADROOM)


def start_slots(counts, kernels, kernel_buffer, sems):
    for slot in range(kernel_buffer.shape[0]):

        @pl.when(slot < counts[0, 0])
        def _():
            pltpu.make_async_copy(
                kernels.at[slot], kernel_buffer.at[slot], sems.at[slot]
            ).start()


def sum_slots(counts, offsets, history, kernels, kernel_buffer, sems, total, span):
    steps = history.shape[0] - span
    loads, columns = history.shape[1:]
    total[...] = jnp.zeros_like(total)

    def add(slot, carry):
        pltpu.make_async_copy(
            kernels.at[slot], kernel_buffer.at[slot], sems.at[slot]
        ).wait()
        window = history[pl.ds(span - offsets[0, 0, slot], steps)]
        total[...] += jnp.dot(
            window.reshape(steps * loads, columns),
            kernel_buffer[slot],
            preferred_element_type=F32,
        )
        return carry

    lax.fori_loop(0, counts[0, 0], add, 0)


def split_loads(total, strided, by_load, loads, steps):
    for group in range(total.shape[1] // LANES):
        lanes = slice(group * LANES, (group + 1) * LANES)
        strided[group] = total[:, lanes]
        for load in range(loads):
            by_load[load, :, lanes] = strided[group, pl.ds(load, steps, stride=loads), :]


def write_chunks(by_load, outs, share, row, sources):
    loads, steps, rows = by_load.shape
    size = share * steps
    source = lax.axis_index("src")
    for index, out in enumerate(outs):
        first = partner(source, index, sources) * share % loads
        for item in range(share):
            out[item * steps : (item + 1) * steps] = by_load[first + item]
        if index > 0:
            out[:size], power = scaled(out[:size])
            out[row : row + 1] = jnp.broadcast_to(power, (1, rows))
        else:
            out[row : row + 1] = jnp.full((1, rows), HEADROOM, F32)


def far_first_kernel(
    span, couplings, share, sources, ratio, counts, offsets, past, kernels, *refs
):
    (*outs, history, kernel_buffer, total, strided, by_load, sems, past_sem) = refs
    fetched = pltpu.make_async_copy(past, history, past_sem)
    fetched.start()
    start_slots(counts, kernels, kernel_buffer, sems)
    steps = history.shape[0] - span
    loads = history.shape[1]
    rows = total.shape[1]
    size = share * steps
    fetched.wait()
    sum_slots(counts, offsets, history, kernels, kernel_buffer, sems, total, span)
    split_loads(total, strided, by_load, loads, steps)
    target, source = lax.axis_index("tgt"), lax.axis_index("src")
    holds = source == target // ratio
    at = pl.multiple_of(target % ratio * rows, LANES)
    recent = history[history.shape[0] - couplings :, :, pl.ds(at, rows)].astype(F32)
    recent = jnp.where(holds, recent, jnp.zeros_like(recent))
    for step in range(couplings):
        for group in range(rows // LANES):
            strided[group, step * loads : (step + 1) * loads] = recent[
                step, :, group * LANES : (group + 1) * LANES
            ]
    for index, out in enumerate(outs):
        first = partner(source, index, sources) * share % loads
        out[size:] = jnp.zeros_like(out[size:])
        for item in range(share):
            for step in range(couplings):
                row = size + item * couplings + step
                for group in range(rows // LANES):
                    out[row : row + 1, group * LANES : (group + 1) * LANES] = strided[
                        group, pl.ds(step * loads + first + item, 1), :
                    ]
    write_chunks(by_load, outs, share, size + share * couplings, sources)


def far_next_kernel(
    span, couplings, share, sources, ratio, counts, offsets, firsts, past, kernels, *refs
):
    arrived, refs = refs[: sources * ratio], refs[sources * ratio :]
    (*outs, kernel_buffer, total, strided, by_load, stage, history, sems, past_sem) = refs
    steps = history.shape[0] - span
    loads, columns = history.shape[1:]
    rows = total.shape[1]
    start_slots(counts, kernels, kernel_buffer, sems)
    tail = pltpu.make_async_copy(
        past.at[pl.ds(steps, span)], history.at[pl.ds(0, span)], past_sem
    )
    tail.start()
    own = lax.axis_index("tgt") % ratio
    for index in range(sources):
        first = firsts[0, 0, index]
        for turn in range(ratio):
            chunk = arrived[turn * sources + index]
            part = lax.rem(own + ratio - turn, ratio)
            for item in range(share):
                stage[part, first + item] = chunk[
                    item * steps : (item + 1) * steps
                ].astype(F32)
    for group in range(columns // LANES):
        part, at = divmod(group * LANES, rows)
        for load in range(loads):
            strided[group, pl.ds(load, steps, stride=loads), :] = stage[
                part, load, :, at : at + LANES
            ]
        history[span:, :, group * LANES : (group + 1) * LANES] = (
            strided[group].reshape(steps, loads, LANES).astype(BF16)
        )
    tail.wait()
    sum_slots(counts, offsets, history, kernels, kernel_buffer, sems, total, span)
    split_loads(total, strided, by_load, loads, steps)
    write_chunks(by_load, outs, share, share * steps, sources)


def prepare_kernel(levels, couplings, inverse, *refs):
    (
        inverse_high,
        inverse_low,
        coupling_high,
        coupling_low,
        first_high,
        first_low,
        *powers,
        matrix,
    ) = refs
    count, rows, _ = couplings.shape
    high, low = split(inverse[...])
    inverse_high[...] = high
    inverse_low[...] = low
    matrix[...] = jnp.zeros_like(matrix)
    identity = (
        lax.broadcasted_iota(jnp.int32, (rows, rows), 0)
        == lax.broadcasted_iota(jnp.int32, (rows, rows), 1)
    ).astype(F32)
    for lag in range(count):
        coupling_high[lag], coupling_low[lag] = split(couplings[lag])
        matrix[lag * rows : (lag + 1) * rows, :rows] = -dot3(couplings[lag], high, low)
        if lag + 1 < count:
            matrix[
                lag * rows : (lag + 1) * rows, (lag + 1) * rows : (lag + 2) * rows
            ] = identity
    first_high[...], first_low[...] = split(matrix[:rows, :rows])
    power_high, power_low = split(matrix[...])
    for level in range(1, levels):
        wide = powers[2 * (level - 1)].shape[1]
        product = dot3(matrix[...], power_high[:, :wide], power_low[:, :wide])
        power_high, power_low = split(product)
        powers[2 * (level - 1)][...] = power_high
        powers[2 * (level - 1) + 1][...] = power_low
        if level + 1 < levels:
            matrix[...] = product


def solve_kernel(steps, share, levels, parts, packed, *refs):
    partials, refs = refs[:parts], refs[parts:]
    (
        driving,
        earlier,
        inverse_high,
        inverse_low,
        coupling_high,
        coupling_low,
        first_high,
        first_low,
        *powers,
    ) = refs[: 8 + 2 * (levels - 1)]
    solved, rounded, state, sent = refs[8 + 2 * (levels - 1) :]
    count, rows, _ = coupling_high.shape
    size = share * steps
    power_row = size + share * count if packed else size
    adjusted = driving[...].astype(F32)
    for partial in partials:
        adjusted = adjusted - unscaled(partial, size, power_row)
    row_of = lax.broadcasted_iota(jnp.int32, (size, 1), 0)
    padded = -(-share // SUBLANES) * SUBLANES
    if packed:
        known = partials[0][size:]
        for partial in partials[1:]:
            known = known + partial[size:]
    else:
        known = earlier[...]

    def back(lag):
        pieces = [
            known[item * count + count - lag : item * count + count - lag + 1]
            for item in range(share)
        ]
        pieces.append(jnp.zeros((padded - share, rows), F32))
        return jnp.concatenate(pieces, 0)

    for step in range(count):
        pull = None
        for lag in range(step + 1, count + 1):
            term = dot3(back(lag - step), coupling_high[lag - 1], coupling_low[lag - 1])
            pull = term if pull is None else pull + term
        for item in range(share):
            adjusted = adjusted - jnp.where(
                row_of == item * steps + step, pull[item : item + 1], 0.0
            )
    within = row_of % steps
    driven = dot3(adjusted, inverse_high[...], inverse_low[...])

    def delayed(value, delay):
        return jnp.where(within >= delay, pltpu.roll(value, delay, 0), 0.0)

    columns = [driven + delayed(dot3(driven, first_high[...], first_low[...]), 1)]
    if count > 1:
        columns.append(delayed(driven, 1))
    columns += [jnp.zeros_like(driven)] * (count - 2)
    total = jnp.concatenate(columns, 1)
    for level in range(1, levels):
        high, low = powers[2 * (level - 1)], powers[2 * (level - 1) + 1]
        wide = high.shape[1]
        total = total[:, :wide] + delayed(dot3(total, high[...], low[...]), 2**level)
    result = total[:, :rows]
    solved[...] = result
    rounded[...] = result.astype(BF16)
    sent[:size], power = scaled(result)
    sent[size:] = jnp.broadcast_to(power, (sent.shape[0] - size, rows))
    state[...] = jnp.zeros_like(state)
    for item in range(share):
        state[item * count : (item + 1) * count] = result[
            (item + 1) * steps - count : (item + 1) * steps
        ]


def spread_kernel(steps, share, own, *refs):
    (*chunks, out, by_load, strided) = refs
    loads, rows = out.shape[1:]
    sources = len(chunks) + 1
    size = share * steps
    source = lax.axis_index("src")
    for index, chunk in enumerate([own, *chunks]):
        first = sender(source, index, sources) * share % loads
        value = chunk[...] if index == 0 else unscaled(chunk, size, size)
        for item in range(share):
            by_load[first + item] = value[item * steps : (item + 1) * steps]
    for group in range(rows // LANES):
        lanes = slice(group * LANES, (group + 1) * LANES)
        for load in range(loads):
            strided[group, pl.ds(load, steps, stride=loads), :] = by_load[load, :, lanes]
        out[:, :, lanes] = strided[group].reshape(steps, loads, LANES)


def landing(plane, sources):
    shares = sorted(range(sources), key=lambda z: (-abs(z - plane), z))
    if sources & (sources - 1) == 0:
        chips = sorted(range(sources), key=lambda e: (bin(e ^ plane).count("1"), e))
    else:
        chips = sorted(range(sources), key=lambda e: (abs(e - plane), e))
    where = [0] * sources
    for one, chip in zip(shares, chips):
        where[one] = chip
    return where


def local(incident, past_density, kernels, lag_offset, lag_counts, couplings, inverse):
    all_steps, loads, rows = incident.shape
    columns = past_density.shape[2]
    slots = kernels.shape[0]
    span = lag_offset.shape[2]
    steps = past_density.shape[0] - span
    blocks = all_steps // steps
    count = couplings.shape[0]
    levels = steps.bit_length() - 1
    ratio = columns // rows
    sources = lax.axis_size("src")
    targets = lax.axis_size("tgt")
    target = lax.axis_index("tgt")
    source = lax.axis_index("src")
    share = max(loads // sources, 1)
    size = share * steps
    groups = rows // LANES
    pad = -(-(share * count + 1) // SUBLANES) * SUBLANES

    table = [landing(plane, sources) for plane in range(sources)]
    firsts = [
        [
            [
                table[plane].index(sender(chip, k, sources)) * share % loads
                for k in range(sources)
            ]
            for plane in range(sources)
        ]
        for chip in range(sources)
    ]
    firsts = lax.dynamic_slice(
        jnp.array(firsts, jnp.int32), (target // ratio, source, 0), (1, 1, sources)
    )

    def params(mebibytes):
        return pltpu.CompilerParams(vmem_limit_bytes=mebibytes * 2**20)

    def cost(work):
        return pl.CostEstimate(flops=work * 10**9, bytes_accessed=0, transcendentals=0)

    def trade(value, shift):
        pairs = [(i, partner(i, shift, sources)) for i in range(sources)]
        return lax.ppermute(value, "src", pairs)

    def trade_each(values):
        return [
            trade(value.astype(jnp.float16), k).astype(F32)
            for k, value in enumerate(values, 1)
        ]

    prepared = pl.pallas_call(
        functools.partial(prepare_kernel, levels),
        out_shape=[jax.ShapeDtypeStruct((rows, rows), BF16)] * 2
        + [jax.ShapeDtypeStruct((count, rows, rows), BF16)] * 2
        + [jax.ShapeDtypeStruct((rows, rows), BF16)] * 2
        + [jax.ShapeDtypeStruct((count * rows, count * rows), BF16)] * (2 * (levels - 2))
        + [jax.ShapeDtypeStruct((count * rows, rows), BF16)] * 2,
        in_specs=[VMEM, VMEM],
        out_specs=[VMEM] * (6 + 2 * (levels - 1)),
        scratch_shapes=[pltpu.VMEM((count * rows, count * rows), F32)],
        compiler_params=params(16),
        cost_estimate=cost(5),
        name="prepare",
    )(couplings, inverse)

    def solve(partials, driving, earlier, packed):
        operands = [*partials, driving, earlier, *prepared]
        return pl.pallas_call(
            functools.partial(solve_kernel, steps, share, levels, len(partials), packed),
            out_shape=[
                jax.ShapeDtypeStruct((size, rows), F32),
                jax.ShapeDtypeStruct((size, rows), BF16),
                jax.ShapeDtypeStruct((pad, rows), F32),
                jax.ShapeDtypeStruct((size + SUBLANES, rows), F32),
            ],
            in_specs=[VMEM] * len(operands),
            out_specs=[VMEM] * 4,
            compiler_params=params(12),
            cost_estimate=cost(3),
            name="solve",
        )(*operands)

    def spread(own, chunks):
        return pl.pallas_call(
            functools.partial(spread_kernel, steps, share),
            out_shape=jax.ShapeDtypeStruct((steps, loads, rows), F32),
            in_specs=[VMEM] * sources,
            out_specs=VMEM,
            scratch_shapes=[
                pltpu.VMEM((loads, steps, rows), F32),
                pltpu.VMEM((groups, steps * loads, LANES), F32),
            ],
            compiler_params=params(8),
            name="spread",
        )(own, *chunks)

    own_incident = lax.dynamic_slice_in_dim(incident, source * share % loads, share, 1)
    own_incident = own_incident.reshape(blocks, steps, share, rows)
    own_incident = own_incident.transpose(0, 2, 1, 3).reshape(blocks, size, rows)

    far_scratch = [
        pltpu.VMEM(kernels.shape, BF16),
        pltpu.VMEM((steps * loads, rows), F32),
        pltpu.VMEM((columns // LANES, steps * loads, LANES), F32),
        pltpu.VMEM((loads, steps, rows), F32),
    ]
    far_sems = [pltpu.SemaphoreType.DMA((slots,)), pltpu.SemaphoreType.DMA]
    history_scratch = pltpu.VMEM((span + steps, loads, columns), BF16)

    partials = pl.pallas_call(
        functools.partial(far_first_kernel, span, count, share, sources, ratio),
        out_shape=[jax.ShapeDtypeStruct((size + pad, rows), F32)] * sources,
        in_specs=[SMEM, SMEM, HBM, HBM],
        out_specs=[VMEM] * sources,
        scratch_shapes=[history_scratch, *far_scratch, *far_sems],
        compiler_params=params(12),
        cost_estimate=cost(2),
        name="far_first",
    )(lag_counts, lag_offset, past_density, kernels)

    state = jnp.zeros((pad, rows), F32)
    produced = []
    for block in range(blocks):
        if block > 0:
            moves = [
                (
                    (one * ratio + part) * sources + z,
                    (table[one][z] * ratio + part) * sources + one,
                )
                for one in range(sources)
                for part in range(ratio)
                for z in range(sources)
            ]
            landed = lax.ppermute(rounded, ("tgt", "src"), moves)
            chunks = trade_each([sent] * (sources - 1))
            arrived = [landed]
            for k in range(1, sources):
                pairs = [
                    (e * ratio + part, partner(e, k, sources) * ratio + part)
                    for e in range(sources)
                    for part in range(ratio)
                ]
                arrived.append(lax.ppermute(landed, "tgt", pairs))
            swapped = []
            for turn in range(1, ratio):
                pairs = [
                    (e * ratio + part, e * ratio + (part + turn) % ratio)
                    for e in range(sources)
                    for part in range(ratio)
                ]
                swapped += [lax.ppermute(chunk, "tgt", pairs) for chunk in arrived]
            partials = pl.pallas_call(
                functools.partial(far_next_kernel, span, count, share, sources, ratio),
                out_shape=[jax.ShapeDtypeStruct((size + SUBLANES, rows), F32)] * sources,
                in_specs=[SMEM, SMEM, SMEM, HBM, HBM] + [VMEM] * (sources * ratio),
                out_specs=[VMEM] * sources,
                scratch_shapes=far_scratch
                + [pltpu.VMEM((ratio, loads, steps, rows), F32), history_scratch]
                + far_sems,
                compiler_params=params(12),
                cost_estimate=cost(3),
                name="far_next",
            )(lag_counts, lag_offset, firsts, past_density, kernels, *arrived, *swapped)
            produced.append(spread(solved, chunks))
        received = [partials[0]] + trade_each(partials[1:])
        solved, rounded, state, sent = solve(
            received, own_incident[block], state, block == 0
        )
    produced.append(spread(solved, trade_each([sent] * (sources - 1))))
    return jnp.concatenate(produced, 0)


def solution(mesh):
    return jax.shard_map(
        local,
        mesh=mesh,
        in_specs=(
            P(None, None, "tgt"),
            P(None, None, "src"),
            P(None, "src", "tgt"),
            P("tgt", "src", None),
            P("tgt", "src"),
            P(None, "tgt", None),
            P("tgt", None),
        ),
        out_specs=P(None, None, "tgt"),
        check_vma=False,
    )
```

time: 108 us -> 64.6 us (0.60)
  local copies, waits for them, and re-layouts: 26.8 us -> 5.41 us
  waiting for transfers between devices: 25.7 us -> 13.8 us
  starting transfers between devices: 33.7 us -> 26.9 us
  between operations: 3.86 us -> 1.52 us
  Pallas kernels: 16.3 us -> 15.1 us
    ppermute x12, waiting for transfers between devices: 19.5 us -> 5.79 us  [trade(): return lax.ppermute(value, 'src', pairs)]
    another operation x3 -> x0, local copies, waits for them, and re-layouts: 11 us -> none  [the longest x1 5.08 us: local(): ints_next = jnp.stack(scalars + wanted + arrived).astype(jnp.int32)]
    unnamed x83, local copies, waits for them, and re-layouts: 8.86 us -> 4.57 us
    gather x2 -> x0, local copies, waits for them, and re-layouts: 3.73 us -> none  [local(): every = every[:, order]]
    ppermute x12, starting transfers between devices: 25 us -> 21.9 us  [trade(): return lax.ppermute(value, 'src', pairs)]
    ppermute x1, waiting for transfers between devices: 2.91 us -> 4.84 us  [local(): landed = lax.ppermute(rounded, ('tgt', 'src'), moves)]
    ppermute x1, starting transfers between devices: 3.18 us -> 1.28 us  [local(): landed = lax.ppermute(rounded, ('tgt', 'src'), moves)]
    ppermute x4 -> x7, starting transfers between devices: 5.52 us -> 3.71 us  [the longest x3 3.49 us: local(): arrived.append(lax.ppermute(landed, 'tgt', pairs))]
  transfers between devices with their start and end apart: 17 -> 20, of which waited for: 8 -> 8; matrix products, arithmetic and copies ran while one was open for 6% -> 2% of each run, Pallas kernels for 8% -> 12%
where the time goes in v2:
time: 64.6 us; the launch traced here: 64 us
  starting transfers between devices  26.9 us (42%)
  Pallas kernels  15.1 us (23%)
  waiting for transfers between devices  13.8 us (21%)
  local copies, waits for them, and re-layouts  5.41 us (8%)
  between operations  1.52 us (2%)
  other arithmetic  1.26 us (2%)
    ppermute x12, starting transfers between devices, trade(): return lax.ppermute(value, 'src', pairs)  21.9 us
    ppermute x12, waiting for transfers between devices, trade(): return lax.ppermute(value, 'src', pairs)  5.79 us
    pallas_call x2, Pallas kernels, solve(): pl.pallas_call(functools.partial(solve_kernel, steps, share, levels, len(...  5.37 us
    ppermute x1, waiting for transfers between devices, local(): landed = lax.ppermute(rounded, ('tgt', 'src'), moves)  4.84 us
    pallas_call x1, Pallas kernels, local(): pl.pallas_call(functools.partial(prepare_kernel, levels), out_shape=[jax....  4.78 us
    unnamed x83, local copies, waits for them, and re-layouts  4.57 us
    ppermute x3, starting transfers between devices, local(): arrived.append(lax.ppermute(landed, 'tgt', pairs))  3.49 us
    ppermute x3, waiting for transfers between devices, local(): arrived.append(lax.ppermute(landed, 'tgt', pairs))  2.79 us
  transfers between devices with their start and end apart: 20, of which 8 were waited for; matrix products, arithmetic and copies ran while one was open for 2% of the time, Pallas kernels for 12%

profile of v2, /device:TPU:0, one launch (start us, length us, event | category | flops | bytes accessed | tf_op | source)
XLA Modules:
  0.0 64.0 jit_solution(15357388599997764256)
XLA Ops:
  0.7 1.6 %copy-done.1 = bf16[8,512,256]{2,1,0:T(8,128)(2,1)S(1)} copy-done((bf16[8,512,256]{2,1,0:T(8,128)(2,1)S(1)}, bf16[8,512,256]{2,1,0:T(8,128)(2,1)}, u32[]{:S(2)}) %copy-start.1) | copy-done | bytes 2097176
  2.3 1.1 %copy-done.3 = bf16[76,8,512]{2,1,0:T(8,128)(2,1)S(1)} copy-done((bf16[76,8,512]{2,1,0:T(8,128)(2,1)S(1)}, bf16[76,8,512]{2,1,0:T(8,128)(2,1)}, u32[]{:S(2)}) %copy-start.3) | copy-done | bytes 622616
  3.4 0.7 %copy-done.7 = s32[1,1,12]{2,1,0:T(1,128)S(1)} copy-done((s32[1,1,12]{2,1,0:T(1,128)S(1)}, s32[1,1,12]{2,1,0:T(1,128)}, u32[]{:S(2)}) %copy-start.7) | copy-done | bytes 72
  4.0 2.1 %far_first.1 = (f32[136,256]{1,0:T(8,128)S(1)}, f32[136,256]{1,0:T(8,128)S(1)}, f32[136,256]{1,0:T(8,128)S(1)}, f32[136,256]{1,0:T(8,128)S(1)}) custom-call(s32[1,1]{1,0:T(1,128)S(6)} %copy.11.counts, s32[1,1,12]{2,1,0:T(1,128)S(1)} %copy-done.7, bf16[76,8,512]{2,1,0:T(8,128)(2,1)S(1)} %copy-done.3, bf16[8,512,256]{2,1,0:T(8,128)(2,1)S(1)} %copy-done.1), custom_call_target="tpu_custom_call" | custom-call | flops 2000000000 | tf_op jit(solution)/shard_map/far_first/pallas_call | solution.py:439
  6.2 6.7 %collective-permute-start.2 = (f16[136,256]{1,0:T(8,128)(2,1)S(1)}, f16[136,256]{1,0:T(8,128)(2,1)S(1)}, u32[]{:S(2)}, u32[]{:S(2)}) collective-permute-start(f16[136,256]{1,0:T(8,128)(2,1)S(1)} %convert_element_type.68), channel_id=1, source_target_pairs={{0,3},{1,2},{2,1},{3,0},{4,7},{5,6},{6,5},{7,4},{8,11},{9,10},{10,... | collective-permute-start | bytes 208904 | tf_op jit(solution)/shard_map/ppermute | solution.py:372
  13.0 0.6 collective-permute-start
  13.8 4.8 %prepare.1 = (bf16[256,256]{1,0:T(8,128)(2,1)S(1)}, bf16[256,256]{1,0:T(8,128)(2,1)S(1)}, bf16[2,256,256]{2,1,0:T(8,128)(2,1)S(1)}, bf16[2,256,256]{2,1,0:T(8,12...) custom-call(f32[2,256,256]{2,1,0:T(8,128)S(1)} %copy-done.5, ...), custom_call_target="tpu_custom_call" | custom-call | flops 5000000000 | tf_op jit(solution)/shard_map/prepare/pallas_call | solution.py:380
  18.9 2.4 %solve.2 = (f32[128,256]{1,0:T(8,128)S(1)}, bf16[128,256]{1,0:T(8,128)(2,1)S(1)}, f32[8,256]{1,0:T(8,128)S(1)}, f32[136,256]{1,0:T(8,128)S(1)}) custom-call(f32[136,256]{1,0:T(8,128)S(1)} %copy-done.32, f32[136,256]{1,0:T(8,128)S(1)} %convert_element_type.65.refs_1_, f32[136,256]{1,0:T(8,128)S(1)} %convert_element_type.67.refs_2_, ...), custom_call_target="tpu_custom_call" | custom-call | flops 3000000000 | tf_op jit(solution)/shard_map/solve/pallas_call | solution.py:397
  21.5 1.3 %collective-permute-start.6 = (bf16[128,256]{1,0:T(8,128)(2,1)S(1)}, bf16[128,256]{1,0:T(8,128)(2,1)S(1)}, u32[]{:S(2)}, u32[]{:S(2)}) collective-permute-start(bf16[128,256]{1,0:T(8,128)(2,1)S(1)} %get-tuple-element.57), channel_id=1, source_target_pairs={{0,24},{1,16},{2,8},{3,0},{4,28},{5,20},{6,12},{7,4},{8,1},{9,17},... | collective-permute-start | bytes 196616 | tf_op jit(solution)/shard_map/ppermute | solution.py:463
  22.7 4.8 %collective-permute-done.6.refs_0_ = bf16[128,256]{1,0:T(8,128)(2,1)S(1)} collective-permute-done((bf16[128,256]{1,0:T(8,128)(2,1)S(1)}, bf16[128,256]{1,0:T(8,128)(2,1)S(1)}, u32[]{:S(2)}, u32[]{:S(2)}) %collective-permute-start.6) | collective-permute-done | bytes 65568 | tf_op jit(solution)/shard_map/ppermute | solution.py:463
  27.6 1.7 %collective-permute-start.9 = (bf16[128,256]{1,0:T(8,128)(2,1)S(1)}, bf16[128,256]{1,0:T(8,128)(2,1)S(1)}, u32[]{:S(2)}, u32[]{:S(2)}) collective-permute-start(bf16[128,256]{1,0:T(8,128)(2,1)S(1)} %collective-permute-done.6.refs_0_), channel_id=1, source_target_pairs={{0,24},{4,28},{8,16},{12,20},{16,8},{20,12},{24,0},{28,4},{1,25},{... | collective-permute-start | bytes 196616 | tf_op jit(solution)/shard_map/ppermute | solution.py:472
  29.3 0.3 collective-permute-start.8
  29.6 1.5 %collective-permute-start.7 = (bf16[128,256]{1,0:T(8,128)(2,1)S(1)}, bf16[128,256]{1,0:T(8,128)(2,1)S(1)}, u32[]{:S(2)}, u32[]{:S(2)}) collective-permute-start(bf16[128,256]{1,0:T(8,128)(2,1)S(1)} %collective-permute-done.6.refs_0_), channel_id=1, source_target_pairs={{0,8},{4,12},{8,0},{12,4},{16,24},{20,28},{24,16},{28,20},{1,9},{5... | collective-permute-start | bytes 196616 | tf_op jit(solution)/shard_map/ppermute | solution.py:472
  31.1 1.7 %collective-permute-done.9.refs_3_ = bf16[128,256]{1,0:T(8,128)(2,1)S(1)} collective-permute-done((bf16[128,256]{1,0:T(8,128)(2,1)S(1)}, bf16[128,256]{1,0:T(8,128)(2,1)S(1)}, u32[]{:S(2)}, u32[]{:S(2)}) %collective-permute-start.9) | collective-permute-done | bytes 65568 | tf_op jit(solution)/shard_map/ppermute | solution.py:472
  32.8 0.8 %collective-permute-done.8.refs_2_ = bf16[128,256]{1,0:T(8,128)(2,1)S(1)} collective-permute-done((bf16[128,256]{1,0:T(8,128)(2,1)S(1)}, bf16[128,256]{1,0:T(8,128)(2,1)S(1)}, u32[]{:S(2)}, u32[]{:S(2)}) %collective-permute-start.8) | collective-permute-done | bytes 65568 | tf_op jit(solution)/shard_map/ppermute | solution.py:472
  33.6 0.3 collective-permute-done.7.refs_1_
  33.9 0.2 collective-permute-start.11
  34.1 0.7 %constant_dynamic-slice_fusion.firsts = s32[1,1,4]{2,1,0:T(1,128)S(1)} fusion(s32[4,4,4]{2,1,0:T(4,128)} %constant.43.clone, s32[]{:T(128)S(6)} %select_n.23, s32[]{:T(128)S(6)} %select_n.24), kind=kLoop, calls=%fused_computation.1 | loop fusion | bytes 40 | tf_op jit(solution)/shard_map/dynamic_slice | solution.py:360
  34.8 0.3 collective-permute-done.11.refs_5_
  35.1 1.1 %copy-done.4 = bf16[76,8,512]{2,1,0:T(8,128)(2,1)S(1)} copy-done((bf16[76,8,512]{2,1,0:T(8,128)(2,1)S(1)}, bf16[76,8,512]{2,1,0:T(8,128)(2,1)}, u32[]{:S(2)}) %copy-start.4) | copy-done | bytes 622616
  36.3 2.5 %far_next.1 = (f32[136,256]{1,0:T(8,128)S(1)}, f32[136,256]{1,0:T(8,128)S(1)}, f32[136,256]{1,0:T(8,128)S(1)}, f32[136,256]{1,0:T(8,128)S(1)}) custom-call(s32[1,1]{1,0:T(1,128)S(6)} %copy.11.counts, s32[1,1,12]{2,1,0:T(1,128)S(1)} %copy-done.8, s32[1,1,4]{2,1,0:T(1,128)S(1)} %constant_dynamic-slice_fusion.firsts, bf16[76,8,512]{2,1,0:T(8,128)(2,1)S(1)} %copy-done.4, ...), custom_call_target="tpu_custom_call" | custom-call | flops 3000000000 | tf_op jit(solution)/shard_map/far_next/pallas_call | solution.py:481
  38.8 4.8 %collective-permute-start.16 = (f16[136,256]{1,0:T(8,128)(2,1)S(1)}, f16[136,256]{1,0:T(8,128)(2,1)S(1)}, u32[]{:S(2)}, u32[]{:S(2)}) collective-permute-start(f16[136,256]{1,0:T(8,128)(2,1)S(1)} %convert_element_type.78), channel_id=1, source_target_pairs={{0,3},{1,2},{2,1},{3,0},{4,7},{5,6},{6,5},{7,4},{8,11},{9,10},{10,... | collective-permute-start | bytes 208904 | tf_op jit(solution)/shard_map/ppermute | solution.py:372
  43.8 0.6 collective-permute-start.14
  44.4 3.9 %collective-permute-start.5 = (f16[136,256]{1,0:T(8,128)(2,1)S(1)}, f16[136,256]{1,0:T(8,128)(2,1)S(1)}, u32[]{:S(2)}, u32[]{:S(2)}) collective-permute-start(f16[136,256]{1,0:T(8,128)(2,1)S(1)} %convert_element_type.70), channel_id=1, source_target_pairs={{0,3},{1,2},{2,1},{3,0},{4,7},{5,6},{6,5},{7,4},{8,11},{9,10},{10,... | collective-permute-start | bytes 208904 | tf_op jit(solution)/shard_map/ppermute | solution.py:372
  48.3 0.6 %collective-permute-start.3 = (f16[136,256]{1,0:T(8,128)(2,1)S(1)}, f16[136,256]{1,0:T(8,128)(2,1)S(1)}, u32[]{:S(2)}, u32[]{:S(2)}) collective-permute-start(f16[136,256]{1,0:T(8,128)(2,1)S(1)} %convert_element_type.70), channel_id=1, source_target_pairs={{0,1},{1,0},{2,3},{3,2},{4,5},{5,4},{6,7},{7,6},{8,9},{9,8},{10,11... | collective-permute-start | bytes 208904 | tf_op jit(solution)/shard_map/ppermute | solution.py:372
  49.0 3.3 %collective-permute-done.15 = f16[136,256]{1,0:T(8,128)(2,1)S(1)} collective-permute-done((f16[136,256]{1,0:T(8,128)(2,1)S(1)}, f16[136,256]{1,0:T(8,128)(2,1)S(1)}, u32[]{:S(2)}, u32[]{:S(2)}) %collective-permute-start.15) | collective-permute-done | bytes 69664 | tf_op jit(solution)/shard_map/ppermute | solution.py:372
  52.4 3.0 %solve.3 = (f32[128,256]{1,0:T(8,128)S(1)}, bf16[128,256]{1,0:T(8,128)(2,1)}, f32[8,256]{1,0:T(8,128)}, f32[136,256]{1,0:T(8,128)S(1)}) custom-call(f32[136,256]{1,0:T(8,128)S(1)} %get-tuple-element.58.refs_0_, f32[136,256]{1,0:T(8,128)S(1)} %convert_element_type.75.refs_1_, f32[136,256]{1,0:T(8,128)S(1)} %convert_element_type.77.refs_2_, ...), custom_call_target="tpu_custom_call" | custom-call | flops 3000000000 | tf_op jit(solution)/shard_map/solve/pallas_call | solution.py:397
  55.4 0.6 collective-permute-start.19
  56.0 3.9 %collective-permute-start.17 = (f16[136,256]{1,0:T(8,128)(2,1)S(1)}, f16[136,256]{1,0:T(8,128)(2,1)S(1)}, u32[]{:S(2)}, u32[]{:S(2)}) collective-permute-start(f16[136,256]{1,0:T(8,128)(2,1)S(1)} %convert_element_type.80), channel_id=1, source_target_pairs={{0,1},{1,0},{2,3},{3,2},{4,5},{5,4},{6,7},{7,6},{8,9},{9,8},{10,11... | collective-permute-start | bytes 208904 | tf_op jit(solution)/shard_map/ppermute | solution.py:372
  60.1 1.6 %collective-permute-done.19 = f16[136,256]{1,0:T(8,128)(2,1)S(1)} collective-permute-done((f16[136,256]{1,0:T(8,128)(2,1)S(1)}, f16[136,256]{1,0:T(8,128)(2,1)S(1)}, u32[]{:S(2)}, u32[]{:S(2)}) %collective-permute-start.19) | collective-permute-done | bytes 69664 | tf_op jit(solution)/shard_map/ppermute | solution.py:372
  61.7 1.0 %collective-permute-done.18 = f16[136,256]{1,0:T(8,128)(2,1)S(1)} collective-permute-done((f16[136,256]{1,0:T(8,128)(2,1)S(1)}, f16[136,256]{1,0:T(8,128)(2,1)S(1)}, u32[]{:S(2)}, u32[]{:S(2)}) %collective-permute-start.18) | collective-permute-done | bytes 69664 | tf_op jit(solution)/shard_map/ppermute | solution.py:372
  62.9 1.0 %pad_maximum_fusion = f32[128,8,256]{2,1,0:T(8,128)} fusion(f32[64,8,256]{2,1,0:T(8,128)S(1)} %spread.3, f32[64,8,256]{2,1,0:T(8,128)S(1)} %spread.2), kind=kLoop, calls=%fused_computation | loop fusion | flops 262144 | bytes 2097152 | tf_op jit(solution)/shard_map/concatenate | solution.py:499
  (123 shorter events, 1.2 us)
Async XLA Ops:
  6.2 12.6 %collective-permute-start.2 = (f16[136,256]{1,0:T(8,128)(2,1)S(1)}, f16[136,256]{1,0:T(8,128)(2,1)S(1)}, u32[]{:S(2)}, u32[]{:S(2)}) collective-permute-start(f16[136,256]{1,0:T(8,128)(2,1)S(1)} %convert_element_type.68), channel_id=1, source_target_pairs={{0,3},{1,2},{2,1},{3,0},{4,7},{5,6},{6,5},{7,4},{8,11},{9,10},{10,... | collective-permute-start | bytes 208904 | tf_op jit(solution)/shard_map/ppermute | solution.py:372
  12.9 5.9 %collective-permute-start.1 = (f16[136,256]{1,0:T(8,128)(2,1)S(1)}, f16[136,256]{1,0:T(8,128)(2,1)S(1)}, u32[]{:S(2)}, u32[]{:S(2)}) collective-permute-start(f16[136,256]{1,0:T(8,128)(2,1)S(1)} %convert_element_type.66), channel_id=1, source_target_pairs={{0,2},{1,3},{2,0},{3,1},{4,6},{5,7},{6,4},{7,5},{8,10},{9,11},{10,... | collective-permute-start | bytes 208904 | tf_op jit(solution)/shard_map/ppermute | solution.py:372
  13.0 5.9 %collective-permute-start = (f16[136,256]{1,0:T(8,128)(2,1)S(1)}, f16[136,256]{1,0:T(8,128)(2,1)S(1)}, u32[]{:S(2)}, u32[]{:S(2)}) collective-permute-start(f16[136,256]{1,0:T(8,128)(2,1)S(1)} %convert_element_type.64), channel_id=1, source_target_pairs={{0,1},{1,0},{2,3},{3,2},{4,5},{5,4},{6,7},{7,6},{8,9},{9,8},{10,11... | collective-permute-start | bytes 208904 | tf_op jit(solution)/shard_map/ppermute | solution.py:372
  18.9 16.3 %copy-start.2 = (bf16[8,512,256]{2,1,0:T(8,128)(2,1)S(1)}, bf16[8,512,256]{2,1,0:T(8,128)(2,1)}, u32[]{:S(2)}) copy-start(bf16[8,512,256]{2,1,0:T(8,128)(2,1)} %kernels.3) | copy-start | bytes 6291460
  18.9 16.3 %copy-start.8 = (s32[1,1,12]{2,1,0:T(1,128)S(1)}, s32[1,1,12]{2,1,0:T(1,128)}, u32[]{:S(2)}) copy-start(s32[1,1,12]{2,1,0:T(1,128)} %offsets.3) | copy-start | bytes 148
  21.5 6.1 %collective-permute-start.6 = (bf16[128,256]{1,0:T(8,128)(2,1)S(1)}, bf16[128,256]{1,0:T(8,128)(2,1)S(1)}, u32[]{:S(2)}, u32[]{:S(2)}) collective-permute-start(bf16[128,256]{1,0:T(8,128)(2,1)S(1)} %get-tuple-element.57), channel_id=1, source_target_pairs={{0,24},{1,16},{2,8},{3,0},{4,28},{5,20},{6,12},{7,4},{8,1},{9,17},... | collective-permute-start | bytes 196616 | tf_op jit(solution)/shard_map/ppermute | solution.py:463
  27.6 5.2 %collective-permute-start.9 = (bf16[128,256]{1,0:T(8,128)(2,1)S(1)}, bf16[128,256]{1,0:T(8,128)(2,1)S(1)}, u32[]{:S(2)}, u32[]{:S(2)}) collective-permute-start(bf16[128,256]{1,0:T(8,128)(2,1)S(1)} %collective-permute-done.6.refs_0_), channel_id=1, source_target_pairs={{0,24},{4,28},{8,16},{12,20},{16,8},{20,12},{24,0},{28,4},{1,25},{... | collective-permute-start | bytes 196616 | tf_op jit(solution)/shard_map/ppermute | solution.py:472
  29.3 4.3 %collective-permute-start.8 = (bf16[128,256]{1,0:T(8,128)(2,1)S(1)}, bf16[128,256]{1,0:T(8,128)(2,1)S(1)}, u32[]{:S(2)}, u32[]{:S(2)}) collective-permute-start(bf16[128,256]{1,0:T(8,128)(2,1)S(1)} %collective-permute-done.6.refs_0_), channel_id=1, source_target_pairs={{0,16},{4,20},{8,24},{12,28},{16,0},{20,4},{24,8},{28,12},{1,17},{... | collective-permute-start | bytes 196616 | tf_op jit(solution)/shard_map/ppermute | solution.py:472
  29.6 4.3 %collective-permute-start.7 = (bf16[128,256]{1,0:T(8,128)(2,1)S(1)}, bf16[128,256]{1,0:T(8,128)(2,1)S(1)}, u32[]{:S(2)}, u32[]{:S(2)}) collective-permute-start(bf16[128,256]{1,0:T(8,128)(2,1)S(1)} %collective-permute-done.6.refs_0_), channel_id=1, source_target_pairs={{0,8},{4,12},{8,0},{12,4},{16,24},{20,28},{24,16},{28,20},{1,9},{5... | collective-permute-start | bytes 196616 | tf_op jit(solution)/shard_map/ppermute | solution.py:472
  31.1 3.7 %collective-permute-start.10 = (bf16[128,256]{1,0:T(8,128)(2,1)S(1)}, bf16[128,256]{1,0:T(8,128)(2,1)S(1)}, u32[]{:S(2)}, u32[]{:S(2)}) collective-permute-start(bf16[128,256]{1,0:T(8,128)(2,1)S(1)} %collective-permute-done.6.refs_0_), channel_id=1, source_target_pairs={{0,4},{4,0},{8,12},{12,8},{16,20},{20,16},{24,28},{28,24},{1,5},{5... | collective-permute-start | bytes 196616 | tf_op jit(solution)/shard_map/ppermute | solution.py:480
  32.8 2.0 %collective-permute-start.13 = (bf16[128,256]{1,0:T(8,128)(2,1)S(1)}, bf16[128,256]{1,0:T(8,128)(2,1)S(1)}, u32[]{:S(2)}, u32[]{:S(2)}) collective-permute-start(bf16[128,256]{1,0:T(8,128)(2,1)S(1)} %collective-permute-done.9.refs_3_), channel_id=1, source_target_pairs={{0,4},{4,0},{8,12},{12,8},{16,20},{20,16},{24,28},{28,24},{1,5},{5... | collective-permute-start | bytes 196616 | tf_op jit(solution)/shard_map/ppermute | solution.py:480
  33.6 1.3 %collective-permute-start.12 = (bf16[128,256]{1,0:T(8,128)(2,1)S(1)}, bf16[128,256]{1,0:T(8,128)(2,1)S(1)}, u32[]{:S(2)}, u32[]{:S(2)}) collective-permute-start(bf16[128,256]{1,0:T(8,128)(2,1)S(1)} %collective-permute-done.8.refs_2_), channel_id=1, source_target_pairs={{0,4},{4,0},{8,12},{12,8},{16,20},{20,16},{24,28},{28,24},{1,5},{5... | collective-permute-start | bytes 196616 | tf_op jit(solution)/shard_map/ppermute | solution.py:480
  33.9 1.3 %collective-permute-start.11 = (bf16[128,256]{1,0:T(8,128)(2,1)S(1)}, bf16[128,256]{1,0:T(8,128)(2,1)S(1)}, u32[]{:S(2)}, u32[]{:S(2)}) collective-permute-start(bf16[128,256]{1,0:T(8,128)(2,1)S(1)} %collective-permute-done.7.refs_1_), channel_id=1, source_target_pairs={{0,4},{4,0},{8,12},{12,8},{16,20},{20,16},{24,28},{28,24},{1,5},{5... | collective-permute-start | bytes 196616 | tf_op jit(solution)/shard_map/ppermute | solution.py:480
  36.2 16.1 %copy-start.18 = (bf16[512,512]{1,0:T(8,128)(2,1)S(1)}, bf16[512,512]{1,0:T(8,128)(2,1)}, u32[]{:S(2)}) copy-start(bf16[512,512]{1,0:T(8,128)(2,1)} %copy-done.17) | copy-start | bytes 1572868
  36.2 16.1 %copy-start.20 = (bf16[512,512]{1,0:T(8,128)(2,1)S(1)}, bf16[512,512]{1,0:T(8,128)(2,1)}, u32[]{:S(2)}) copy-start(bf16[512,512]{1,0:T(8,128)(2,1)} %copy-done.19) | copy-start | bytes 1572868
  36.2 16.1 %copy-start.22 = (bf16[512,512]{1,0:T(8,128)(2,1)S(1)}, bf16[512,512]{1,0:T(8,128)(2,1)}, u32[]{:S(2)}) copy-start(bf16[512,512]{1,0:T(8,128)(2,1)} %copy-done.21) | copy-start | bytes 1572868
  36.3 16.1 %copy-start.24 = (bf16[512,512]{1,0:T(8,128)(2,1)S(1)}, bf16[512,512]{1,0:T(8,128)(2,1)}, u32[]{:S(2)}) copy-start(bf16[512,512]{1,0:T(8,128)(2,1)} %copy-done.23) | copy-start | bytes 1572868
  36.3 16.1 %copy-start.26 = (bf16[2,256,256]{2,1,0:T(8,128)(2,1)S(1)}, bf16[2,256,256]{2,1,0:T(8,128)(2,1)}, u32[]{:S(2)}) copy-start(bf16[2,256,256]{2,1,0:T(8,128)(2,1)} %copy-done.25) | copy-start | bytes 786436
  36.3 16.1 %copy-start.28 = (bf16[512,256]{1,0:T(8,128)(2,1)S(1)}, bf16[512,256]{1,0:T(8,128)(2,1)}, u32[]{:S(2)}) copy-start(bf16[512,256]{1,0:T(8,128)(2,1)} %copy-done.27) | copy-start | bytes 786436
  36.3 16.1 %copy-start.30 = (bf16[512,256]{1,0:T(8,128)(2,1)S(1)}, bf16[512,256]{1,0:T(8,128)(2,1)}, u32[]{:S(2)}) copy-start(bf16[512,256]{1,0:T(8,128)(2,1)} %copy-done.29) | copy-start | bytes 786436
  36.3 16.1 %copy-start.34 = (bf16[256,256]{1,0:T(8,128)(2,1)S(1)}, bf16[256,256]{1,0:T(8,128)(2,1)}, u32[]{:S(2)}) copy-start(bf16[256,256]{1,0:T(8,128)(2,1)} %copy-done.33) | copy-start | bytes 393220
  36.3 16.1 %copy-start.36 = (bf16[256,256]{1,0:T(8,128)(2,1)S(1)}, bf16[256,256]{1,0:T(8,128)(2,1)}, u32[]{:S(2)}) copy-start(bf16[256,256]{1,0:T(8,128)(2,1)} %copy-done.35) | copy-start | bytes 393220
  36.3 16.1 %copy-start.38 = (bf16[256,256]{1,0:T(8,128)(2,1)S(1)}, bf16[256,256]{1,0:T(8,128)(2,1)}, u32[]{:S(2)}) copy-start(bf16[256,256]{1,0:T(8,128)(2,1)} %copy-done.37) | copy-start | bytes 393220
  38.8 9.5 %collective-permute-start.16 = (f16[136,256]{1,0:T(8,128)(2,1)S(1)}, f16[136,256]{1,0:T(8,128)(2,1)S(1)}, u32[]{:S(2)}, u32[]{:S(2)}) collective-permute-start(f16[136,256]{1,0:T(8,128)(2,1)S(1)} %convert_element_type.78), channel_id=1, source_target_pairs={{0,3},{1,2},{2,1},{3,0},{4,7},{5,6},{6,5},{7,4},{8,11},{9,10},{10,... | collective-permute-start | bytes 208904 | tf_op jit(solution)/shard_map/ppermute | solution.py:372
  43.7 8.5 %collective-permute-start.15 = (f16[136,256]{1,0:T(8,128)(2,1)S(1)}, f16[136,256]{1,0:T(8,128)(2,1)S(1)}, u32[]{:S(2)}, u32[]{:S(2)}) collective-permute-start(f16[136,256]{1,0:T(8,128)(2,1)S(1)} %convert_element_type.76), channel_id=1, source_target_pairs={{0,2},{1,3},{2,0},{3,1},{4,6},{5,7},{6,4},{7,5},{8,10},{9,11},{10,... | collective-permute-start | bytes 208904 | tf_op jit(solution)/shard_map/ppermute | solution.py:372
  43.8 8.4 %collective-permute-start.14 = (f16[136,256]{1,0:T(8,128)(2,1)S(1)}, f16[136,256]{1,0:T(8,128)(2,1)S(1)}, u32[]{:S(2)}, u32[]{:S(2)}) collective-permute-start(f16[136,256]{1,0:T(8,128)(2,1)S(1)} %convert_element_type.74), channel_id=1, source_target_pairs={{0,1},{1,0},{2,3},{3,2},{4,5},{5,4},{6,7},{7,6},{8,9},{9,8},{10,11... | collective-permute-start | bytes 208904 | tf_op jit(solution)/shard_map/ppermute | solution.py:372
  44.4 11.5 %collective-permute-start.5 = (f16[136,256]{1,0:T(8,128)(2,1)S(1)}, f16[136,256]{1,0:T(8,128)(2,1)S(1)}, u32[]{:S(2)}, u32[]{:S(2)}) collective-permute-start(f16[136,256]{1,0:T(8,128)(2,1)S(1)} %convert_element_type.70), channel_id=1, source_target_pairs={{0,3},{1,2},{2,1},{3,0},{4,7},{5,6},{6,5},{7,4},{8,11},{9,10},{10,... | collective-permute-start | bytes 208904 | tf_op jit(solution)/shard_map/ppermute | solution.py:372
  48.3 11.5 %collective-permute-start.4 = (f16[136,256]{1,0:T(8,128)(2,1)S(1)}, f16[136,256]{1,0:T(8,128)(2,1)S(1)}, u32[]{:S(2)}, u32[]{:S(2)}) collective-permute-start(f16[136,256]{1,0:T(8,128)(2,1)S(1)} %convert_element_type.70), channel_id=1, source_target_pairs={{0,2},{1,3},{2,0},{3,1},{4,6},{5,7},{6,4},{7,5},{8,10},{9,11},{10,... | collective-permute-start | bytes 208904 | tf_op jit(solution)/shard_map/ppermute | solution.py:372
  48.3 11.6 %collective-permute-start.3 = (f16[136,256]{1,0:T(8,128)(2,1)S(1)}, f16[136,256]{1,0:T(8,128)(2,1)S(1)}, u32[]{:S(2)}, u32[]{:S(2)}) collective-permute-start(f16[136,256]{1,0:T(8,128)(2,1)S(1)} %convert_element_type.70), channel_id=1, source_target_pairs={{0,1},{1,0},{2,3},{3,2},{4,5},{5,4},{6,7},{7,6},{8,9},{9,8},{10,11... | collective-permute-start | bytes 208904 | tf_op jit(solution)/shard_map/ppermute | solution.py:372
  55.4 6.3 %collective-permute-start.19 = (f16[136,256]{1,0:T(8,128)(2,1)S(1)}, f16[136,256]{1,0:T(8,128)(2,1)S(1)}, u32[]{:S(2)}, u32[]{:S(2)}) collective-permute-start(f16[136,256]{1,0:T(8,128)(2,1)S(1)} %convert_element_type.80), channel_id=1, source_target_pairs={{0,3},{1,2},{2,1},{3,0},{4,7},{5,6},{6,5},{7,4},{8,11},{9,10},{10,... | collective-permute-start | bytes 208904 | tf_op jit(solution)/shard_map/ppermute | solution.py:372
  56.0 6.7 %collective-permute-start.18 = (f16[136,256]{1,0:T(8,128)(2,1)S(1)}, f16[136,256]{1,0:T(8,128)(2,1)S(1)}, u32[]{:S(2)}, u32[]{:S(2)}) collective-permute-start(f16[136,256]{1,0:T(8,128)(2,1)S(1)} %convert_element_type.80), channel_id=1, source_target_pairs={{0,2},{1,3},{2,0},{3,1},{4,6},{5,7},{6,4},{7,5},{8,10},{9,11},{10,... | collective-permute-start | bytes 208904 | tf_op jit(solution)/shard_map/ppermute | solution.py:372
  56.0 6.7 %collective-permute-start.17 = (f16[136,256]{1,0:T(8,128)(2,1)S(1)}, f16[136,256]{1,0:T(8,128)(2,1)S(1)}, u32[]{:S(2)}, u32[]{:S(2)}) collective-permute-start(f16[136,256]{1,0:T(8,128)(2,1)S(1)} %convert_element_type.80), channel_id=1, source_target_pairs={{0,1},{1,0},{2,3},{3,2},{4,5},{5,4},{6,7},{7,6},{8,9},{9,8},{10,11... | collective-permute-start | bytes 208904 | tf_op jit(solution)/shard_map/ppermute | solution.py:372
  (29 other events, 170.8 us)

commit v3 on v2

--- a/solution.py
+++ b/solution.py
@@ -70,119 +70,136 @@
 def sum_slots(counts, offsets, history, kernels, kernel_buffer, sems, total, span):
     steps = history.shape[0] - span
     loads, columns = history.shape[1:]
+    count = counts[0, 0]
     total[...] = jnp.zeros_like(total)
 
-    def add(slot, carry):
-        pltpu.make_async_copy(
-            kernels.at[slot], kernel_buffer.at[slot], sems.at[slot]
-        ).wait()
-        window = history[pl.ds(span - offsets[0, 0, slot], steps)]
-        total[...] += jnp.dot(
-            window.reshape(steps * loads, columns),
-            kernel_buffer[slot],
-            preferred_element_type=F32,
-        )
-        return carry
-
-    lax.fori_loop(0, counts[0, 0], add, 0)
-
-
-def split_loads(total, strided, by_load, loads, steps):
-    for group in range(total.shape[1] // LANES):
-        lanes = slice(group * LANES, (group + 1) * LANES)
-        strided[group] = total[:, lanes]
-        for load in range(loads):
-            by_load[load, :, lanes] = strided[group, pl.ds(load, steps, stride=loads), :]
-
-
-def write_chunks(by_load, outs, share, row, sources):
-    loads, steps, rows = by_load.shape
-    size = share * steps
-    source = lax.axis_index("src")
+    def window(slot):
+        taken = history[pl.ds(span - offsets[0, 0, slot], steps)]
+        return taken.reshape(steps * loads, columns)
+
+    def add(first, together):
+        for slot in range(together):
+            pltpu.make_async_copy(
+                kernels.at[first + slot], kernel_buffer.at[first + slot], sems.at[first + slot]
+            ).wait()
+        windows = jnp.concatenate([window(first + slot) for slot in range(together)], 1)
+        matrix = kernel_buffer[pl.ds(first, together)].reshape(together * columns, -1)
+        product = jnp.dot(windows, matrix, preferred_element_type=F32)
+        for group in range(total.shape[0]):
+            total[group] += product[:, group * LANES : (group + 1) * LANES]
+
+    done = 0
+    together = 1 << (kernel_buffer.shape[0].bit_length() - 1)
+    while together:
+        rounds = (count - done) // together
+
+        def step(index, carry, first=done, together=together):
+            add(first + index * together, together)
+            return carry
+
+        lax.fori_loop(0, rounds, step, 0)
+        done += rounds * together
+        together //= 2
+
+
+def write_chunks(total, outs, share, loads, row):
+    groups, size, _ = total.shape
+    steps = size // loads
+    source, sources = lax.axis_index("src"), len(outs)
     for index, out in enumerate(outs):
         first = partner(source, index, sources) * share % loads
-        for item in range(share):
-            out[item * steps : (item + 1) * steps] = by_load[first + item]
+        columns = [
+            jnp.concatenate(
+                [
+                    total[group, pl.ds(first + item, steps, stride=loads), :]
+                    for item in range(share)
+                ],
+                0,
+            )
+            for group in range(groups)
+        ]
+        chunk = jnp.concatenate(columns, 1)
         if index > 0:
-            out[:size], power = scaled(out[:size])
-            out[row : row + 1] = jnp.broadcast_to(power, (1, rows))
+            chunk, power = scaled(chunk)
         else:
-            out[row : row + 1] = jnp.full((1, rows), HEADROOM, F32)
+            power = jnp.full((1, 1), HEADROOM, F32)
+        out[: share * steps] = chunk
+        out[row : row + 1] = jnp.broadcast_to(power, (1, groups * LANES))
 
 
 def far_first_kernel(
     span, couplings, share, sources, ratio, counts, offsets, past, kernels, *refs
 ):
-    (*outs, history, kernel_buffer, total, strided, by_load, sems, past_sem) = refs
+    (*outs, tail, history, kernel_buffer, total, sems, past_sem) = refs
     fetched = pltpu.make_async_copy(past, history, past_sem)
     fetched.start()
     start_slots(counts, kernels, kernel_buffer, sems)
     steps = history.shape[0] - span
     loads = history.shape[1]
-    rows = total.shape[1]
+    groups = total.shape[0]
+    rows = groups * LANES
     size = share * steps
     fetched.wait()
+    tail[...] = history[steps:]
     sum_slots(counts, offsets, history, kernels, kernel_buffer, sems, total, span)
-    split_loads(total, strided, by_load, loads, steps)
+    for out in outs:
+        out[size:] = jnp.zeros_like(out[size:])
+    write_chunks(total, outs, share, loads, size + share * couplings)
     target, source = lax.axis_index("tgt"), lax.axis_index("src")
     holds = source == target // ratio
     at = pl.multiple_of(target % ratio * rows, LANES)
     recent = history[history.shape[0] - couplings :, :, pl.ds(at, rows)].astype(F32)
-    recent = jnp.where(holds, recent, jnp.zeros_like(recent))
-    for step in range(couplings):
-        for group in range(rows // LANES):
-            strided[group, step * loads : (step + 1) * loads] = recent[
-                step, :, group * LANES : (group + 1) * LANES
-            ]
+    recent = jnp.where(holds, recent, jnp.zeros_like(recent)).reshape(couplings * loads, rows)
+    for group in range(groups):
+        total[group, : couplings * loads] = recent[:, group * LANES : (group + 1) * LANES]
     for index, out in enumerate(outs):
         first = partner(source, index, sources) * share % loads
-        out[size:] = jnp.zeros_like(out[size:])
         for item in range(share):
             for step in range(couplings):
                 row = size + item * couplings + step
-                for group in range(rows // LANES):
-                    out[row : row + 1, group * LANES : (group + 1) * LANES] = strided[
+                for group in range(groups):
+                    out[row : row + 1, group * LANES : (group + 1) * LANES] = total[
                         group, pl.ds(step * loads + first + item, 1), :
                     ]
-    write_chunks(by_load, outs, share, size + share * couplings, sources)
-
-
-def far_next_kernel(
-    span, couplings, share, sources, ratio, counts, offsets, firsts, past, kernels, *refs
-):
+
+
+def far_next_kernel(table, span, share, ratio, counts, offsets, tail, kernels, *refs):
+    sources = len(table)
     arrived, refs = refs[: sources * ratio], refs[sources * ratio :]
-    (*outs, kernel_buffer, total, strided, by_load, stage, history, sems, past_sem) = refs
+    (*outs, kernel_buffer, total, strided, history, sems) = refs
     steps = history.shape[0] - span
     loads, columns = history.shape[1:]
-    rows = total.shape[1]
+    groups = total.shape[0]
     start_slots(counts, kernels, kernel_buffer, sems)
-    tail = pltpu.make_async_copy(
-        past.at[pl.ds(steps, span)], history.at[pl.ds(0, span)], past_sem
-    )
-    tail.start()
-    own = lax.axis_index("tgt") % ratio
+    history[:span] = tail[...]
+    target, source = lax.axis_index("tgt"), lax.axis_index("src")
+    chip, own = target // ratio, lax.rem(target, ratio)
     for index in range(sources):
-        first = firsts[0, 0, index]
+        first = 0
+        for plane in range(sources):
+            for one in range(sources):
+                here = partner(table[plane][one], index, sources)
+                first = jnp.where(
+                    (source == plane) & (chip == here), one * share % loads, first
+                )
         for turn in range(ratio):
             chunk = arrived[turn * sources + index]
             part = lax.rem(own + ratio - turn, ratio)
             for item in range(share):
-                stage[part, first + item] = chunk[
-                    item * steps : (item + 1) * steps
-                ].astype(F32)
+                for group in range(groups):
+                    strided[
+                        part * groups + group,
+                        pl.ds(first + item, steps, stride=loads),
+                        :,
+                    ] = chunk[
+                        item * steps : (item + 1) * steps, group * LANES : (group + 1) * LANES
+                    ].astype(F32)
     for group in range(columns // LANES):
-        part, at = divmod(group * LANES, rows)
-        for load in range(loads):
-            strided[group, pl.ds(load, steps, stride=loads), :] = stage[
-                part, load, :, at : at + LANES
-            ]
         history[span:, :, group * LANES : (group + 1) * LANES] = (
             strided[group].reshape(steps, loads, LANES).astype(BF16)
         )
-    tail.wait()
     sum_slots(counts, offsets, history, kernels, kernel_buffer, sems, total, span)
-    split_loads(total, strided, by_load, loads, steps)
-    write_chunks(by_load, outs, share, share * steps, sources)
+    write_chunks(total, outs, share, loads, share * steps)
 
 
 def prepare_kernel(levels, couplings, inverse, *refs):
@@ -216,7 +233,13 @@
     power_high, power_low = split(matrix[...])
     for level in range(1, levels):
         wide = powers[2 * (level - 1)].shape[1]
-        product = dot3(matrix[...], power_high[:, :wide], power_low[:, :wide])
+        if level == 1 and wide == count * rows:
+            column = matrix[:, :rows]
+            product = dot3(column, first_high[...], first_low[...])
+            product += jnp.concatenate([column[rows:], jnp.zeros((rows, rows), F32)], 0)
+            product = jnp.concatenate([product, matrix[:, : wide - rows]], 1)
+        else:
+            product = dot3(matrix[...], power_high[:, :wide], power_low[:, :wide])
         power_high, power_low = split(product)
         powers[2 * (level - 1)][...] = power_high
         powers[2 * (level - 1) + 1][...] = power_low
@@ -297,22 +320,27 @@
         ]
 
 
-def spread_kernel(steps, share, own, *refs):
-    (*chunks, out, by_load, strided) = refs
-    loads, rows = out.shape[1:]
-    sources = len(chunks) + 1
+def spread_kernel(block, share, own, *refs):
+    (*chunks, out, strided, ready, sem) = refs
+    steps, loads, rows = ready.shape
+    sources = (len(chunks) + 1) if block == 0 else len(chunks)
     size = share * steps
     source = lax.axis_index("src")
-    for index, chunk in enumerate([own, *chunks]):
+    for index, chunk in enumerate([own, *chunks][:sources]):
         first = sender(source, index, sources) * share % loads
         value = chunk[...] if index == 0 else unscaled(chunk, size, size)
         for item in range(share):
-            by_load[first + item] = value[item * steps : (item + 1) * steps]
+            for group in range(rows // LANES):
+                strided[group, pl.ds(first + item, steps, stride=loads), :] = value[
+                    item * steps : (item + 1) * steps, group * LANES : (group + 1) * LANES
+                ]
     for group in range(rows // LANES):
-        lanes = slice(group * LANES, (group + 1) * LANES)
-        for load in range(loads):
-            strided[group, pl.ds(load, steps, stride=loads), :] = by_load[load, :, lanes]
-        out[:, :, lanes] = strided[group].reshape(steps, loads, LANES)
+        ready[:, :, group * LANES : (group + 1) * LANES] = strided[group].reshape(
+            steps, loads, LANES
+        )
+    copy = pltpu.make_async_copy(ready, out.at[pl.ds(block * steps, steps)], sem)
+    copy.start()
+    copy.wait()
 
 
 def landing(plane, sources):
@@ -347,19 +375,6 @@
     pad = -(-(share * count + 1) // SUBLANES) * SUBLANES
 
     table = [landing(plane, sources) for plane in range(sources)]
-    firsts = [
-        [
-            [
-                table[plane].index(sender(chip, k, sources)) * share % loads
-                for k in range(sources)
-            ]
-            for plane in range(sources)
-        ]
-        for chip in range(sources)
-    ]
-    firsts = lax.dynamic_slice(
-        jnp.array(firsts, jnp.int32), (target // ratio, source, 0), (1, 1, sources)
-    )
 
     def params(mebibytes):
         return pltpu.CompilerParams(vmem_limit_bytes=mebibytes * 2**20)
@@ -409,19 +424,22 @@
             name="solve",
         )(*operands)
 
-    def spread(own, chunks):
+    def spread(block, before, own, chunks):
+        last = [] if block == 0 else [before]
         return pl.pallas_call(
-            functools.partial(spread_kernel, steps, share),
-            out_shape=jax.ShapeDtypeStruct((steps, loads, rows), F32),
-            in_specs=[VMEM] * sources,
-            out_specs=VMEM,
+            functools.partial(spread_kernel, block, share),
+            out_shape=jax.ShapeDtypeStruct((all_steps, loads, rows), F32),
+            in_specs=[VMEM] * sources + [HBM] * len(last),
+            out_specs=HBM,
             scratch_shapes=[
-                pltpu.VMEM((loads, steps, rows), F32),
                 pltpu.VMEM((groups, steps * loads, LANES), F32),
+                pltpu.VMEM((steps, loads, rows), F32),
+                pltpu.SemaphoreType.DMA,
             ],
+            input_output_aliases={sources: 0} if last else {},
             compiler_params=params(8),
             name="spread",
-        )(own, *chunks)
+        )(own, *chunks, *last)
 
     own_incident = lax.dynamic_slice_in_dim(incident, source * share % loads, share, 1)
     own_incident = own_incident.reshape(blocks, steps, share, rows)
@@ -429,26 +447,25 @@
 
     far_scratch = [
         pltpu.VMEM(kernels.shape, BF16),
-        pltpu.VMEM((steps * loads, rows), F32),
-        pltpu.VMEM((columns // LANES, steps * loads, LANES), F32),
-        pltpu.VMEM((loads, steps, rows), F32),
+        pltpu.VMEM((groups, steps * loads, LANES), F32),
     ]
-    far_sems = [pltpu.SemaphoreType.DMA((slots,)), pltpu.SemaphoreType.DMA]
+    far_sems = pltpu.SemaphoreType.DMA((slots,))
     history_scratch = pltpu.VMEM((span + steps, loads, columns), BF16)
 
-    partials = pl.pallas_call(
+    *partials, tail = pl.pallas_call(
         functools.partial(far_first_kernel, span, count, share, sources, ratio),
-        out_shape=[jax.ShapeDtypeStruct((size + pad, rows), F32)] * sources,
+        out_shape=[jax.ShapeDtypeStruct((size + pad, rows), F32)] * sources
+        + [jax.ShapeDtypeStruct((span, loads, columns), BF16)],
         in_specs=[SMEM, SMEM, HBM, HBM],
-        out_specs=[VMEM] * sources,
-        scratch_shapes=[history_scratch, *far_scratch, *far_sems],
-        compiler_params=params(12),
+        out_specs=[VMEM] * (sources + 1),
+        scratch_shapes=[history_scratch, *far_scratch, far_sems, pltpu.SemaphoreType.DMA],
+        compiler_params=params(53),
         cost_estimate=cost(2),
         name="far_first",
     )(lag_counts, lag_offset, past_density, kernels)
 
     state = jnp.zeros((pad, rows), F32)
-    produced = []
+    output = None
     for block in range(blocks):
         if block > 0:
             moves = [
@@ -479,24 +496,26 @@
                 ]
                 swapped += [lax.ppermute(chunk, "tgt", pairs) for chunk in arrived]
             partials = pl.pallas_call(
-                functools.partial(far_next_kernel, span, count, share, sources, ratio),
+                functools.partial(far_next_kernel, table, span, share, ratio),
                 out_shape=[jax.ShapeDtypeStruct((size + SUBLANES, rows), F32)] * sources,
-                in_specs=[SMEM, SMEM, SMEM, HBM, HBM] + [VMEM] * (sources * ratio),
+                in_specs=[SMEM, SMEM, VMEM, HBM] + [VMEM] * (sources * ratio),
                 out_specs=[VMEM] * sources,
                 scratch_shapes=far_scratch
-                + [pltpu.VMEM((ratio, loads, steps, rows), F32), history_scratch]
-                + far_sems,
+                + [
+                    pltpu.VMEM((columns // LANES, steps * loads, LANES), F32),
+                    history_scratch,
+                    far_sems,
+                ],
                 compiler_params=params(12),
                 cost_estimate=cost(3),
                 name="far_next",
-            )(lag_counts, lag_offset, firsts, past_density, kernels, *arrived, *swapped)
-            produced.append(spread(solved, chunks))
+            )(lag_counts, lag_offset, tail, kernels, *arrived, *swapped)
+            output = spread(block - 1, output, solved, chunks)
         received = [partials[0]] + trade_each(partials[1:])
         solved, rounded, state, sent = solve(
             received, own_incident[block], state, block == 0
         )
-    produced.append(spread(solved, trade_each([sent] * (sources - 1))))
-    return jnp.concatenate(produced, 0)
+    return spread(blocks - 1, output, solved, trade_each([sent] * (sources - 1)))
 
 
 def solution(mesh):

time: 64.6 us -> 59.6 us (0.923); the launches traced: 64 us -> 60.1 us
  local copies, waits for them, and re-layouts: 5.41 us -> 0.84 us
  Pallas kernels: 15.1 us -> 16.3 us
  waiting for transfers between devices: 13.8 us -> 15 us
  other arithmetic: 1.26 us -> 0.22 us
    unnamed x83 -> x13, local copies, waits for them, and re-layouts: 4.57 us -> 0.69 us
    ppermute x3, waiting for transfers between devices: 2.79 us -> 4.25 us  [local(): arrived.append(lax.ppermute(landed, 'tgt', pairs))]
    ppermute x12, starting transfers between devices: 21.9 us -> 20.5 us  [trade(): return lax.ppermute(value, 'src', pairs)]
    ppermute x1, starting transfers between devices: 1.28 us -> 2.4 us  [local(): landed = lax.ppermute(rounded, ('tgt', 'src'), moves)]
    pallas_call x3, Pallas kernels: 2.9 us -> 3.97 us  [the longest x1 1.99 us: local(): pl.pallas_call(functools.partial(far_next_kernel, table, span, share, rat...]
    concatenate x1 -> x0, other arithmetic: 1.04 us -> none  [local(): return jnp.concatenate(produced, 0)]
    ppermute x1, waiting for transfers between devices: 4.84 us -> 3.89 us  [local(): landed = lax.ppermute(rounded, ('tgt', 'src'), moves)]
    ppermute x4, waiting for transfers between devices: 0.35 us -> 1.24 us  [local(): swapped += [lax.ppermute(chunk, 'tgt', pairs) for chunk in arrived]]
  transfers between devices with their start and end apart: 20 -> 20, of which waited for: 8 -> 9; matrix products, arithmetic and copies ran while one was open for 2% -> 1% of each run, Pallas kernels for 12% -> 14%
where the time goes in v3:
time: 59.6 us; the launch traced here: 60.1 us
  starting transfers between devices  26.5 us (44%)
  Pallas kernels  16.3 us (27%)
  waiting for transfers between devices  15 us (25%)
  between operations  1.19 us (2%)
  local copies, waits for them, and re-layouts  0.84 us (1%)
    ppermute x12, starting transfers between devices, trade(): return lax.ppermute(value, 'src', pairs)  20.5 us
    ppermute x12, waiting for transfers between devices, trade(): return lax.ppermute(value, 'src', pairs)  5.57 us
    pallas_call x2, Pallas kernels, solve(): pl.pallas_call(functools.partial(solve_kernel, steps, share, levels, len(...  5.4 us
    pallas_call x1, Pallas kernels, local(): pl.pallas_call(functools.partial(prepare_kernel, levels), out_shape=[jax....  4.36 us
    ppermute x3, waiting for transfers between devices, local(): arrived.append(lax.ppermute(landed, 'tgt', pairs))  4.25 us
    ppermute x1, waiting for transfers between devices, local(): landed = lax.ppermute(rounded, ('tgt', 'src'), moves)  3.89 us
    ppermute x3, starting transfers between devices, local(): arrived.append(lax.ppermute(landed, 'tgt', pairs))  3.62 us
    pallas_call x1, Pallas kernels, local(): pl.pallas_call(functools.partial(far_first_kernel, span, count, share, so...  2.58 us
  transfers between devices with their start and end apart: 20, of which 9 were waited for; matrix products, arithmetic and copies ran while one was open for 1% of the time, Pallas kernels for 14%

profile of v3, /device:TPU:0, one launch (start us, length us, event | category | flops | bytes accessed | tf_op | source)
XLA Modules:
  0.0 60.1 jit_solution(17287785713208561001)
XLA Ops:
  0.7 0.6 %copy-done.4 = s32[1,1,12]{2,1,0:T(1,128)S(1)} copy-done((s32[1,1,12]{2,1,0:T(1,128)S(1)}, s32[1,1,12]{2,1,0:T(1,128)}, u32[]{:S(2)}) %copy-start.4) | copy-done | bytes 72
  1.4 2.6 %far_first.1 = (f32[136,256]{1,0:T(8,128)S(1)}, f32[136,256]{1,0:T(8,128)S(1)}, f32[136,256]{1,0:T(8,128)S(1)}, f32[136,256]{1,0:T(8,128)S(1)}, bf16[12,8,512]{2,1,0:T(8,128)(2,1)S(1)}) custom-call(s32[1,1]{1,0:T(1,128)S(6)} %copy.12.counts, s32[1,1,12]{2,1,0:T(1,128)S(1)} %copy-done.4, bf16[76,8,512]{2,1,0:T(8,128)(2,1)} %past.1, bf16[8,512,256]{2,1,0:T(8,128)(2,1)} %kernels.3), custom_call_target="tpu_custom_call" | custom-call | flops 2000000000 | tf_op jit(solution)/shard_map/far_first/pallas_call | solution.py:455
  4.0 6.3 %collective-permute-start.2 = (f16[136,256]{1,0:T(8,128)(2,1)S(1)}, f16[136,256]{1,0:T(8,128)(2,1)S(1)}, u32[]{:S(2)}, u32[]{:S(2)}) collective-permute-start(f16[136,256]{1,0:T(8,128)(2,1)S(1)} %convert_element_type.68), channel_id=1, source_target_pairs={{0,3},{1,2},{2,1},{3,0},{4,7},{5,6},{6,5},{7,4},{8,11},{9,10},{10,... | collective-permute-start | bytes 208904 | tf_op jit(solution)/shard_map/ppermute | solution.py:387
  10.3 0.1 collective-permute-start.1
  10.4 0.6 %collective-permute-start = (f16[136,256]{1,0:T(8,128)(2,1)S(1)}, f16[136,256]{1,0:T(8,128)(2,1)S(1)}, u32[]{:S(2)}, u32[]{:S(2)}) collective-permute-start(f16[136,256]{1,0:T(8,128)(2,1)S(1)} %convert_element_type.64), channel_id=1, source_target_pairs={{0,1},{1,0},{2,3},{3,2},{4,5},{5,4},{6,7},{7,6},{8,9},{9,8},{10,11... | collective-permute-start | bytes 208904 | tf_op jit(solution)/shard_map/ppermute | solution.py:387
  11.1 0.1 constant_dynamic-slice_fusion
  11.3 4.4 %prepare.1 = (bf16[256,256]{1,0:T(8,128)(2,1)S(1)}, bf16[256,256]{1,0:T(8,128)(2,1)S(1)}, bf16[2,256,256]{2,1,0:T(8,128)(2,1)S(1)}, bf16[2,256,256]{2,1,0:T(8,12...) custom-call(f32[2,256,256]{2,1,0:T(8,128)S(1)} %copy-done.2, ...), custom_call_target="tpu_custom_call" | custom-call | flops 5000000000 | tf_op jit(solution)/shard_map/prepare/pallas_call | solution.py:395
  15.7 0.3 collective-permute-done
  16.0 0.0 copy-start.1
  16.1 2.4 %solve.2 = (f32[128,256]{1,0:T(8,128)S(1)}, bf16[128,256]{1,0:T(8,128)(2,1)S(1)}, f32[8,256]{1,0:T(8,128)S(1)}, f32[136,256]{1,0:T(8,128)S(1)}) custom-call(f32[136,256]{1,0:T(8,128)S(1)} %get-tuple-element.37.refs_0_, f32[136,256]{1,0:T(8,128)S(1)} %convert_element_type.65.refs_1_, f32[136,256]{1,0:T(8,128)S(1)} %convert_element_type.67.refs_2_, ...), custom_call_target="tpu_custom_call" | custom-call | flops 3000000000 | tf_op jit(solution)/shard_map/solve/pallas_call | solution.py:412
  18.5 2.4 %collective-permute-start.3 = (bf16[128,256]{1,0:T(8,128)(2,1)S(1)}, bf16[128,256]{1,0:T(8,128)(2,1)S(1)}, u32[]{:S(2)}, u32[]{:S(2)}) collective-permute-start(bf16[128,256]{1,0:T(8,128)(2,1)S(1)} %get-tuple-element.57), channel_id=1, source_target_pairs={{0,24},{1,16},{2,8},{3,0},{4,28},{5,20},{6,12},{7,4},{8,1},{9,17},... | collective-permute-start | bytes 196616 | tf_op jit(solution)/shard_map/ppermute | solution.py:480
  20.9 3.9 %collective-permute-done.3.refs_0_ = bf16[128,256]{1,0:T(8,128)(2,1)S(1)} collective-permute-done((bf16[128,256]{1,0:T(8,128)(2,1)S(1)}, bf16[128,256]{1,0:T(8,128)(2,1)S(1)}, u32[]{:S(2)}, u32[]{:S(2)}) %collective-permute-start.3) | collective-permute-done | bytes 65568 | tf_op jit(solution)/shard_map/ppermute | solution.py:480
  24.8 1.8 %collective-permute-start.6 = (bf16[128,256]{1,0:T(8,128)(2,1)S(1)}, bf16[128,256]{1,0:T(8,128)(2,1)S(1)}, u32[]{:S(2)}, u32[]{:S(2)}) collective-permute-start(bf16[128,256]{1,0:T(8,128)(2,1)S(1)} %collective-permute-done.3.refs_0_), channel_id=1, source_target_pairs={{0,24},{4,28},{8,16},{12,20},{16,8},{20,12},{24,0},{28,4},{1,25},{... | collective-permute-start | bytes 196616 | tf_op jit(solution)/shard_map/ppermute | solution.py:489
  26.6 1.9 %collective-permute-start.5 = (bf16[128,256]{1,0:T(8,128)(2,1)S(1)}, bf16[128,256]{1,0:T(8,128)(2,1)S(1)}, u32[]{:S(2)}, u32[]{:S(2)}) collective-permute-start(bf16[128,256]{1,0:T(8,128)(2,1)S(1)} %collective-permute-done.3.refs_0_), channel_id=1, source_target_pairs={{0,16},{4,20},{8,24},{12,28},{16,0},{20,4},{24,8},{28,12},{1,17},{... | collective-permute-start | bytes 196616 | tf_op jit(solution)/shard_map/ppermute | solution.py:489
  28.4 1.5 %collective-permute-done.6.refs_3_ = bf16[128,256]{1,0:T(8,128)(2,1)S(1)} collective-permute-done((bf16[128,256]{1,0:T(8,128)(2,1)S(1)}, bf16[128,256]{1,0:T(8,128)(2,1)S(1)}, u32[]{:S(2)}, u32[]{:S(2)}) %collective-permute-start.6) | collective-permute-done | bytes 65568 | tf_op jit(solution)/shard_map/ppermute | solution.py:489
  30.0 0.8 %collective-permute-done.5.refs_2_ = bf16[128,256]{1,0:T(8,128)(2,1)S(1)} collective-permute-done((bf16[128,256]{1,0:T(8,128)(2,1)S(1)}, bf16[128,256]{1,0:T(8,128)(2,1)S(1)}, u32[]{:S(2)}, u32[]{:S(2)}) %collective-permute-start.5) | collective-permute-done | bytes 65568 | tf_op jit(solution)/shard_map/ppermute | solution.py:489
  30.8 1.9 %collective-permute-done.4.refs_1_ = bf16[128,256]{1,0:T(8,128)(2,1)S(1)} collective-permute-done((bf16[128,256]{1,0:T(8,128)(2,1)S(1)}, bf16[128,256]{1,0:T(8,128)(2,1)S(1)}, u32[]{:S(2)}, u32[]{:S(2)}) %collective-permute-start.4) | collective-permute-done | bytes 65568 | tf_op jit(solution)/shard_map/ppermute | solution.py:489
  32.7 1.2 %collective-permute-done.8.refs_5_ = bf16[128,256]{1,0:T(8,128)(2,1)S(1)} collective-permute-done((bf16[128,256]{1,0:T(8,128)(2,1)S(1)}, bf16[128,256]{1,0:T(8,128)(2,1)S(1)}, u32[]{:S(2)}, u32[]{:S(2)}) %collective-permute-start.8) | collective-permute-done | bytes 65568 | tf_op jit(solution)/shard_map/ppermute | solution.py:497
  34.0 2.0 %far_next.1 = (f32[136,256]{1,0:T(8,128)S(1)}, f32[136,256]{1,0:T(8,128)S(1)}, f32[136,256]{1,0:T(8,128)S(1)}, f32[136,256]{1,0:T(8,128)S(1)}) custom-call(s32[1,1]{1,0:T(1,128)S(6)} %copy.12.counts, s32[1,1,12]{2,1,0:T(1,128)S(1)} %copy-done.5, bf16[12,8,512]{2,1,0:T(8,128)(2,1)S(1)} %get-tuple-element.36.tail, bf16[8,512,256]{2,1,0:T(8,128)(2,1)S(1)} %copy-done.1, ...), custom_call_target="tpu_custom_call" | custom-call | flops 3000000000 | tf_op jit(solution)/shard_map/far_next/pallas_call | solution.py:498
  36.0 3.6 %collective-permute-start.13 = (f16[136,256]{1,0:T(8,128)(2,1)S(1)}, f16[136,256]{1,0:T(8,128)(2,1)S(1)}, u32[]{:S(2)}, u32[]{:S(2)}) collective-permute-start(f16[136,256]{1,0:T(8,128)(2,1)S(1)} %convert_element_type.74), channel_id=1, source_target_pairs={{0,3},{1,2},{2,1},{3,0},{4,7},{5,6},{6,5},{7,4},{8,11},{9,10},{10,... | collective-permute-start | bytes 208904 | tf_op jit(solution)/shard_map/ppermute | solution.py:387
  39.6 0.1 collective-permute-start.12
  39.7 0.9 %collective-permute-start.11 = (f16[136,256]{1,0:T(8,128)(2,1)S(1)}, f16[136,256]{1,0:T(8,128)(2,1)S(1)}, u32[]{:S(2)}, u32[]{:S(2)}) collective-permute-start(f16[136,256]{1,0:T(8,128)(2,1)S(1)} %convert_element_type.70), channel_id=1, source_target_pairs={{0,1},{1,0},{2,3},{3,2},{4,5},{5,4},{6,7},{7,6},{8,9},{9,8},{10,11... | collective-permute-start | bytes 208904 | tf_op jit(solution)/shard_map/ppermute | solution.py:387
  40.6 3.6 %collective-permute-start.19 = (f16[136,256]{1,0:T(8,128)(2,1)S(1)}, f16[136,256]{1,0:T(8,128)(2,1)S(1)}, u32[]{:S(2)}, u32[]{:S(2)}) collective-permute-start(f16[136,256]{1,0:T(8,128)(2,1)S(1)} %convert_element_type.80), channel_id=1, source_target_pairs={{0,3},{1,2},{2,1},{3,0},{4,7},{5,6},{6,5},{7,4},{8,11},{9,10},{10,... | collective-permute-start | bytes 208904 | tf_op jit(solution)/shard_map/ppermute | solution.py:387
  44.2 0.9 %collective-permute-start.17 = (f16[136,256]{1,0:T(8,128)(2,1)S(1)}, f16[136,256]{1,0:T(8,128)(2,1)S(1)}, u32[]{:S(2)}, u32[]{:S(2)}) collective-permute-start(f16[136,256]{1,0:T(8,128)(2,1)S(1)} %convert_element_type.80), channel_id=1, source_target_pairs={{0,1},{1,0},{2,3},{3,2},{4,5},{5,4},{6,7},{7,6},{8,9},{9,8},{10,11... | collective-permute-start | bytes 208904 | tf_op jit(solution)/shard_map/ppermute | solution.py:387
  45.1 2.6 %collective-permute-done.12 = f16[136,256]{1,0:T(8,128)(2,1)S(1)} collective-permute-done((f16[136,256]{1,0:T(8,128)(2,1)S(1)}, f16[136,256]{1,0:T(8,128)(2,1)S(1)}, u32[]{:S(2)}, u32[]{:S(2)}) %collective-permute-start.12) | collective-permute-done | bytes 69664 | tf_op jit(solution)/shard_map/ppermute | solution.py:387
  47.8 3.0 %solve.3 = (f32[128,256]{1,0:T(8,128)S(1)}, bf16[128,256]{1,0:T(8,128)(2,1)}, f32[8,256]{1,0:T(8,128)}, f32[136,256]{1,0:T(8,128)S(1)}) custom-call(f32[136,256]{1,0:T(8,128)S(1)} %get-tuple-element.58.refs_0_, f32[136,256]{1,0:T(8,128)S(1)} %convert_element_type.71.refs_1_, f32[136,256]{1,0:T(8,128)S(1)} %convert_element_type.73.refs_2_, ...), custom_call_target="tpu_custom_call" | custom-call | flops 3000000000 | tf_op jit(solution)/shard_map/solve/pallas_call | solution.py:412
  50.7 1.9 %collective-permute-start.16 = (f16[136,256]{1,0:T(8,128)(2,1)S(1)}, f16[136,256]{1,0:T(8,128)(2,1)S(1)}, u32[]{:S(2)}, u32[]{:S(2)}) collective-permute-start(f16[136,256]{1,0:T(8,128)(2,1)S(1)} %convert_element_type.76), channel_id=1, source_target_pairs={{0,3},{1,2},{2,1},{3,0},{4,7},{5,6},{6,5},{7,4},{8,11},{9,10},{10,... | collective-permute-start | bytes 208904 | tf_op jit(solution)/shard_map/ppermute | solution.py:387
  52.6 2.6 %collective-permute-start.14 = (f16[136,256]{1,0:T(8,128)(2,1)S(1)}, f16[136,256]{1,0:T(8,128)(2,1)S(1)}, u32[]{:S(2)}, u32[]{:S(2)}) collective-permute-start(f16[136,256]{1,0:T(8,128)(2,1)S(1)} %convert_element_type.76), channel_id=1, source_target_pairs={{0,1},{1,0},{2,3},{3,2},{4,5},{5,4},{6,7},{7,6},{8,9},{9,8},{10,11... | collective-permute-start | bytes 208904 | tf_op jit(solution)/shard_map/ppermute | solution.py:387
  55.3 1.0 %spread.2.refs_3_ = f32[128,8,256]{2,1,0:T(8,128)} custom-call(f32[128,256]{1,0:T(8,128)S(1)} %get-tuple-element.65.own, f32[136,256]{1,0:T(8,128)S(1)} %convert_element_type.81.refs_0_, f32[136,256]{1,0:T(8,128)S(1)} %convert_element_type.82.refs_1_, f32[136,256]{1,0:T(8,128)S(1)} %convert_element_type.83.refs_2_), custom_call_target="tpu_custom_call" | custom-call | tf_op jit(solution)/shard_map/spread/pallas_call | solution.py:429
  56.3 1.3 %collective-permute-done.16 = f16[136,256]{1,0:T(8,128)(2,1)S(1)} collective-permute-done((f16[136,256]{1,0:T(8,128)(2,1)S(1)}, f16[136,256]{1,0:T(8,128)(2,1)S(1)}, u32[]{:S(2)}, u32[]{:S(2)}) %collective-permute-start.16) | collective-permute-done | bytes 69664 | tf_op jit(solution)/shard_map/ppermute | solution.py:387
  57.6 1.3 %collective-permute-done.15 = f16[136,256]{1,0:T(8,128)(2,1)S(1)} collective-permute-done((f16[136,256]{1,0:T(8,128)(2,1)S(1)}, f16[136,256]{1,0:T(8,128)(2,1)S(1)}, u32[]{:S(2)}, u32[]{:S(2)}) %collective-permute-start.15) | collective-permute-done | bytes 69664 | tf_op jit(solution)/shard_map/ppermute | solution.py:387
  58.9 1.0 %spread.3 = f32[128,8,256]{2,1,0:T(8,128)} custom-call(f32[128,256]{1,0:T(8,128)S(1)} %get-tuple-element.63.own, f32[136,256]{1,0:T(8,128)S(1)} %convert_element_type.77.refs_0_, f32[136,256]{1,0:T(8,128)S(1)} %convert_element_type.78.refs_1_, f32[136,256]{1,0:T(8,128)S(1)} %convert_element_type.79.refs_2_, ...), custom_call_target="tpu_custom_call", output_to_operand_aliasing={{}: (4, {})} | custom-call | tf_op jit(solution)/shard_map/spread/pallas_call | solution.py:429
  (51 shorter events, 0.3 us)
Async XLA Ops:
  0.0 11.1 %copy-start = (bf16[128,8,256]{2,1,0:T(8,128)(2,1)S(1)}, bf16[128,8,256]{2,1,0:T(8,128)(2,1)}, u32[]{:S(2)}) copy-start(bf16[128,8,256]{2,1,0:T(8,128)(2,1)} %param.7) | copy-start | bytes 1572868
  0.7 0.7 %copy-start.4 = (s32[1,1,12]{2,1,0:T(1,128)S(1)}, s32[1,1,12]{2,1,0:T(1,128)}, u32[]{:S(2)}) copy-start(s32[1,1,12]{2,1,0:T(1,128)} %offsets.3) | copy-start | bytes 148
  1.4 9.9 %copy-start.2 = (f32[2,256,256]{2,1,0:T(8,128)S(1)}, f32[2,256,256]{2,1,0:T(8,128)}, u32[]{:S(2)}) copy-start(f32[2,256,256]{2,1,0:T(8,128)} %couplings.1) | copy-start | bytes 1572868
  1.4 9.9 %copy-start.3 = (f32[256,256]{1,0:T(8,128)S(1)}, f32[256,256]{1,0:T(8,128)}, u32[]{:S(2)}) copy-start(f32[256,256]{1,0:T(8,128)} %inverse.1) | copy-start | bytes 786436
  4.0 11.7 %collective-permute-start.2 = (f16[136,256]{1,0:T(8,128)(2,1)S(1)}, f16[136,256]{1,0:T(8,128)(2,1)S(1)}, u32[]{:S(2)}, u32[]{:S(2)}) collective-permute-start(f16[136,256]{1,0:T(8,128)(2,1)S(1)} %convert_element_type.68), channel_id=1, source_target_pairs={{0,3},{1,2},{2,1},{3,0},{4,7},{5,6},{6,5},{7,4},{8,11},{9,10},{10,... | collective-permute-start | bytes 208904 | tf_op jit(solution)/shard_map/ppermute | solution.py:387
  10.3 5.3 %collective-permute-start.1 = (f16[136,256]{1,0:T(8,128)(2,1)S(1)}, f16[136,256]{1,0:T(8,128)(2,1)S(1)}, u32[]{:S(2)}, u32[]{:S(2)}) collective-permute-start(f16[136,256]{1,0:T(8,128)(2,1)S(1)} %convert_element_type.66), channel_id=1, source_target_pairs={{0,2},{1,3},{2,0},{3,1},{4,6},{5,7},{6,4},{7,5},{8,10},{9,11},{10,... | collective-permute-start | bytes 208904 | tf_op jit(solution)/shard_map/ppermute | solution.py:387
  10.4 5.6 %collective-permute-start = (f16[136,256]{1,0:T(8,128)(2,1)S(1)}, f16[136,256]{1,0:T(8,128)(2,1)S(1)}, u32[]{:S(2)}, u32[]{:S(2)}) collective-permute-start(f16[136,256]{1,0:T(8,128)(2,1)S(1)} %convert_element_type.64), channel_id=1, source_target_pairs={{0,1},{1,0},{2,3},{3,2},{4,5},{5,4},{6,7},{7,6},{8,9},{9,8},{10,11... | collective-permute-start | bytes 208904 | tf_op jit(solution)/shard_map/ppermute | solution.py:387
  16.0 17.9 %copy-start.1 = (bf16[8,512,256]{2,1,0:T(8,128)(2,1)S(1)}, bf16[8,512,256]{2,1,0:T(8,128)(2,1)}, u32[]{:S(2)}) copy-start(bf16[8,512,256]{2,1,0:T(8,128)(2,1)} %kernels.3) | copy-start | bytes 6291460
  16.1 17.9 %copy-start.5 = (s32[1,1,12]{2,1,0:T(1,128)S(1)}, s32[1,1,12]{2,1,0:T(1,128)}, u32[]{:S(2)}) copy-start(s32[1,1,12]{2,1,0:T(1,128)} %offsets.3) | copy-start | bytes 148
  18.5 6.3 %collective-permute-start.3 = (bf16[128,256]{1,0:T(8,128)(2,1)S(1)}, bf16[128,256]{1,0:T(8,128)(2,1)S(1)}, u32[]{:S(2)}, u32[]{:S(2)}) collective-permute-start(bf16[128,256]{1,0:T(8,128)(2,1)S(1)} %get-tuple-element.57), channel_id=1, source_target_pairs={{0,24},{1,16},{2,8},{3,0},{4,28},{5,20},{6,12},{7,4},{8,1},{9,17},... | collective-permute-start | bytes 196616 | tf_op jit(solution)/shard_map/ppermute | solution.py:480
  24.8 5.2 %collective-permute-start.6 = (bf16[128,256]{1,0:T(8,128)(2,1)S(1)}, bf16[128,256]{1,0:T(8,128)(2,1)S(1)}, u32[]{:S(2)}, u32[]{:S(2)}) collective-permute-start(bf16[128,256]{1,0:T(8,128)(2,1)S(1)} %collective-permute-done.3.refs_0_), channel_id=1, source_target_pairs={{0,24},{4,28},{8,16},{12,20},{16,8},{20,12},{24,0},{28,4},{1,25},{... | collective-permute-start | bytes 196616 | tf_op jit(solution)/shard_map/ppermute | solution.py:489
  26.6 4.3 %collective-permute-start.5 = (bf16[128,256]{1,0:T(8,128)(2,1)S(1)}, bf16[128,256]{1,0:T(8,128)(2,1)S(1)}, u32[]{:S(2)}, u32[]{:S(2)}) collective-permute-start(bf16[128,256]{1,0:T(8,128)(2,1)S(1)} %collective-permute-done.3.refs_0_), channel_id=1, source_target_pairs={{0,16},{4,20},{8,24},{12,28},{16,0},{20,4},{24,8},{28,12},{1,17},{... | collective-permute-start | bytes 196616 | tf_op jit(solution)/shard_map/ppermute | solution.py:489
  28.4 4.3 %collective-permute-start.4 = (bf16[128,256]{1,0:T(8,128)(2,1)S(1)}, bf16[128,256]{1,0:T(8,128)(2,1)S(1)}, u32[]{:S(2)}, u32[]{:S(2)}) collective-permute-start(bf16[128,256]{1,0:T(8,128)(2,1)S(1)} %collective-permute-done.3.refs_0_), channel_id=1, source_target_pairs={{0,8},{4,12},{8,0},{12,4},{16,24},{20,28},{24,16},{28,20},{1,9},{5... | collective-permute-start | bytes 196616 | tf_op jit(solution)/shard_map/ppermute | solution.py:489
  28.4 4.3 %collective-permute-start.7 = (bf16[128,256]{1,0:T(8,128)(2,1)S(1)}, bf16[128,256]{1,0:T(8,128)(2,1)S(1)}, u32[]{:S(2)}, u32[]{:S(2)}) collective-permute-start(bf16[128,256]{1,0:T(8,128)(2,1)S(1)} %collective-permute-done.3.refs_0_), channel_id=1, source_target_pairs={{0,4},{4,0},{8,12},{12,8},{16,20},{20,16},{24,28},{28,24},{1,5},{5... | collective-permute-start | bytes 196616 | tf_op jit(solution)/shard_map/ppermute | solution.py:497
  30.0 2.7 %collective-permute-start.10 = (bf16[128,256]{1,0:T(8,128)(2,1)S(1)}, bf16[128,256]{1,0:T(8,128)(2,1)S(1)}, u32[]{:S(2)}, u32[]{:S(2)}) collective-permute-start(bf16[128,256]{1,0:T(8,128)(2,1)S(1)} %collective-permute-done.6.refs_3_), channel_id=1, source_target_pairs={{0,4},{4,0},{8,12},{12,8},{16,20},{20,16},{24,28},{28,24},{1,5},{5... | collective-permute-start | bytes 196616 | tf_op jit(solution)/shard_map/ppermute | solution.py:497
  30.8 1.9 %collective-permute-start.9 = (bf16[128,256]{1,0:T(8,128)(2,1)S(1)}, bf16[128,256]{1,0:T(8,128)(2,1)S(1)}, u32[]{:S(2)}, u32[]{:S(2)}) collective-permute-start(bf16[128,256]{1,0:T(8,128)(2,1)S(1)} %collective-permute-done.5.refs_2_), channel_id=1, source_target_pairs={{0,4},{4,0},{8,12},{12,8},{16,20},{20,16},{24,28},{28,24},{1,5},{5... | collective-permute-start | bytes 196616 | tf_op jit(solution)/shard_map/ppermute | solution.py:497
  32.7 1.3 %collective-permute-start.8 = (bf16[128,256]{1,0:T(8,128)(2,1)S(1)}, bf16[128,256]{1,0:T(8,128)(2,1)S(1)}, u32[]{:S(2)}, u32[]{:S(2)}) collective-permute-start(bf16[128,256]{1,0:T(8,128)(2,1)S(1)} %collective-permute-done.4.refs_1_), channel_id=1, source_target_pairs={{0,4},{4,0},{8,12},{12,8},{16,20},{20,16},{24,28},{28,24},{1,5},{5... | collective-permute-start | bytes 196616 | tf_op jit(solution)/shard_map/ppermute | solution.py:497
  36.0 8.2 %collective-permute-start.13 = (f16[136,256]{1,0:T(8,128)(2,1)S(1)}, f16[136,256]{1,0:T(8,128)(2,1)S(1)}, u32[]{:S(2)}, u32[]{:S(2)}) collective-permute-start(f16[136,256]{1,0:T(8,128)(2,1)S(1)} %convert_element_type.74), channel_id=1, source_target_pairs={{0,3},{1,2},{2,1},{3,0},{4,7},{5,6},{6,5},{7,4},{8,11},{9,10},{10,... | collective-permute-start | bytes 208904 | tf_op jit(solution)/shard_map/ppermute | solution.py:387
  39.6 8.1 %collective-permute-start.12 = (f16[136,256]{1,0:T(8,128)(2,1)S(1)}, f16[136,256]{1,0:T(8,128)(2,1)S(1)}, u32[]{:S(2)}, u32[]{:S(2)}) collective-permute-start(f16[136,256]{1,0:T(8,128)(2,1)S(1)} %convert_element_type.72), channel_id=1, source_target_pairs={{0,2},{1,3},{2,0},{3,1},{4,6},{5,7},{6,4},{7,5},{8,10},{9,11},{10,... | collective-permute-start | bytes 208904 | tf_op jit(solution)/shard_map/ppermute | solution.py:387
  39.7 8.1 %collective-permute-start.11 = (f16[136,256]{1,0:T(8,128)(2,1)S(1)}, f16[136,256]{1,0:T(8,128)(2,1)S(1)}, u32[]{:S(2)}, u32[]{:S(2)}) collective-permute-start(f16[136,256]{1,0:T(8,128)(2,1)S(1)} %convert_element_type.70), channel_id=1, source_target_pairs={{0,1},{1,0},{2,3},{3,2},{4,5},{5,4},{6,7},{7,6},{8,9},{9,8},{10,11... | collective-permute-start | bytes 208904 | tf_op jit(solution)/shard_map/ppermute | solution.py:387
  40.6 12.0 %collective-permute-start.19 = (f16[136,256]{1,0:T(8,128)(2,1)S(1)}, f16[136,256]{1,0:T(8,128)(2,1)S(1)}, u32[]{:S(2)}, u32[]{:S(2)}) collective-permute-start(f16[136,256]{1,0:T(8,128)(2,1)S(1)} %convert_element_type.80), channel_id=1, source_target_pairs={{0,3},{1,2},{2,1},{3,0},{4,7},{5,6},{6,5},{7,4},{8,11},{9,10},{10,... | collective-permute-start | bytes 208904 | tf_op jit(solution)/shard_map/ppermute | solution.py:387
  44.2 11.0 %collective-permute-start.18 = (f16[136,256]{1,0:T(8,128)(2,1)S(1)}, f16[136,256]{1,0:T(8,128)(2,1)S(1)}, u32[]{:S(2)}, u32[]{:S(2)}) collective-permute-start(f16[136,256]{1,0:T(8,128)(2,1)S(1)} %convert_element_type.80), channel_id=1, source_target_pairs={{0,2},{1,3},{2,0},{3,1},{4,6},{5,7},{6,4},{7,5},{8,10},{9,11},{10,... | collective-permute-start | bytes 208904 | tf_op jit(solution)/shard_map/ppermute | solution.py:387
  44.2 11.0 %collective-permute-start.17 = (f16[136,256]{1,0:T(8,128)(2,1)S(1)}, f16[136,256]{1,0:T(8,128)(2,1)S(1)}, u32[]{:S(2)}, u32[]{:S(2)}) collective-permute-start(f16[136,256]{1,0:T(8,128)(2,1)S(1)} %convert_element_type.80), channel_id=1, source_target_pairs={{0,1},{1,0},{2,3},{3,2},{4,5},{5,4},{6,7},{7,6},{8,9},{9,8},{10,11... | collective-permute-start | bytes 208904 | tf_op jit(solution)/shard_map/ppermute | solution.py:387
  50.7 6.9 %collective-permute-start.16 = (f16[136,256]{1,0:T(8,128)(2,1)S(1)}, f16[136,256]{1,0:T(8,128)(2,1)S(1)}, u32[]{:S(2)}, u32[]{:S(2)}) collective-permute-start(f16[136,256]{1,0:T(8,128)(2,1)S(1)} %convert_element_type.76), channel_id=1, source_target_pairs={{0,3},{1,2},{2,1},{3,0},{4,7},{5,6},{6,5},{7,4},{8,11},{9,10},{10,... | collective-permute-start | bytes 208904 | tf_op jit(solution)/shard_map/ppermute | solution.py:387
  52.6 6.2 %collective-permute-start.15 = (f16[136,256]{1,0:T(8,128)(2,1)S(1)}, f16[136,256]{1,0:T(8,128)(2,1)S(1)}, u32[]{:S(2)}, u32[]{:S(2)}) collective-permute-start(f16[136,256]{1,0:T(8,128)(2,1)S(1)} %convert_element_type.76), channel_id=1, source_target_pairs={{0,2},{1,3},{2,0},{3,1},{4,6},{5,7},{6,4},{7,5},{8,10},{9,11},{10,... | collective-permute-start | bytes 208904 | tf_op jit(solution)/shard_map/ppermute | solution.py:387
  52.6 6.3 %collective-permute-start.14 = (f16[136,256]{1,0:T(8,128)(2,1)S(1)}, f16[136,256]{1,0:T(8,128)(2,1)S(1)}, u32[]{:S(2)}, u32[]{:S(2)}) collective-permute-start(f16[136,256]{1,0:T(8,128)(2,1)S(1)} %convert_element_type.76), channel_id=1, source_target_pairs={{0,1},{1,0},{2,3},{3,2},{4,5},{5,4},{6,7},{7,6},{8,9},{9,8},{10,11... | collective-permute-start | bytes 208904 | tf_op jit(solution)/shard_map/ppermute | solution.py:387

commit v4 on v3

--- a/solution.py
+++ b/solution.py
@@ -67,7 +67,7 @@
             ).start()
 
 
-def sum_slots(counts, offsets, history, kernels, kernel_buffer, sems, total, span):
+def sum_slots(counts, offsets, history, kernels, total, span, arrived=None):
     steps = history.shape[0] - span
     loads, columns = history.shape[1:]
     count = counts[0, 0]
@@ -78,18 +78,17 @@
         return taken.reshape(steps * loads, columns)
 
     def add(first, together):
-        for slot in range(together):
-            pltpu.make_async_copy(
-                kernels.at[first + slot], kernel_buffer.at[first + slot], sems.at[first + slot]
-            ).wait()
+        if arrived is not None:
+            for slot in range(together):
+                arrived(first + slot)
         windows = jnp.concatenate([window(first + slot) for slot in range(together)], 1)
-        matrix = kernel_buffer[pl.ds(first, together)].reshape(together * columns, -1)
+        matrix = kernels[pl.ds(first, together)].reshape(together * columns, -1)
         product = jnp.dot(windows, matrix, preferred_element_type=F32)
         for group in range(total.shape[0]):
             total[group] += product[:, group * LANES : (group + 1) * LANES]
 
     done = 0
-    together = 1 << (kernel_buffer.shape[0].bit_length() - 1)
+    together = 1 << (kernels.shape[0].bit_length() - 1)
     while together:
         rounds = (count - done) // together
 
@@ -130,8 +129,10 @@
 def far_first_kernel(
     span, couplings, share, sources, ratio, counts, offsets, past, kernels, *refs
 ):
-    (*outs, tail, history, kernel_buffer, total, sems, past_sem) = refs
+    (*outs, tail, history, kernel_buffer, total, scalars, sems, past_sem, scalar_sem) = refs
     fetched = pltpu.make_async_copy(past, history, past_sem)
+    listed = pltpu.make_async_copy(offsets, scalars, scalar_sem)
+    listed.start()
     fetched.start()
     start_slots(counts, kernels, kernel_buffer, sems)
     steps = history.shape[0] - span
@@ -139,9 +140,16 @@
     groups = total.shape[0]
     rows = groups * LANES
     size = share * steps
+    listed.wait()
     fetched.wait()
     tail[...] = history[steps:]
-    sum_slots(counts, offsets, history, kernels, kernel_buffer, sems, total, span)
+
+    def arrived(slot):
+        pltpu.make_async_copy(
+            kernels.at[slot], kernel_buffer.at[slot], sems.at[slot]
+        ).wait()
+
+    sum_slots(counts, scalars, history, kernel_buffer, total, span, arrived)
     for out in outs:
         out[size:] = jnp.zeros_like(out[size:])
     write_chunks(total, outs, share, loads, size + share * couplings)
@@ -166,11 +174,10 @@
 def far_next_kernel(table, span, share, ratio, counts, offsets, tail, kernels, *refs):
     sources = len(table)
     arrived, refs = refs[: sources * ratio], refs[sources * ratio :]
-    (*outs, kernel_buffer, total, strided, history, sems) = refs
+    (*outs, total, strided, history) = refs
     steps = history.shape[0] - span
     loads, columns = history.shape[1:]
     groups = total.shape[0]
-    start_slots(counts, kernels, kernel_buffer, sems)
     history[:span] = tail[...]
     target, source = lax.axis_index("tgt"), lax.axis_index("src")
     chip, own = target // ratio, lax.rem(target, ratio)
@@ -198,7 +205,7 @@
         history[span:, :, group * LANES : (group + 1) * LANES] = (
             strided[group].reshape(steps, loads, LANES).astype(BF16)
         )
-    sum_slots(counts, offsets, history, kernels, kernel_buffer, sems, total, span)
+    sum_slots(counts, offsets, history, kernels, total, span)
     write_chunks(total, outs, share, loads, share * steps)
 
 
@@ -260,7 +267,7 @@
         first_low,
         *powers,
     ) = refs[: 8 + 2 * (levels - 1)]
-    solved, rounded, state, sent = refs[8 + 2 * (levels - 1) :]
+    solved, sent, *following = refs[8 + 2 * (levels - 1) :]
     count, rows, _ = coupling_high.shape
     size = share * steps
     power_row = size + share * count if packed else size
@@ -310,14 +317,16 @@
         total = total[:, :wide] + delayed(dot3(total, high[...], low[...]), 2**level)
     result = total[:, :rows]
     solved[...] = result
-    rounded[...] = result.astype(BF16)
     sent[:size], power = scaled(result)
     sent[size:] = jnp.broadcast_to(power, (sent.shape[0] - size, rows))
-    state[...] = jnp.zeros_like(state)
-    for item in range(share):
-        state[item * count : (item + 1) * count] = result[
-            (item + 1) * steps - count : (item + 1) * steps
-        ]
+    if following:
+        rounded, state = following
+        rounded[...] = result.astype(BF16)
+        state[...] = jnp.zeros_like(state)
+        for item in range(share):
+            state[item * count : (item + 1) * count] = result[
+                (item + 1) * steps - count : (item + 1) * steps
+            ]
 
 
 def spread_kernel(block, share, own, *refs):
@@ -407,18 +416,20 @@
         name="prepare",
     )(couplings, inverse)
 
-    def solve(partials, driving, earlier, packed):
+    def solve(partials, driving, earlier, first, last):
         operands = [*partials, driving, earlier, *prepared]
+        shapes = [
+            jax.ShapeDtypeStruct((size, rows), F32),
+            jax.ShapeDtypeStruct((size + SUBLANES, rows), F32),
+        ]
+        if not last:
+            shapes.append(jax.ShapeDtypeStruct((size, rows), BF16))
+            shapes.append(jax.ShapeDtypeStruct((pad, rows), F32))
         return pl.pallas_call(
-            functools.partial(solve_kernel, steps, share, levels, len(partials), packed),
-            out_shape=[
-                jax.ShapeDtypeStruct((size, rows), F32),
-                jax.ShapeDtypeStruct((size, rows), BF16),
-                jax.ShapeDtypeStruct((pad, rows), F32),
-                jax.ShapeDtypeStruct((size + SUBLANES, rows), F32),
-            ],
+            functools.partial(solve_kernel, steps, share, levels, len(partials), first),
+            out_shape=shapes,
             in_specs=[VMEM] * len(operands),
-            out_specs=[VMEM] * 4,
+            out_specs=[VMEM] * len(shapes),
             compiler_params=params(12),
             cost_estimate=cost(3),
             name="solve",
@@ -445,20 +456,24 @@
     own_incident = own_incident.reshape(blocks, steps, share, rows)
     own_incident = own_incident.transpose(0, 2, 1, 3).reshape(blocks, size, rows)
 
-    far_scratch = [
-        pltpu.VMEM(kernels.shape, BF16),
-        pltpu.VMEM((groups, steps * loads, LANES), F32),
-    ]
-    far_sems = pltpu.SemaphoreType.DMA((slots,))
+    total_scratch = pltpu.VMEM((groups, steps * loads, LANES), F32)
     history_scratch = pltpu.VMEM((span + steps, loads, columns), BF16)
 
     *partials, tail = pl.pallas_call(
         functools.partial(far_first_kernel, span, count, share, sources, ratio),
         out_shape=[jax.ShapeDtypeStruct((size + pad, rows), F32)] * sources
         + [jax.ShapeDtypeStruct((span, loads, columns), BF16)],
-        in_specs=[SMEM, SMEM, HBM, HBM],
+        in_specs=[SMEM, HBM, HBM, HBM],
         out_specs=[VMEM] * (sources + 1),
-        scratch_shapes=[history_scratch, *far_scratch, far_sems, pltpu.SemaphoreType.DMA],
+        scratch_shapes=[
+            history_scratch,
+            pltpu.VMEM(kernels.shape, BF16),
+            total_scratch,
+            pltpu.SMEM(lag_offset.shape, jnp.int32),
+            pltpu.SemaphoreType.DMA((slots,)),
+            pltpu.SemaphoreType.DMA,
+            pltpu.SemaphoreType.DMA,
+        ],
         compiler_params=params(53),
         cost_estimate=cost(2),
         name="far_first",
@@ -498,13 +513,12 @@
             partials = pl.pallas_call(
                 functools.partial(far_next_kernel, table, span, share, ratio),
                 out_shape=[jax.ShapeDtypeStruct((size + SUBLANES, rows), F32)] * sources,
-                in_specs=[SMEM, SMEM, VMEM, HBM] + [VMEM] * (sources * ratio),
+                in_specs=[SMEM, SMEM, VMEM, VMEM] + [VMEM] * (sources * ratio),
                 out_specs=[VMEM] * sources,
-                scratch_shapes=far_scratch
-                + [
+                scratch_shapes=[
+                    total_scratch,
                     pltpu.VMEM((columns // LANES, steps * loads, LANES), F32),
                     history_scratch,
-                    far_sems,
                 ],
                 compiler_params=params(12),
                 cost_estimate=cost(3),
@@ -512,9 +526,11 @@
             )(lag_counts, lag_offset, tail, kernels, *arrived, *swapped)
             output = spread(block - 1, output, solved, chunks)
         received = [partials[0]] + trade_each(partials[1:])
-        solved, rounded, state, sent = solve(
-            received, own_incident[block], state, block == 0
+        solved, sent, *following = solve(
+            received, own_incident[block], state, block == 0, block + 1 == blocks
         )
+        if following:
+            rounded, state = following
     return spread(blocks - 1, output, solved, trade_each([sent] * (sources - 1)))
 
 

time: 59.6 us -> 57.7 us (0.968); the launches traced: 60.1 us -> 57.3 us
  waiting for transfers between devices: 15 us -> 12.8 us
  Pallas kernels: 16.3 us -> 15.2 us
  starting transfers between devices: 26.5 us -> 27.1 us
    ppermute x1, waiting for transfers between devices: 3.89 us -> 3.07 us  [local(): landed = lax.ppermute(rounded, ('tgt', 'src'), moves)]
    ppermute x1, starting transfers between devices: 2.4 us -> 3.2 us  [local(): landed = lax.ppermute(rounded, ('tgt', 'src'), moves)]
    ppermute x12, starting transfers between devices: 20.5 us -> 19.7 us  [trade(): return lax.ppermute(value, 'src', pairs)]
    ppermute x12, waiting for transfers between devices: 5.57 us -> 4.82 us  [trade(): return lax.ppermute(value, 'src', pairs)]
    ppermute x3, waiting for transfers between devices: 4.25 us -> 3.65 us  [local(): arrived.append(lax.ppermute(landed, 'tgt', pairs))]
where the time goes in v4:
time: 57.7 us; the launch traced here: 57.3 us
  starting transfers between devices  27.1 us (47%)
  Pallas kernels  15.2 us (26%)
  waiting for transfers between devices  12.8 us (22%)
  between operations  1.19 us (2%)
  local copies, waits for them, and re-layouts  0.84 us (1%)
    ppermute x12, starting transfers between devices, trade(): return lax.ppermute(value, 'src', pairs)  19.7 us
    pallas_call x2, Pallas kernels, solve(): pl.pallas_call(functools.partial(solve_kernel, steps, share, levels, len(...  4.87 us
    ppermute x12, waiting for transfers between devices, trade(): return lax.ppermute(value, 'src', pairs)  4.82 us
    pallas_call x1, Pallas kernels, local(): pl.pallas_call(functools.partial(prepare_kernel, levels), out_shape=[jax....  4.36 us
    ppermute x3, starting transfers between devices, local(): arrived.append(lax.ppermute(landed, 'tgt', pairs))  4.18 us
    ppermute x3, waiting for transfers between devices, local(): arrived.append(lax.ppermute(landed, 'tgt', pairs))  3.65 us
    ppermute x1, starting transfers between devices, local(): landed = lax.ppermute(rounded, ('tgt', 'src'), moves)  3.2 us
    ppermute x1, waiting for transfers between devices, local(): landed = lax.ppermute(rounded, ('tgt', 'src'), moves)  3.07 us
  transfers between devices with their start and end apart: 20, of which 9 were waited for; matrix products, arithmetic and copies ran while one was open for 1% of the time, Pallas kernels for 14%

profile of v4, /device:TPU:0, one launch (start us, length us, event | category | flops | bytes accessed | tf_op | source)
XLA Modules:
  0.0 57.3 jit_solution(12041398872825565575)
XLA Ops:
  0.7 0.6 %copy-done.4 = s32[1,1,12]{2,1,0:T(1,128)S(1)} copy-done((s32[1,1,12]{2,1,0:T(1,128)S(1)}, s32[1,1,12]{2,1,0:T(1,128)}, u32[]{:S(2)}) %copy-start.4) | copy-done | bytes 72
  1.4 2.1 %far_first.1 = (f32[136,256]{1,0:T(8,128)S(1)}, f32[136,256]{1,0:T(8,128)S(1)}, f32[136,256]{1,0:T(8,128)S(1)}, f32[136,256]{1,0:T(8,128)S(1)}, bf16[12,8,512]{2,1,0:T(8,128)(2,1)S(1)}) custom-call(s32[1,1]{1,0:T(1,128)S(6)} %copy.12.counts, s32[1,1,12]{2,1,0:T(1,128)S(1)} %copy-done.4, bf16[76,8,512]{2,1,0:T(8,128)(2,1)} %past.1, bf16[8,512,256]{2,1,0:T(8,128)(2,1)} %kernels.3), custom_call_target="tpu_custom_call" | custom-call | flops 2000000000 | tf_op jit(solution)/shard_map/far_first/pallas_call | solution.py:462
  3.5 5.5 %collective-permute-start.2 = (f16[136,256]{1,0:T(8,128)(2,1)S(1)}, f16[136,256]{1,0:T(8,128)(2,1)S(1)}, u32[]{:S(2)}, u32[]{:S(2)}) collective-permute-start(f16[136,256]{1,0:T(8,128)(2,1)S(1)} %convert_element_type.68), channel_id=1, source_target_pairs={{0,3},{1,2},{2,1},{3,0},{4,7},{5,6},{6,5},{7,4},{8,11},{9,10},{10,... | collective-permute-start | bytes 208904 | tf_op jit(solution)/shard_map/ppermute | solution.py:396
  9.0 0.1 collective-permute-start.1
  9.1 0.6 %collective-permute-start = (f16[136,256]{1,0:T(8,128)(2,1)S(1)}, f16[136,256]{1,0:T(8,128)(2,1)S(1)}, u32[]{:S(2)}, u32[]{:S(2)}) collective-permute-start(f16[136,256]{1,0:T(8,128)(2,1)S(1)} %convert_element_type.64), channel_id=1, source_target_pairs={{0,1},{1,0},{2,3},{3,2},{4,5},{5,4},{6,7},{7,6},{8,9},{9,8},{10,11... | collective-permute-start | bytes 208904 | tf_op jit(solution)/shard_map/ppermute | solution.py:396
  9.8 0.1 constant_dynamic-slice_fusion
  9.9 4.4 %prepare.1 = (bf16[256,256]{1,0:T(8,128)(2,1)S(1)}, bf16[256,256]{1,0:T(8,128)(2,1)S(1)}, bf16[2,256,256]{2,1,0:T(8,128)(2,1)S(1)}, bf16[2,256,256]{2,1,0:T(8,12...) custom-call(f32[2,256,256]{2,1,0:T(8,128)S(1)} %copy-done.2, ...), custom_call_target="tpu_custom_call" | custom-call | flops 5000000000 | tf_op jit(solution)/shard_map/prepare/pallas_call | solution.py:404
  14.4 0.6 %collective-permute-done.1 = f16[136,256]{1,0:T(8,128)(2,1)S(1)} collective-permute-done((f16[136,256]{1,0:T(8,128)(2,1)S(1)}, f16[136,256]{1,0:T(8,128)(2,1)S(1)}, u32[]{:S(2)}, u32[]{:S(2)}) %collective-permute-start.1) | collective-permute-done | bytes 69664 | tf_op jit(solution)/shard_map/ppermute | solution.py:396
  15.1 2.4 %solve.2 = (f32[128,256]{1,0:T(8,128)S(1)}, f32[136,256]{1,0:T(8,128)S(1)}, bf16[128,256]{1,0:T(8,128)(2,1)S(1)}, f32[8,256]{1,0:T(8,128)S(1)}) custom-call(f32[136,256]{1,0:T(8,128)S(1)} %get-tuple-element.37.refs_0_, f32[136,256]{1,0:T(8,128)S(1)} %convert_element_type.65.refs_1_, f32[136,256]{1,0:T(8,128)S(1)} %convert_element_type.67.refs_2_, ...), custom_call_target="tpu_custom_call" | custom-call | flops 3000000000 | tf_op jit(solution)/shard_map/solve/pallas_call | solution.py:428
  17.5 3.2 %collective-permute-start.3 = (bf16[128,256]{1,0:T(8,128)(2,1)S(1)}, bf16[128,256]{1,0:T(8,128)(2,1)S(1)}, u32[]{:S(2)}, u32[]{:S(2)}) collective-permute-start(bf16[128,256]{1,0:T(8,128)(2,1)S(1)} %get-tuple-element.57), channel_id=1, source_target_pairs={{0,24},{1,16},{2,8},{3,0},{4,28},{5,20},{6,12},{7,4},{8,1},{9,17},... | collective-permute-start | bytes 196616 | tf_op jit(solution)/shard_map/ppermute | solution.py:495
  20.7 3.1 %collective-permute-done.3.refs_0_ = bf16[128,256]{1,0:T(8,128)(2,1)S(1)} collective-permute-done((bf16[128,256]{1,0:T(8,128)(2,1)S(1)}, bf16[128,256]{1,0:T(8,128)(2,1)S(1)}, u32[]{:S(2)}, u32[]{:S(2)}) %collective-permute-start.3) | collective-permute-done | bytes 65568 | tf_op jit(solution)/shard_map/ppermute | solution.py:495
  23.8 2.4 %collective-permute-start.6 = (bf16[128,256]{1,0:T(8,128)(2,1)S(1)}, bf16[128,256]{1,0:T(8,128)(2,1)S(1)}, u32[]{:S(2)}, u32[]{:S(2)}) collective-permute-start(bf16[128,256]{1,0:T(8,128)(2,1)S(1)} %collective-permute-done.3.refs_0_), channel_id=1, source_target_pairs={{0,24},{4,28},{8,16},{12,20},{16,8},{20,12},{24,0},{28,4},{1,25},{... | collective-permute-start | bytes 196616 | tf_op jit(solution)/shard_map/ppermute | solution.py:504
  26.1 1.2 %collective-permute-start.5 = (bf16[128,256]{1,0:T(8,128)(2,1)S(1)}, bf16[128,256]{1,0:T(8,128)(2,1)S(1)}, u32[]{:S(2)}, u32[]{:S(2)}) collective-permute-start(bf16[128,256]{1,0:T(8,128)(2,1)S(1)} %collective-permute-done.3.refs_0_), channel_id=1, source_target_pairs={{0,16},{4,20},{8,24},{12,28},{16,0},{20,4},{24,8},{28,12},{1,17},{... | collective-permute-start | bytes 196616 | tf_op jit(solution)/shard_map/ppermute | solution.py:504
  27.3 0.6 %collective-permute-start.4 = (bf16[128,256]{1,0:T(8,128)(2,1)S(1)}, bf16[128,256]{1,0:T(8,128)(2,1)S(1)}, u32[]{:S(2)}, u32[]{:S(2)}) collective-permute-start(bf16[128,256]{1,0:T(8,128)(2,1)S(1)} %collective-permute-done.3.refs_0_), channel_id=1, source_target_pairs={{0,8},{4,12},{8,0},{12,4},{16,24},{20,28},{24,16},{28,20},{1,9},{5... | collective-permute-start | bytes 196616 | tf_op jit(solution)/shard_map/ppermute | solution.py:504
  28.0 1.5 %collective-permute-done.6.refs_3_ = bf16[128,256]{1,0:T(8,128)(2,1)S(1)} collective-permute-done((bf16[128,256]{1,0:T(8,128)(2,1)S(1)}, bf16[128,256]{1,0:T(8,128)(2,1)S(1)}, u32[]{:S(2)}, u32[]{:S(2)}) %collective-permute-start.6) | collective-permute-done | bytes 65568 | tf_op jit(solution)/shard_map/ppermute | solution.py:504
  29.4 1.0 %collective-permute-done.5.refs_2_ = bf16[128,256]{1,0:T(8,128)(2,1)S(1)} collective-permute-done((bf16[128,256]{1,0:T(8,128)(2,1)S(1)}, bf16[128,256]{1,0:T(8,128)(2,1)S(1)}, u32[]{:S(2)}, u32[]{:S(2)}) %collective-permute-start.5) | collective-permute-done | bytes 65568 | tf_op jit(solution)/shard_map/ppermute | solution.py:504
  30.4 1.2 %collective-permute-done.4.refs_1_ = bf16[128,256]{1,0:T(8,128)(2,1)S(1)} collective-permute-done((bf16[128,256]{1,0:T(8,128)(2,1)S(1)}, bf16[128,256]{1,0:T(8,128)(2,1)S(1)}, u32[]{:S(2)}, u32[]{:S(2)}) %collective-permute-start.4) | collective-permute-done | bytes 65568 | tf_op jit(solution)/shard_map/ppermute | solution.py:504
  31.7 1.2 %collective-permute-done.8.refs_5_ = bf16[128,256]{1,0:T(8,128)(2,1)S(1)} collective-permute-done((bf16[128,256]{1,0:T(8,128)(2,1)S(1)}, bf16[128,256]{1,0:T(8,128)(2,1)S(1)}, u32[]{:S(2)}, u32[]{:S(2)}) %collective-permute-start.8) | collective-permute-done | bytes 65568 | tf_op jit(solution)/shard_map/ppermute | solution.py:512
  32.9 1.8 %far_next.1 = (f32[136,256]{1,0:T(8,128)S(1)}, f32[136,256]{1,0:T(8,128)S(1)}, f32[136,256]{1,0:T(8,128)S(1)}, f32[136,256]{1,0:T(8,128)S(1)}) custom-call(s32[1,1]{1,0:T(1,128)S(6)} %copy.12.counts, s32[1,1,12]{2,1,0:T(1,128)S(1)} %copy-done.5, bf16[12,8,512]{2,1,0:T(8,128)(2,1)S(1)} %get-tuple-element.36.tail, bf16[8,512,256]{2,1,0:T(8,128)(2,1)S(1)} %copy-done.1, ...), custom_call_target="tpu_custom_call" | custom-call | flops 3000000000 | tf_op jit(solution)/shard_map/far_next/pallas_call | solution.py:513
  34.7 3.9 %collective-permute-start.13 = (f16[136,256]{1,0:T(8,128)(2,1)S(1)}, f16[136,256]{1,0:T(8,128)(2,1)S(1)}, u32[]{:S(2)}, u32[]{:S(2)}) collective-permute-start(f16[136,256]{1,0:T(8,128)(2,1)S(1)} %convert_element_type.74), channel_id=1, source_target_pairs={{0,3},{1,2},{2,1},{3,0},{4,7},{5,6},{6,5},{7,4},{8,11},{9,10},{10,... | collective-permute-start | bytes 208904 | tf_op jit(solution)/shard_map/ppermute | solution.py:396
  38.6 0.1 collective-permute-start.12
  38.7 0.6 %collective-permute-start.11 = (f16[136,256]{1,0:T(8,128)(2,1)S(1)}, f16[136,256]{1,0:T(8,128)(2,1)S(1)}, u32[]{:S(2)}, u32[]{:S(2)}) collective-permute-start(f16[136,256]{1,0:T(8,128)(2,1)S(1)} %convert_element_type.70), channel_id=1, source_target_pairs={{0,1},{1,0},{2,3},{3,2},{4,5},{5,4},{6,7},{7,6},{8,9},{9,8},{10,11... | collective-permute-start | bytes 208904 | tf_op jit(solution)/shard_map/ppermute | solution.py:396
  39.3 3.9 %collective-permute-start.19 = (f16[136,256]{1,0:T(8,128)(2,1)S(1)}, f16[136,256]{1,0:T(8,128)(2,1)S(1)}, u32[]{:S(2)}, u32[]{:S(2)}) collective-permute-start(f16[136,256]{1,0:T(8,128)(2,1)S(1)} %convert_element_type.80), channel_id=1, source_target_pairs={{0,3},{1,2},{2,1},{3,0},{4,7},{5,6},{6,5},{7,4},{8,11},{9,10},{10,... | collective-permute-start | bytes 208904 | tf_op jit(solution)/shard_map/ppermute | solution.py:396
  43.2 0.6 %collective-permute-start.17 = (f16[136,256]{1,0:T(8,128)(2,1)S(1)}, f16[136,256]{1,0:T(8,128)(2,1)S(1)}, u32[]{:S(2)}, u32[]{:S(2)}) collective-permute-start(f16[136,256]{1,0:T(8,128)(2,1)S(1)} %convert_element_type.80), channel_id=1, source_target_pairs={{0,1},{1,0},{2,3},{3,2},{4,5},{5,4},{6,7},{7,6},{8,9},{9,8},{10,11... | collective-permute-start | bytes 208904 | tf_op jit(solution)/shard_map/ppermute | solution.py:396
  43.9 2.1 %collective-permute-done.12 = f16[136,256]{1,0:T(8,128)(2,1)S(1)} collective-permute-done((f16[136,256]{1,0:T(8,128)(2,1)S(1)}, f16[136,256]{1,0:T(8,128)(2,1)S(1)}, u32[]{:S(2)}, u32[]{:S(2)}) %collective-permute-start.12) | collective-permute-done | bytes 69664 | tf_op jit(solution)/shard_map/ppermute | solution.py:396
  46.0 2.4 %solve.3 = (f32[128,256]{1,0:T(8,128)S(1)}, f32[136,256]{1,0:T(8,128)S(1)}) custom-call(f32[136,256]{1,0:T(8,128)S(1)} %get-tuple-element.58.refs_0_, f32[136,256]{1,0:T(8,128)S(1)} %convert_element_type.71.refs_1_, f32[136,256]{1,0:T(8,128)S(1)} %convert_element_type.73.refs_2_, f32[136,256]{1,0:T(8,128)S(1)} %convert_element_type.75.refs_3_, ...), custom_call_target="tpu_custom_call" | custom-call | flops 3000000000 | tf_op jit(solution)/shard_map/solve/pallas_call | solution.py:428
  48.4 2.2 %collective-permute-start.16 = (f16[136,256]{1,0:T(8,128)(2,1)S(1)}, f16[136,256]{1,0:T(8,128)(2,1)S(1)}, u32[]{:S(2)}, u32[]{:S(2)}) collective-permute-start(f16[136,256]{1,0:T(8,128)(2,1)S(1)} %convert_element_type.76), channel_id=1, source_target_pairs={{0,3},{1,2},{2,1},{3,0},{4,7},{5,6},{6,5},{7,4},{8,11},{9,10},{10,... | collective-permute-start | bytes 208904 | tf_op jit(solution)/shard_map/ppermute | solution.py:396
  50.6 2.3 %collective-permute-start.14 = (f16[136,256]{1,0:T(8,128)(2,1)S(1)}, f16[136,256]{1,0:T(8,128)(2,1)S(1)}, u32[]{:S(2)}, u32[]{:S(2)}) collective-permute-start(f16[136,256]{1,0:T(8,128)(2,1)S(1)} %convert_element_type.76), channel_id=1, source_target_pairs={{0,1},{1,0},{2,3},{3,2},{4,5},{5,4},{6,7},{7,6},{8,9},{9,8},{10,11... | collective-permute-start | bytes 208904 | tf_op jit(solution)/shard_map/ppermute | solution.py:396
  53.0 1.0 %spread.2.refs_3_ = f32[128,8,256]{2,1,0:T(8,128)} custom-call(f32[128,256]{1,0:T(8,128)S(1)} %get-tuple-element.65.own, f32[136,256]{1,0:T(8,128)S(1)} %convert_element_type.81.refs_0_, f32[136,256]{1,0:T(8,128)S(1)} %convert_element_type.82.refs_1_, f32[136,256]{1,0:T(8,128)S(1)} %convert_element_type.83.refs_2_), custom_call_target="tpu_custom_call" | custom-call | tf_op jit(solution)/shard_map/spread/pallas_call | solution.py:440
  54.0 0.7 %collective-permute-done.16 = f16[136,256]{1,0:T(8,128)(2,1)S(1)} collective-permute-done((f16[136,256]{1,0:T(8,128)(2,1)S(1)}, f16[136,256]{1,0:T(8,128)(2,1)S(1)}, u32[]{:S(2)}, u32[]{:S(2)}) %collective-permute-start.16) | collective-permute-done | bytes 69664 | tf_op jit(solution)/shard_map/ppermute | solution.py:396
  54.6 1.5 %collective-permute-done.15 = f16[136,256]{1,0:T(8,128)(2,1)S(1)} collective-permute-done((f16[136,256]{1,0:T(8,128)(2,1)S(1)}, f16[136,256]{1,0:T(8,128)(2,1)S(1)}, u32[]{:S(2)}, u32[]{:S(2)}) %collective-permute-start.15) | collective-permute-done | bytes 69664 | tf_op jit(solution)/shard_map/ppermute | solution.py:396
  56.1 1.0 %spread.3 = f32[128,8,256]{2,1,0:T(8,128)} custom-call(f32[128,256]{1,0:T(8,128)S(1)} %get-tuple-element.63.own, f32[136,256]{1,0:T(8,128)S(1)} %convert_element_type.77.refs_0_, f32[136,256]{1,0:T(8,128)S(1)} %convert_element_type.78.refs_1_, f32[136,256]{1,0:T(8,128)S(1)} %convert_element_type.79.refs_2_, ...), custom_call_target="tpu_custom_call", output_to_operand_aliasing={{}: (4, {})} | custom-call | tf_op jit(solution)/shard_map/spread/pallas_call | solution.py:440
  (51 shorter events, 0.4 us)
Async XLA Ops:
  0.0 9.8 %copy-start = (bf16[128,8,256]{2,1,0:T(8,128)(2,1)S(1)}, bf16[128,8,256]{2,1,0:T(8,128)(2,1)}, u32[]{:S(2)}) copy-start(bf16[128,8,256]{2,1,0:T(8,128)(2,1)} %param.7) | copy-start | bytes 1572868
  0.7 0.7 %copy-start.4 = (s32[1,1,12]{2,1,0:T(1,128)S(1)}, s32[1,1,12]{2,1,0:T(1,128)}, u32[]{:S(2)}) copy-start(s32[1,1,12]{2,1,0:T(1,128)} %offsets.3) | copy-start | bytes 148
  1.4 8.5 %copy-start.2 = (f32[2,256,256]{2,1,0:T(8,128)S(1)}, f32[2,256,256]{2,1,0:T(8,128)}, u32[]{:S(2)}) copy-start(f32[2,256,256]{2,1,0:T(8,128)} %couplings.1) | copy-start | bytes 1572868
  1.4 8.6 %copy-start.3 = (f32[256,256]{1,0:T(8,128)S(1)}, f32[256,256]{1,0:T(8,128)}, u32[]{:S(2)}) copy-start(f32[256,256]{1,0:T(8,128)} %inverse.1) | copy-start | bytes 786436
  3.5 10.8 %collective-permute-start.2 = (f16[136,256]{1,0:T(8,128)(2,1)S(1)}, f16[136,256]{1,0:T(8,128)(2,1)S(1)}, u32[]{:S(2)}, u32[]{:S(2)}) collective-permute-start(f16[136,256]{1,0:T(8,128)(2,1)S(1)} %convert_element_type.68), channel_id=1, source_target_pairs={{0,3},{1,2},{2,1},{3,0},{4,7},{5,6},{6,5},{7,4},{8,11},{9,10},{10,... | collective-permute-start | bytes 208904 | tf_op jit(solution)/shard_map/ppermute | solution.py:396
  9.0 6.0 %collective-permute-start.1 = (f16[136,256]{1,0:T(8,128)(2,1)S(1)}, f16[136,256]{1,0:T(8,128)(2,1)S(1)}, u32[]{:S(2)}, u32[]{:S(2)}) collective-permute-start(f16[136,256]{1,0:T(8,128)(2,1)S(1)} %convert_element_type.66), channel_id=1, source_target_pairs={{0,2},{1,3},{2,0},{3,1},{4,6},{5,7},{6,4},{7,5},{8,10},{9,11},{10,... | collective-permute-start | bytes 208904 | tf_op jit(solution)/shard_map/ppermute | solution.py:396
  9.1 5.9 %collective-permute-start = (f16[136,256]{1,0:T(8,128)(2,1)S(1)}, f16[136,256]{1,0:T(8,128)(2,1)S(1)}, u32[]{:S(2)}, u32[]{:S(2)}) collective-permute-start(f16[136,256]{1,0:T(8,128)(2,1)S(1)} %convert_element_type.64), channel_id=1, source_target_pairs={{0,1},{1,0},{2,3},{3,2},{4,5},{5,4},{6,7},{7,6},{8,9},{9,8},{10,11... | collective-permute-start | bytes 208904 | tf_op jit(solution)/shard_map/ppermute | solution.py:396
  15.0 17.8 %copy-start.1 = (bf16[8,512,256]{2,1,0:T(8,128)(2,1)S(1)}, bf16[8,512,256]{2,1,0:T(8,128)(2,1)}, u32[]{:S(2)}) copy-start(bf16[8,512,256]{2,1,0:T(8,128)(2,1)} %kernels.3) | copy-start | bytes 6291460
  15.0 17.8 %copy-start.5 = (s32[1,1,12]{2,1,0:T(1,128)S(1)}, s32[1,1,12]{2,1,0:T(1,128)}, u32[]{:S(2)}) copy-start(s32[1,1,12]{2,1,0:T(1,128)} %offsets.3) | copy-start | bytes 148
  17.5 6.3 %collective-permute-start.3 = (bf16[128,256]{1,0:T(8,128)(2,1)S(1)}, bf16[128,256]{1,0:T(8,128)(2,1)S(1)}, u32[]{:S(2)}, u32[]{:S(2)}) collective-permute-start(bf16[128,256]{1,0:T(8,128)(2,1)S(1)} %get-tuple-element.57), channel_id=1, source_target_pairs={{0,24},{1,16},{2,8},{3,0},{4,28},{5,20},{6,12},{7,4},{8,1},{9,17},... | collective-permute-start | bytes 196616 | tf_op jit(solution)/shard_map/ppermute | solution.py:495
  23.8 5.6 %collective-permute-start.6 = (bf16[128,256]{1,0:T(8,128)(2,1)S(1)}, bf16[128,256]{1,0:T(8,128)(2,1)S(1)}, u32[]{:S(2)}, u32[]{:S(2)}) collective-permute-start(bf16[128,256]{1,0:T(8,128)(2,1)S(1)} %collective-permute-done.3.refs_0_), channel_id=1, source_target_pairs={{0,24},{4,28},{8,16},{12,20},{16,8},{20,12},{24,0},{28,4},{1,25},{... | collective-permute-start | bytes 196616 | tf_op jit(solution)/shard_map/ppermute | solution.py:504
  26.1 4.3 %collective-permute-start.5 = (bf16[128,256]{1,0:T(8,128)(2,1)S(1)}, bf16[128,256]{1,0:T(8,128)(2,1)S(1)}, u32[]{:S(2)}, u32[]{:S(2)}) collective-permute-start(bf16[128,256]{1,0:T(8,128)(2,1)S(1)} %collective-permute-done.3.refs_0_), channel_id=1, source_target_pairs={{0,16},{4,20},{8,24},{12,28},{16,0},{20,4},{24,8},{28,12},{1,17},{... | collective-permute-start | bytes 196616 | tf_op jit(solution)/shard_map/ppermute | solution.py:504
  27.3 4.3 %collective-permute-start.4 = (bf16[128,256]{1,0:T(8,128)(2,1)S(1)}, bf16[128,256]{1,0:T(8,128)(2,1)S(1)}, u32[]{:S(2)}, u32[]{:S(2)}) collective-permute-start(bf16[128,256]{1,0:T(8,128)(2,1)S(1)} %collective-permute-done.3.refs_0_), channel_id=1, source_target_pairs={{0,8},{4,12},{8,0},{12,4},{16,24},{20,28},{24,16},{28,20},{1,9},{5... | collective-permute-start | bytes 196616 | tf_op jit(solution)/shard_map/ppermute | solution.py:504
  28.0 3.7 %collective-permute-start.7 = (bf16[128,256]{1,0:T(8,128)(2,1)S(1)}, bf16[128,256]{1,0:T(8,128)(2,1)S(1)}, u32[]{:S(2)}, u32[]{:S(2)}) collective-permute-start(bf16[128,256]{1,0:T(8,128)(2,1)S(1)} %collective-permute-done.3.refs_0_), channel_id=1, source_target_pairs={{0,4},{4,0},{8,12},{12,8},{16,20},{20,16},{24,28},{28,24},{1,5},{5... | collective-permute-start | bytes 196616 | tf_op jit(solution)/shard_map/ppermute | solution.py:512
  29.4 2.2 %collective-permute-start.10 = (bf16[128,256]{1,0:T(8,128)(2,1)S(1)}, bf16[128,256]{1,0:T(8,128)(2,1)S(1)}, u32[]{:S(2)}, u32[]{:S(2)}) collective-permute-start(bf16[128,256]{1,0:T(8,128)(2,1)S(1)} %collective-permute-done.6.refs_3_), channel_id=1, source_target_pairs={{0,4},{4,0},{8,12},{12,8},{16,20},{20,16},{24,28},{28,24},{1,5},{5... | collective-permute-start | bytes 196616 | tf_op jit(solution)/shard_map/ppermute | solution.py:512
  30.4 1.3 %collective-permute-start.9 = (bf16[128,256]{1,0:T(8,128)(2,1)S(1)}, bf16[128,256]{1,0:T(8,128)(2,1)S(1)}, u32[]{:S(2)}, u32[]{:S(2)}) collective-permute-start(bf16[128,256]{1,0:T(8,128)(2,1)S(1)} %collective-permute-done.5.refs_2_), channel_id=1, source_target_pairs={{0,4},{4,0},{8,12},{12,8},{16,20},{20,16},{24,28},{28,24},{1,5},{5... | collective-permute-start | bytes 196616 | tf_op jit(solution)/shard_map/ppermute | solution.py:512
  31.6 1.3 %collective-permute-start.8 = (bf16[128,256]{1,0:T(8,128)(2,1)S(1)}, bf16[128,256]{1,0:T(8,128)(2,1)S(1)}, u32[]{:S(2)}, u32[]{:S(2)}) collective-permute-start(bf16[128,256]{1,0:T(8,128)(2,1)S(1)} %collective-permute-done.4.refs_1_), channel_id=1, source_target_pairs={{0,4},{4,0},{8,12},{12,8},{16,20},{20,16},{24,28},{28,24},{1,5},{5... | collective-permute-start | bytes 196616 | tf_op jit(solution)/shard_map/ppermute | solution.py:512
  34.7 8.5 %collective-permute-start.13 = (f16[136,256]{1,0:T(8,128)(2,1)S(1)}, f16[136,256]{1,0:T(8,128)(2,1)S(1)}, u32[]{:S(2)}, u32[]{:S(2)}) collective-permute-start(f16[136,256]{1,0:T(8,128)(2,1)S(1)} %convert_element_type.74), channel_id=1, source_target_pairs={{0,3},{1,2},{2,1},{3,0},{4,7},{5,6},{6,5},{7,4},{8,11},{9,10},{10,... | collective-permute-start | bytes 208904 | tf_op jit(solution)/shard_map/ppermute | solution.py:396
  38.6 7.3 %collective-permute-start.12 = (f16[136,256]{1,0:T(8,128)(2,1)S(1)}, f16[136,256]{1,0:T(8,128)(2,1)S(1)}, u32[]{:S(2)}, u32[]{:S(2)}) collective-permute-start(f16[136,256]{1,0:T(8,128)(2,1)S(1)} %convert_element_type.72), channel_id=1, source_target_pairs={{0,2},{1,3},{2,0},{3,1},{4,6},{5,7},{6,4},{7,5},{8,10},{9,11},{10,... | collective-permute-start | bytes 208904 | tf_op jit(solution)/shard_map/ppermute | solution.py:396
  38.7 7.3 %collective-permute-start.11 = (f16[136,256]{1,0:T(8,128)(2,1)S(1)}, f16[136,256]{1,0:T(8,128)(2,1)S(1)}, u32[]{:S(2)}, u32[]{:S(2)}) collective-permute-start(f16[136,256]{1,0:T(8,128)(2,1)S(1)} %convert_element_type.70), channel_id=1, source_target_pairs={{0,1},{1,0},{2,3},{3,2},{4,5},{5,4},{6,7},{7,6},{8,9},{9,8},{10,11... | collective-permute-start | bytes 208904 | tf_op jit(solution)/shard_map/ppermute | solution.py:396
  39.3 11.3 %collective-permute-start.19 = (f16[136,256]{1,0:T(8,128)(2,1)S(1)}, f16[136,256]{1,0:T(8,128)(2,1)S(1)}, u32[]{:S(2)}, u32[]{:S(2)}) collective-permute-start(f16[136,256]{1,0:T(8,128)(2,1)S(1)} %convert_element_type.80), channel_id=1, source_target_pairs={{0,3},{1,2},{2,1},{3,0},{4,7},{5,6},{6,5},{7,4},{8,11},{9,10},{10,... | collective-permute-start | bytes 208904 | tf_op jit(solution)/shard_map/ppermute | solution.py:396
  43.2 9.7 %collective-permute-start.18 = (f16[136,256]{1,0:T(8,128)(2,1)S(1)}, f16[136,256]{1,0:T(8,128)(2,1)S(1)}, u32[]{:S(2)}, u32[]{:S(2)}) collective-permute-start(f16[136,256]{1,0:T(8,128)(2,1)S(1)} %convert_element_type.80), channel_id=1, source_target_pairs={{0,2},{1,3},{2,0},{3,1},{4,6},{5,7},{6,4},{7,5},{8,10},{9,11},{10,... | collective-permute-start | bytes 208904 | tf_op jit(solution)/shard_map/ppermute | solution.py:396
  43.2 9.7 %collective-permute-start.17 = (f16[136,256]{1,0:T(8,128)(2,1)S(1)}, f16[136,256]{1,0:T(8,128)(2,1)S(1)}, u32[]{:S(2)}, u32[]{:S(2)}) collective-permute-start(f16[136,256]{1,0:T(8,128)(2,1)S(1)} %convert_element_type.80), channel_id=1, source_target_pairs={{0,1},{1,0},{2,3},{3,2},{4,5},{5,4},{6,7},{7,6},{8,9},{9,8},{10,11... | collective-permute-start | bytes 208904 | tf_op jit(solution)/shard_map/ppermute | solution.py:396
  48.4 6.2 %collective-permute-start.16 = (f16[136,256]{1,0:T(8,128)(2,1)S(1)}, f16[136,256]{1,0:T(8,128)(2,1)S(1)}, u32[]{:S(2)}, u32[]{:S(2)}) collective-permute-start(f16[136,256]{1,0:T(8,128)(2,1)S(1)} %convert_element_type.76), channel_id=1, source_target_pairs={{0,3},{1,2},{2,1},{3,0},{4,7},{5,6},{6,5},{7,4},{8,11},{9,10},{10,... | collective-permute-start | bytes 208904 | tf_op jit(solution)/shard_map/ppermute | solution.py:396
  50.6 5.5 %collective-permute-start.15 = (f16[136,256]{1,0:T(8,128)(2,1)S(1)}, f16[136,256]{1,0:T(8,128)(2,1)S(1)}, u32[]{:S(2)}, u32[]{:S(2)}) collective-permute-start(f16[136,256]{1,0:T(8,128)(2,1)S(1)} %convert_element_type.76), channel_id=1, source_target_pairs={{0,2},{1,3},{2,0},{3,1},{4,6},{5,7},{6,4},{7,5},{8,10},{9,11},{10,... | collective-permute-start | bytes 208904 | tf_op jit(solution)/shard_map/ppermute | solution.py:396
  50.6 5.5 %collective-permute-start.14 = (f16[136,256]{1,0:T(8,128)(2,1)S(1)}, f16[136,256]{1,0:T(8,128)(2,1)S(1)}, u32[]{:S(2)}, u32[]{:S(2)}) collective-permute-start(f16[136,256]{1,0:T(8,128)(2,1)S(1)} %convert_element_type.76), channel_id=1, source_target_pairs={{0,1},{1,0},{2,3},{3,2},{4,5},{5,4},{6,7},{7,6},{8,9},{9,8},{10,11... | collective-permute-start | bytes 208904 | tf_op jit(solution)/shard_map/ppermute | solution.py:396

commit v5 on v4

--- a/solution.py
+++ b/solution.py
@@ -330,26 +330,34 @@
 
 
 def spread_kernel(block, share, own, *refs):
-    (*chunks, out, strided, ready, sem) = refs
-    steps, loads, rows = ready.shape
+    (*chunks, out, ready, sems) = refs
+    groups, steps, loads, _ = ready.shape
     sources = (len(chunks) + 1) if block == 0 else len(chunks)
     size = share * steps
     source = lax.axis_index("src")
-    for index, chunk in enumerate([own, *chunks][:sources]):
-        first = sender(source, index, sources) * share % loads
-        value = chunk[...] if index == 0 else unscaled(chunk, size, size)
-        for item in range(share):
-            for group in range(rows // LANES):
-                strided[group, pl.ds(first + item, steps, stride=loads), :] = value[
-                    item * steps : (item + 1) * steps, group * LANES : (group + 1) * LANES
+    rows_of = ready.reshape(groups, steps * loads, LANES)
+    copies = []
+    for group in range(groups):
+        lanes = slice(group * LANES, (group + 1) * LANES)
+        for index, chunk in enumerate([own, *chunks][:sources]):
+            first = sender(source, index, sources) * share % loads
+            value = chunk[:size, lanes]
+            if index > 0:
+                value = value * jnp.exp2(chunk[size : size + 1, lanes] - HEADROOM)
+            for item in range(share):
+                rows_of[group, pl.ds(first + item, steps, stride=loads), :] = value[
+                    item * steps : (item + 1) * steps
                 ]
-    for group in range(rows // LANES):
-        ready[:, :, group * LANES : (group + 1) * LANES] = strided[group].reshape(
-            steps, loads, LANES
+        copies.append(
+            pltpu.make_async_copy(
+                ready.at[group],
+                out.at[pl.ds(block * steps, steps), :, pl.ds(group * LANES, LANES)],
+                sems.at[group],
+            )
         )
-    copy = pltpu.make_async_copy(ready, out.at[pl.ds(block * steps, steps)], sem)
-    copy.start()
-    copy.wait()
+        copies[-1].start()
+    for copy in copies:
+        copy.wait()
 
 
 def landing(plane, sources):
@@ -443,9 +451,8 @@
             in_specs=[VMEM] * sources + [HBM] * len(last),
             out_specs=HBM,
             scratch_shapes=[
-                pltpu.VMEM((groups, steps * loads, LANES), F32),
-                pltpu.VMEM((steps, loads, rows), F32),
-                pltpu.SemaphoreType.DMA,
+                pltpu.VMEM((groups, steps, loads, LANES), F32),
+                pltpu.SemaphoreType.DMA((groups,)),
             ],
             input_output_aliases={sources: 0} if last else {},
             compiler_params=params(8),

time: 57.7 us -> 57.8 us (level)
  waiting for transfers between devices: 12.8 us -> 14.2 us
  starting transfers between devices: 27.1 us -> 26.5 us
    ppermute x12, waiting for transfers between devices: 4.82 us -> 5.76 us  [trade(): return lax.ppermute(value, 'src', pairs)]
    ppermute x1, starting transfers between devices: 3.2 us -> 2.6 us  [local(): landed = lax.ppermute(rounded, ('tgt', 'src'), moves)]
  transfers between devices with their start and end apart: 20 -> 20, of which waited for: 9 -> 11; matrix products, arithmetic and copies ran while one was open for 1% -> 1% of each run, Pallas kernels for 14% -> 13%
where the time goes in v5:
time: 57.8 us; the launch traced here: 57.9 us
  starting transfers between devices  26.5 us (46%)
  Pallas kernels  15 us (26%)
  waiting for transfers between devices  14.2 us (25%)
  between operations  1.17 us (2%)
  local copies, waits for them, and re-layouts  0.84 us (1%)
    ppermute x12, starting transfers between devices, trade(): return lax.ppermute(value, 'src', pairs)  19.3 us
    ppermute x12, waiting for transfers between devices, trade(): return lax.ppermute(value, 'src', pairs)  5.76 us
    pallas_call x2, Pallas kernels, solve(): pl.pallas_call(functools.partial(solve_kernel, steps, share, levels, len(...  4.87 us
    ppermute x3, starting transfers between devices, local(): arrived.append(lax.ppermute(landed, 'tgt', pairs))  4.56 us
    pallas_call x1, Pallas kernels, local(): pl.pallas_call(functools.partial(prepare_kernel, levels), out_shape=[jax....  4.36 us
    ppermute x1, waiting for transfers between devices, local(): landed = lax.ppermute(rounded, ('tgt', 'src'), moves)  3.62 us
    ppermute x3, waiting for transfers between devices, local(): arrived.append(lax.ppermute(landed, 'tgt', pairs))  3.59 us
    ppermute x1, starting transfers between devices, local(): landed = lax.ppermute(rounded, ('tgt', 'src'), moves)  2.6 us
  transfers between devices with their start and end apart: 20, of which 11 were waited for; matrix products, arithmetic and copies ran while one was open for 1% of the time, Pallas kernels for 13%

profile of v5, /device:TPU:0, one launch (start us, length us, event | category | flops | bytes accessed | tf_op | source)
XLA Modules:
  0.0 57.9 jit_solution(7768089287353606269)
XLA Ops:
  0.7 0.6 %copy-done.4 = s32[1,1,12]{2,1,0:T(1,128)S(1)} copy-done((s32[1,1,12]{2,1,0:T(1,128)S(1)}, s32[1,1,12]{2,1,0:T(1,128)}, u32[]{:S(2)}) %copy-start.4) | copy-done | bytes 72
  1.4 2.1 %far_first.1 = (f32[136,256]{1,0:T(8,128)S(1)}, f32[136,256]{1,0:T(8,128)S(1)}, f32[136,256]{1,0:T(8,128)S(1)}, f32[136,256]{1,0:T(8,128)S(1)}, bf16[12,8,512]{2,1,0:T(8,128)(2,1)S(1)}) custom-call(s32[1,1]{1,0:T(1,128)S(6)} %copy.12.counts, s32[1,1,12]{2,1,0:T(1,128)S(1)} %copy-done.4, bf16[76,8,512]{2,1,0:T(8,128)(2,1)} %past.1, bf16[8,512,256]{2,1,0:T(8,128)(2,1)} %kernels.3), custom_call_target="tpu_custom_call" | custom-call | flops 2000000000 | tf_op jit(solution)/shard_map/far_first/pallas_call | solution.py:469
  3.5 5.1 %collective-permute-start.2 = (f16[136,256]{1,0:T(8,128)(2,1)S(1)}, f16[136,256]{1,0:T(8,128)(2,1)S(1)}, u32[]{:S(2)}, u32[]{:S(2)}) collective-permute-start(f16[136,256]{1,0:T(8,128)(2,1)S(1)} %convert_element_type.68), channel_id=1, source_target_pairs={{0,3},{1,2},{2,1},{3,0},{4,7},{5,6},{6,5},{7,4},{8,11},{9,10},{10,... | collective-permute-start | bytes 208904 | tf_op jit(solution)/shard_map/ppermute | solution.py:404
  8.7 0.6 %collective-permute-start = (f16[136,256]{1,0:T(8,128)(2,1)S(1)}, f16[136,256]{1,0:T(8,128)(2,1)S(1)}, u32[]{:S(2)}, u32[]{:S(2)}) collective-permute-start(f16[136,256]{1,0:T(8,128)(2,1)S(1)} %convert_element_type.64), channel_id=1, source_target_pairs={{0,1},{1,0},{2,3},{3,2},{4,5},{5,4},{6,7},{7,6},{8,9},{9,8},{10,11... | collective-permute-start | bytes 208904 | tf_op jit(solution)/shard_map/ppermute | solution.py:404
  9.4 0.1 constant_dynamic-slice_fusion
  9.6 4.4 %prepare.1 = (bf16[256,256]{1,0:T(8,128)(2,1)S(1)}, bf16[256,256]{1,0:T(8,128)(2,1)S(1)}, bf16[2,256,256]{2,1,0:T(8,128)(2,1)S(1)}, bf16[2,256,256]{2,1,0:T(8,12...) custom-call(f32[2,256,256]{2,1,0:T(8,128)S(1)} %copy-done.2, ...), custom_call_target="tpu_custom_call" | custom-call | flops 5000000000 | tf_op jit(solution)/shard_map/prepare/pallas_call | solution.py:412
  14.0 1.0 %collective-permute-done.1 = f16[136,256]{1,0:T(8,128)(2,1)S(1)} collective-permute-done((f16[136,256]{1,0:T(8,128)(2,1)S(1)}, f16[136,256]{1,0:T(8,128)(2,1)S(1)}, u32[]{:S(2)}, u32[]{:S(2)}) %collective-permute-start.1) | collective-permute-done | bytes 69664 | tf_op jit(solution)/shard_map/ppermute | solution.py:404
  15.0 0.2 collective-permute-done
  15.2 2.4 %solve.2 = (f32[128,256]{1,0:T(8,128)S(1)}, f32[136,256]{1,0:T(8,128)S(1)}, bf16[128,256]{1,0:T(8,128)(2,1)S(1)}, f32[8,256]{1,0:T(8,128)S(1)}) custom-call(f32[136,256]{1,0:T(8,128)S(1)} %get-tuple-element.37.refs_0_, f32[136,256]{1,0:T(8,128)S(1)} %convert_element_type.65.refs_1_, f32[136,256]{1,0:T(8,128)S(1)} %convert_element_type.67.refs_2_, ...), custom_call_target="tpu_custom_call" | custom-call | flops 3000000000 | tf_op jit(solution)/shard_map/solve/pallas_call | solution.py:436
  17.7 2.6 %collective-permute-start.3 = (bf16[128,256]{1,0:T(8,128)(2,1)S(1)}, bf16[128,256]{1,0:T(8,128)(2,1)S(1)}, u32[]{:S(2)}, u32[]{:S(2)}) collective-permute-start(bf16[128,256]{1,0:T(8,128)(2,1)S(1)} %get-tuple-element.57), channel_id=1, source_target_pairs={{0,24},{1,16},{2,8},{3,0},{4,28},{5,20},{6,12},{7,4},{8,1},{9,17},... | collective-permute-start | bytes 196616 | tf_op jit(solution)/shard_map/ppermute | solution.py:502
  20.3 3.6 %collective-permute-done.3.refs_0_ = bf16[128,256]{1,0:T(8,128)(2,1)S(1)} collective-permute-done((bf16[128,256]{1,0:T(8,128)(2,1)S(1)}, bf16[128,256]{1,0:T(8,128)(2,1)S(1)}, u32[]{:S(2)}, u32[]{:S(2)}) %collective-permute-start.3) | collective-permute-done | bytes 65568 | tf_op jit(solution)/shard_map/ppermute | solution.py:502
  23.9 1.9 %collective-permute-start.6 = (bf16[128,256]{1,0:T(8,128)(2,1)S(1)}, bf16[128,256]{1,0:T(8,128)(2,1)S(1)}, u32[]{:S(2)}, u32[]{:S(2)}) collective-permute-start(bf16[128,256]{1,0:T(8,128)(2,1)S(1)} %collective-permute-done.3.refs_0_), channel_id=1, source_target_pairs={{0,24},{4,28},{8,16},{12,20},{16,8},{20,12},{24,0},{28,4},{1,25},{... | collective-permute-start | bytes 196616 | tf_op jit(solution)/shard_map/ppermute | solution.py:511
  25.8 2.0 %collective-permute-start.5 = (bf16[128,256]{1,0:T(8,128)(2,1)S(1)}, bf16[128,256]{1,0:T(8,128)(2,1)S(1)}, u32[]{:S(2)}, u32[]{:S(2)}) collective-permute-start(bf16[128,256]{1,0:T(8,128)(2,1)S(1)} %collective-permute-done.3.refs_0_), channel_id=1, source_target_pairs={{0,16},{4,20},{8,24},{12,28},{16,0},{20,4},{24,8},{28,12},{1,17},{... | collective-permute-start | bytes 196616 | tf_op jit(solution)/shard_map/ppermute | solution.py:511
  27.8 0.7 %collective-permute-start.4 = (bf16[128,256]{1,0:T(8,128)(2,1)S(1)}, bf16[128,256]{1,0:T(8,128)(2,1)S(1)}, u32[]{:S(2)}, u32[]{:S(2)}) collective-permute-start(bf16[128,256]{1,0:T(8,128)(2,1)S(1)} %collective-permute-done.3.refs_0_), channel_id=1, source_target_pairs={{0,8},{4,12},{8,0},{12,4},{16,24},{20,28},{24,16},{28,20},{1,9},{5... | collective-permute-start | bytes 196616 | tf_op jit(solution)/shard_map/ppermute | solution.py:511
  28.4 0.7 %collective-permute-done.6.refs_3_ = bf16[128,256]{1,0:T(8,128)(2,1)S(1)} collective-permute-done((bf16[128,256]{1,0:T(8,128)(2,1)S(1)}, bf16[128,256]{1,0:T(8,128)(2,1)S(1)}, u32[]{:S(2)}, u32[]{:S(2)}) %collective-permute-start.6) | collective-permute-done | bytes 65568 | tf_op jit(solution)/shard_map/ppermute | solution.py:511
  29.2 1.1 %collective-permute-done.5.refs_2_ = bf16[128,256]{1,0:T(8,128)(2,1)S(1)} collective-permute-done((bf16[128,256]{1,0:T(8,128)(2,1)S(1)}, bf16[128,256]{1,0:T(8,128)(2,1)S(1)}, u32[]{:S(2)}, u32[]{:S(2)}) %collective-permute-start.5) | collective-permute-done | bytes 65568 | tf_op jit(solution)/shard_map/ppermute | solution.py:511
  30.3 1.7 %collective-permute-done.4.refs_1_ = bf16[128,256]{1,0:T(8,128)(2,1)S(1)} collective-permute-done((bf16[128,256]{1,0:T(8,128)(2,1)S(1)}, bf16[128,256]{1,0:T(8,128)(2,1)S(1)}, u32[]{:S(2)}, u32[]{:S(2)}) %collective-permute-start.4) | collective-permute-done | bytes 65568 | tf_op jit(solution)/shard_map/ppermute | solution.py:511
  32.1 1.2 %collective-permute-done.8.refs_5_ = bf16[128,256]{1,0:T(8,128)(2,1)S(1)} collective-permute-done((bf16[128,256]{1,0:T(8,128)(2,1)S(1)}, bf16[128,256]{1,0:T(8,128)(2,1)S(1)}, u32[]{:S(2)}, u32[]{:S(2)}) %collective-permute-start.8) | collective-permute-done | bytes 65568 | tf_op jit(solution)/shard_map/ppermute | solution.py:519
  33.3 1.8 %far_next.1 = (f32[136,256]{1,0:T(8,128)S(1)}, f32[136,256]{1,0:T(8,128)S(1)}, f32[136,256]{1,0:T(8,128)S(1)}, f32[136,256]{1,0:T(8,128)S(1)}) custom-call(s32[1,1]{1,0:T(1,128)S(6)} %copy.12.counts, s32[1,1,12]{2,1,0:T(1,128)S(1)} %copy-done.5, bf16[12,8,512]{2,1,0:T(8,128)(2,1)S(1)} %get-tuple-element.36.tail, bf16[8,512,256]{2,1,0:T(8,128)(2,1)S(1)} %copy-done.1, ...), custom_call_target="tpu_custom_call" | custom-call | flops 3000000000 | tf_op jit(solution)/shard_map/far_next/pallas_call | solution.py:520
  35.1 2.8 %collective-permute-start.13 = (f16[136,256]{1,0:T(8,128)(2,1)S(1)}, f16[136,256]{1,0:T(8,128)(2,1)S(1)}, u32[]{:S(2)}, u32[]{:S(2)}) collective-permute-start(f16[136,256]{1,0:T(8,128)(2,1)S(1)} %convert_element_type.74), channel_id=1, source_target_pairs={{0,3},{1,2},{2,1},{3,0},{4,7},{5,6},{6,5},{7,4},{8,11},{9,10},{10,... | collective-permute-start | bytes 208904 | tf_op jit(solution)/shard_map/ppermute | solution.py:404
  37.9 0.1 collective-permute-start.12
  38.0 1.7 %collective-permute-start.11 = (f16[136,256]{1,0:T(8,128)(2,1)S(1)}, f16[136,256]{1,0:T(8,128)(2,1)S(1)}, u32[]{:S(2)}, u32[]{:S(2)}) collective-permute-start(f16[136,256]{1,0:T(8,128)(2,1)S(1)} %convert_element_type.70), channel_id=1, source_target_pairs={{0,1},{1,0},{2,3},{3,2},{4,5},{5,4},{6,7},{7,6},{8,9},{9,8},{10,11... | collective-permute-start | bytes 208904 | tf_op jit(solution)/shard_map/ppermute | solution.py:404
  39.8 2.8 %collective-permute-start.19 = (f16[136,256]{1,0:T(8,128)(2,1)S(1)}, f16[136,256]{1,0:T(8,128)(2,1)S(1)}, u32[]{:S(2)}, u32[]{:S(2)}) collective-permute-start(f16[136,256]{1,0:T(8,128)(2,1)S(1)} %convert_element_type.80), channel_id=1, source_target_pairs={{0,3},{1,2},{2,1},{3,0},{4,7},{5,6},{6,5},{7,4},{8,11},{9,10},{10,... | collective-permute-start | bytes 208904 | tf_op jit(solution)/shard_map/ppermute | solution.py:404
  42.5 1.7 %collective-permute-start.17 = (f16[136,256]{1,0:T(8,128)(2,1)S(1)}, f16[136,256]{1,0:T(8,128)(2,1)S(1)}, u32[]{:S(2)}, u32[]{:S(2)}) collective-permute-start(f16[136,256]{1,0:T(8,128)(2,1)S(1)} %convert_element_type.80), channel_id=1, source_target_pairs={{0,1},{1,0},{2,3},{3,2},{4,5},{5,4},{6,7},{7,6},{8,9},{9,8},{10,11... | collective-permute-start | bytes 208904 | tf_op jit(solution)/shard_map/ppermute | solution.py:404
  44.3 0.6 %collective-permute-done.11 = f16[136,256]{1,0:T(8,128)(2,1)S(1)} collective-permute-done((f16[136,256]{1,0:T(8,128)(2,1)S(1)}, f16[136,256]{1,0:T(8,128)(2,1)S(1)}, u32[]{:S(2)}, u32[]{:S(2)}) %collective-permute-start.11) | collective-permute-done | bytes 69664 | tf_op jit(solution)/shard_map/ppermute | solution.py:404
  44.9 2.4 %solve.3 = (f32[128,256]{1,0:T(8,128)S(1)}, f32[136,256]{1,0:T(8,128)S(1)}) custom-call(f32[136,256]{1,0:T(8,128)S(1)} %get-tuple-element.58.refs_0_, f32[136,256]{1,0:T(8,128)S(1)} %convert_element_type.71.refs_1_, f32[136,256]{1,0:T(8,128)S(1)} %convert_element_type.73.refs_2_, f32[136,256]{1,0:T(8,128)S(1)} %convert_element_type.75.refs_3_, ...), custom_call_target="tpu_custom_call" | custom-call | flops 3000000000 | tf_op jit(solution)/shard_map/solve/pallas_call | solution.py:436
  47.4 2.8 %collective-permute-start.16 = (f16[136,256]{1,0:T(8,128)(2,1)S(1)}, f16[136,256]{1,0:T(8,128)(2,1)S(1)}, u32[]{:S(2)}, u32[]{:S(2)}) collective-permute-start(f16[136,256]{1,0:T(8,128)(2,1)S(1)} %convert_element_type.76), channel_id=1, source_target_pairs={{0,3},{1,2},{2,1},{3,0},{4,7},{5,6},{6,5},{7,4},{8,11},{9,10},{10,... | collective-permute-start | bytes 208904 | tf_op jit(solution)/shard_map/ppermute | solution.py:404
  50.2 1.6 %collective-permute-start.14 = (f16[136,256]{1,0:T(8,128)(2,1)S(1)}, f16[136,256]{1,0:T(8,128)(2,1)S(1)}, u32[]{:S(2)}, u32[]{:S(2)}) collective-permute-start(f16[136,256]{1,0:T(8,128)(2,1)S(1)} %convert_element_type.76), channel_id=1, source_target_pairs={{0,1},{1,0},{2,3},{3,2},{4,5},{5,4},{6,7},{7,6},{8,9},{9,8},{10,11... | collective-permute-start | bytes 208904 | tf_op jit(solution)/shard_map/ppermute | solution.py:404
  51.9 0.9 %spread.2.refs_3_ = f32[128,8,256]{2,1,0:T(8,128)} custom-call(f32[128,256]{1,0:T(8,128)S(1)} %get-tuple-element.65.own, f32[136,256]{1,0:T(8,128)S(1)} %convert_element_type.81.refs_0_, f32[136,256]{1,0:T(8,128)S(1)} %convert_element_type.82.refs_1_, f32[136,256]{1,0:T(8,128)S(1)} %convert_element_type.83.refs_2_), custom_call_target="tpu_custom_call" | custom-call | tf_op jit(solution)/shard_map/spread/pallas_call | solution.py:448
  52.8 1.5 %collective-permute-done.16 = f16[136,256]{1,0:T(8,128)(2,1)S(1)} collective-permute-done((f16[136,256]{1,0:T(8,128)(2,1)S(1)}, f16[136,256]{1,0:T(8,128)(2,1)S(1)}, u32[]{:S(2)}, u32[]{:S(2)}) %collective-permute-start.16) | collective-permute-done | bytes 69664 | tf_op jit(solution)/shard_map/ppermute | solution.py:404
  54.3 2.4 %collective-permute-done.15 = f16[136,256]{1,0:T(8,128)(2,1)S(1)} collective-permute-done((f16[136,256]{1,0:T(8,128)(2,1)S(1)}, f16[136,256]{1,0:T(8,128)(2,1)S(1)}, u32[]{:S(2)}, u32[]{:S(2)}) %collective-permute-start.15) | collective-permute-done | bytes 69664 | tf_op jit(solution)/shard_map/ppermute | solution.py:404
  56.8 0.9 %spread.3 = f32[128,8,256]{2,1,0:T(8,128)} custom-call(f32[128,256]{1,0:T(8,128)S(1)} %get-tuple-element.63.own, f32[136,256]{1,0:T(8,128)S(1)} %convert_element_type.77.refs_0_, f32[136,256]{1,0:T(8,128)S(1)} %convert_element_type.78.refs_1_, f32[136,256]{1,0:T(8,128)S(1)} %convert_element_type.79.refs_2_, ...), custom_call_target="tpu_custom_call", output_to_operand_aliasing={{}: (4, {})} | custom-call | tf_op jit(solution)/shard_map/spread/pallas_call | solution.py:448
  (51 shorter events, 0.4 us)
Async XLA Ops:
  0.0 9.4 %copy-start = (bf16[128,8,256]{2,1,0:T(8,128)(2,1)S(1)}, bf16[128,8,256]{2,1,0:T(8,128)(2,1)}, u32[]{:S(2)}) copy-start(bf16[128,8,256]{2,1,0:T(8,128)(2,1)} %param.7) | copy-start | bytes 1572868
  0.7 0.7 %copy-start.4 = (s32[1,1,12]{2,1,0:T(1,128)S(1)}, s32[1,1,12]{2,1,0:T(1,128)}, u32[]{:S(2)}) copy-start(s32[1,1,12]{2,1,0:T(1,128)} %offsets.3) | copy-start | bytes 148
  1.4 8.2 %copy-start.2 = (f32[2,256,256]{2,1,0:T(8,128)S(1)}, f32[2,256,256]{2,1,0:T(8,128)}, u32[]{:S(2)}) copy-start(f32[2,256,256]{2,1,0:T(8,128)} %couplings.1) | copy-start | bytes 1572868
  1.4 8.2 %copy-start.3 = (f32[256,256]{1,0:T(8,128)S(1)}, f32[256,256]{1,0:T(8,128)}, u32[]{:S(2)}) copy-start(f32[256,256]{1,0:T(8,128)} %inverse.1) | copy-start | bytes 786436
  3.5 10.4 %collective-permute-start.2 = (f16[136,256]{1,0:T(8,128)(2,1)S(1)}, f16[136,256]{1,0:T(8,128)(2,1)S(1)}, u32[]{:S(2)}, u32[]{:S(2)}) collective-permute-start(f16[136,256]{1,0:T(8,128)(2,1)S(1)} %convert_element_type.68), channel_id=1, source_target_pairs={{0,3},{1,2},{2,1},{3,0},{4,7},{5,6},{6,5},{7,4},{8,11},{9,10},{10,... | collective-permute-start | bytes 208904 | tf_op jit(solution)/shard_map/ppermute | solution.py:404
  8.6 6.3 %collective-permute-start.1 = (f16[136,256]{1,0:T(8,128)(2,1)S(1)}, f16[136,256]{1,0:T(8,128)(2,1)S(1)}, u32[]{:S(2)}, u32[]{:S(2)}) collective-permute-start(f16[136,256]{1,0:T(8,128)(2,1)S(1)} %convert_element_type.66), channel_id=1, source_target_pairs={{0,2},{1,3},{2,0},{3,1},{4,6},{5,7},{6,4},{7,5},{8,10},{9,11},{10,... | collective-permute-start | bytes 208904 | tf_op jit(solution)/shard_map/ppermute | solution.py:404
  8.7 6.4 %collective-permute-start = (f16[136,256]{1,0:T(8,128)(2,1)S(1)}, f16[136,256]{1,0:T(8,128)(2,1)S(1)}, u32[]{:S(2)}, u32[]{:S(2)}) collective-permute-start(f16[136,256]{1,0:T(8,128)(2,1)S(1)} %convert_element_type.64), channel_id=1, source_target_pairs={{0,1},{1,0},{2,3},{3,2},{4,5},{5,4},{6,7},{7,6},{8,9},{9,8},{10,11... | collective-permute-start | bytes 208904 | tf_op jit(solution)/shard_map/ppermute | solution.py:404
  15.2 18.1 %copy-start.1 = (bf16[8,512,256]{2,1,0:T(8,128)(2,1)S(1)}, bf16[8,512,256]{2,1,0:T(8,128)(2,1)}, u32[]{:S(2)}) copy-start(bf16[8,512,256]{2,1,0:T(8,128)(2,1)} %kernels.3) | copy-start | bytes 6291460
  15.2 18.1 %copy-start.5 = (s32[1,1,12]{2,1,0:T(1,128)S(1)}, s32[1,1,12]{2,1,0:T(1,128)}, u32[]{:S(2)}) copy-start(s32[1,1,12]{2,1,0:T(1,128)} %offsets.3) | copy-start | bytes 148
  17.7 6.2 %collective-permute-start.3 = (bf16[128,256]{1,0:T(8,128)(2,1)S(1)}, bf16[128,256]{1,0:T(8,128)(2,1)S(1)}, u32[]{:S(2)}, u32[]{:S(2)}) collective-permute-start(bf16[128,256]{1,0:T(8,128)(2,1)S(1)} %get-tuple-element.57), channel_id=1, source_target_pairs={{0,24},{1,16},{2,8},{3,0},{4,28},{5,20},{6,12},{7,4},{8,1},{9,17},... | collective-permute-start | bytes 196616 | tf_op jit(solution)/shard_map/ppermute | solution.py:502
  23.9 5.3 %collective-permute-start.6 = (bf16[128,256]{1,0:T(8,128)(2,1)S(1)}, bf16[128,256]{1,0:T(8,128)(2,1)S(1)}, u32[]{:S(2)}, u32[]{:S(2)}) collective-permute-start(bf16[128,256]{1,0:T(8,128)(2,1)S(1)} %collective-permute-done.3.refs_0_), channel_id=1, source_target_pairs={{0,24},{4,28},{8,16},{12,20},{16,8},{20,12},{24,0},{28,4},{1,25},{... | collective-permute-start | bytes 196616 | tf_op jit(solution)/shard_map/ppermute | solution.py:511
  25.8 4.5 %collective-permute-start.5 = (bf16[128,256]{1,0:T(8,128)(2,1)S(1)}, bf16[128,256]{1,0:T(8,128)(2,1)S(1)}, u32[]{:S(2)}, u32[]{:S(2)}) collective-permute-start(bf16[128,256]{1,0:T(8,128)(2,1)S(1)} %collective-permute-done.3.refs_0_), channel_id=1, source_target_pairs={{0,16},{4,20},{8,24},{12,28},{16,0},{20,4},{24,8},{28,12},{1,17},{... | collective-permute-start | bytes 196616 | tf_op jit(solution)/shard_map/ppermute | solution.py:511
  27.8 4.3 %collective-permute-start.4 = (bf16[128,256]{1,0:T(8,128)(2,1)S(1)}, bf16[128,256]{1,0:T(8,128)(2,1)S(1)}, u32[]{:S(2)}, u32[]{:S(2)}) collective-permute-start(bf16[128,256]{1,0:T(8,128)(2,1)S(1)} %collective-permute-done.3.refs_0_), channel_id=1, source_target_pairs={{0,8},{4,12},{8,0},{12,4},{16,24},{20,28},{24,16},{28,20},{1,9},{5... | collective-permute-start | bytes 196616 | tf_op jit(solution)/shard_map/ppermute | solution.py:511
  28.4 3.6 %collective-permute-start.7 = (bf16[128,256]{1,0:T(8,128)(2,1)S(1)}, bf16[128,256]{1,0:T(8,128)(2,1)S(1)}, u32[]{:S(2)}, u32[]{:S(2)}) collective-permute-start(bf16[128,256]{1,0:T(8,128)(2,1)S(1)} %collective-permute-done.3.refs_0_), channel_id=1, source_target_pairs={{0,4},{4,0},{8,12},{12,8},{16,20},{20,16},{24,28},{28,24},{1,5},{5... | collective-permute-start | bytes 196616 | tf_op jit(solution)/shard_map/ppermute | solution.py:519
  29.2 2.9 %collective-permute-start.10 = (bf16[128,256]{1,0:T(8,128)(2,1)S(1)}, bf16[128,256]{1,0:T(8,128)(2,1)S(1)}, u32[]{:S(2)}, u32[]{:S(2)}) collective-permute-start(bf16[128,256]{1,0:T(8,128)(2,1)S(1)} %collective-permute-done.6.refs_3_), channel_id=1, source_target_pairs={{0,4},{4,0},{8,12},{12,8},{16,20},{20,16},{24,28},{28,24},{1,5},{5... | collective-permute-start | bytes 196616 | tf_op jit(solution)/shard_map/ppermute | solution.py:519
  30.3 1.8 %collective-permute-start.9 = (bf16[128,256]{1,0:T(8,128)(2,1)S(1)}, bf16[128,256]{1,0:T(8,128)(2,1)S(1)}, u32[]{:S(2)}, u32[]{:S(2)}) collective-permute-start(bf16[128,256]{1,0:T(8,128)(2,1)S(1)} %collective-permute-done.5.refs_2_), channel_id=1, source_target_pairs={{0,4},{4,0},{8,12},{12,8},{16,20},{20,16},{24,28},{28,24},{1,5},{5... | collective-permute-start | bytes 196616 | tf_op jit(solution)/shard_map/ppermute | solution.py:519
  32.0 1.3 %collective-permute-start.8 = (bf16[128,256]{1,0:T(8,128)(2,1)S(1)}, bf16[128,256]{1,0:T(8,128)(2,1)S(1)}, u32[]{:S(2)}, u32[]{:S(2)}) collective-permute-start(bf16[128,256]{1,0:T(8,128)(2,1)S(1)} %collective-permute-done.4.refs_1_), channel_id=1, source_target_pairs={{0,4},{4,0},{8,12},{12,8},{16,20},{20,16},{24,28},{28,24},{1,5},{5... | collective-permute-start | bytes 196616 | tf_op jit(solution)/shard_map/ppermute | solution.py:519
  35.1 7.4 %collective-permute-start.13 = (f16[136,256]{1,0:T(8,128)(2,1)S(1)}, f16[136,256]{1,0:T(8,128)(2,1)S(1)}, u32[]{:S(2)}, u32[]{:S(2)}) collective-permute-start(f16[136,256]{1,0:T(8,128)(2,1)S(1)} %convert_element_type.74), channel_id=1, source_target_pairs={{0,3},{1,2},{2,1},{3,0},{4,7},{5,6},{6,5},{7,4},{8,11},{9,10},{10,... | collective-permute-start | bytes 208904 | tf_op jit(solution)/shard_map/ppermute | solution.py:404
  37.9 6.4 %collective-permute-start.12 = (f16[136,256]{1,0:T(8,128)(2,1)S(1)}, f16[136,256]{1,0:T(8,128)(2,1)S(1)}, u32[]{:S(2)}, u32[]{:S(2)}) collective-permute-start(f16[136,256]{1,0:T(8,128)(2,1)S(1)} %convert_element_type.72), channel_id=1, source_target_pairs={{0,2},{1,3},{2,0},{3,1},{4,6},{5,7},{6,4},{7,5},{8,10},{9,11},{10,... | collective-permute-start | bytes 208904 | tf_op jit(solution)/shard_map/ppermute | solution.py:404
  38.0 6.9 %collective-permute-start.11 = (f16[136,256]{1,0:T(8,128)(2,1)S(1)}, f16[136,256]{1,0:T(8,128)(2,1)S(1)}, u32[]{:S(2)}, u32[]{:S(2)}) collective-permute-start(f16[136,256]{1,0:T(8,128)(2,1)S(1)} %convert_element_type.70), channel_id=1, source_target_pairs={{0,1},{1,0},{2,3},{3,2},{4,5},{5,4},{6,7},{7,6},{8,9},{9,8},{10,11... | collective-permute-start | bytes 208904 | tf_op jit(solution)/shard_map/ppermute | solution.py:404
  39.8 10.4 %collective-permute-start.19 = (f16[136,256]{1,0:T(8,128)(2,1)S(1)}, f16[136,256]{1,0:T(8,128)(2,1)S(1)}, u32[]{:S(2)}, u32[]{:S(2)}) collective-permute-start(f16[136,256]{1,0:T(8,128)(2,1)S(1)} %convert_element_type.80), channel_id=1, source_target_pairs={{0,3},{1,2},{2,1},{3,0},{4,7},{5,6},{6,5},{7,4},{8,11},{9,10},{10,... | collective-permute-start | bytes 208904 | tf_op jit(solution)/shard_map/ppermute | solution.py:404
  42.5 9.3 %collective-permute-start.18 = (f16[136,256]{1,0:T(8,128)(2,1)S(1)}, f16[136,256]{1,0:T(8,128)(2,1)S(1)}, u32[]{:S(2)}, u32[]{:S(2)}) collective-permute-start(f16[136,256]{1,0:T(8,128)(2,1)S(1)} %convert_element_type.80), channel_id=1, source_target_pairs={{0,2},{1,3},{2,0},{3,1},{4,6},{5,7},{6,4},{7,5},{8,10},{9,11},{10,... | collective-permute-start | bytes 208904 | tf_op jit(solution)/shard_map/ppermute | solution.py:404
  42.5 9.3 %collective-permute-start.17 = (f16[136,256]{1,0:T(8,128)(2,1)S(1)}, f16[136,256]{1,0:T(8,128)(2,1)S(1)}, u32[]{:S(2)}, u32[]{:S(2)}) collective-permute-start(f16[136,256]{1,0:T(8,128)(2,1)S(1)} %convert_element_type.80), channel_id=1, source_target_pairs={{0,1},{1,0},{2,3},{3,2},{4,5},{5,4},{6,7},{7,6},{8,9},{9,8},{10,11... | collective-permute-start | bytes 208904 | tf_op jit(solution)/shard_map/ppermute | solution.py:404
  47.4 6.9 %collective-permute-start.16 = (f16[136,256]{1,0:T(8,128)(2,1)S(1)}, f16[136,256]{1,0:T(8,128)(2,1)S(1)}, u32[]{:S(2)}, u32[]{:S(2)}) collective-permute-start(f16[136,256]{1,0:T(8,128)(2,1)S(1)} %convert_element_type.76), channel_id=1, source_target_pairs={{0,3},{1,2},{2,1},{3,0},{4,7},{5,6},{6,5},{7,4},{8,11},{9,10},{10,... | collective-permute-start | bytes 208904 | tf_op jit(solution)/shard_map/ppermute | solution.py:404
  50.2 6.5 %collective-permute-start.15 = (f16[136,256]{1,0:T(8,128)(2,1)S(1)}, f16[136,256]{1,0:T(8,128)(2,1)S(1)}, u32[]{:S(2)}, u32[]{:S(2)}) collective-permute-start(f16[136,256]{1,0:T(8,128)(2,1)S(1)} %convert_element_type.76), channel_id=1, source_target_pairs={{0,2},{1,3},{2,0},{3,1},{4,6},{5,7},{6,4},{7,5},{8,10},{9,11},{10,... | collective-permute-start | bytes 208904 | tf_op jit(solution)/shard_map/ppermute | solution.py:404
  50.2 6.6 %collective-permute-start.14 = (f16[136,256]{1,0:T(8,128)(2,1)S(1)}, f16[136,256]{1,0:T(8,128)(2,1)S(1)}, u32[]{:S(2)}, u32[]{:S(2)}) collective-permute-start(f16[136,256]{1,0:T(8,128)(2,1)S(1)} %convert_element_type.76), channel_id=1, source_target_pairs={{0,1},{1,0},{2,3},{3,2},{4,5},{5,4},{6,7},{7,6},{8,9},{9,8},{10,11... | collective-permute-start | bytes 208904 | tf_op jit(solution)/shard_map/ppermute | solution.py:404

commit v6 on v5

--- a/solution.py
+++ b/solution.py
@@ -85,7 +85,7 @@
         matrix = kernels[pl.ds(first, together)].reshape(together * columns, -1)
         product = jnp.dot(windows, matrix, preferred_element_type=F32)
         for group in range(total.shape[0]):
-            total[group] += product[:, group * LANES : (group + 1) * LANES]
+            total[group, : steps * loads] += product[:, group * LANES : (group + 1) * LANES]
 
     done = 0
     together = 1 << (kernels.shape[0].bit_length() - 1)
@@ -103,7 +103,7 @@
 
 def write_chunks(total, outs, share, loads, row):
     groups, size, _ = total.shape
-    steps = size // loads
+    steps = size // loads - 1
     source, sources = lax.axis_index("src"), len(outs)
     for index, out in enumerate(outs):
         first = partner(source, index, sources) * share % loads
@@ -203,7 +203,7 @@
                     ].astype(F32)
     for group in range(columns // LANES):
         history[span:, :, group * LANES : (group + 1) * LANES] = (
-            strided[group].reshape(steps, loads, LANES).astype(BF16)
+            strided[group, : steps * loads].reshape(steps, loads, LANES).astype(BF16)
         )
     sum_slots(counts, offsets, history, kernels, total, span)
     write_chunks(total, outs, share, loads, share * steps)
@@ -332,10 +332,11 @@
 def spread_kernel(block, share, own, *refs):
     (*chunks, out, ready, sems) = refs
     groups, steps, loads, _ = ready.shape
+    rows_of = ready.reshape(groups, steps * loads, LANES)
+    steps -= 1
     sources = (len(chunks) + 1) if block == 0 else len(chunks)
     size = share * steps
     source = lax.axis_index("src")
-    rows_of = ready.reshape(groups, steps * loads, LANES)
     copies = []
     for group in range(groups):
         lanes = slice(group * LANES, (group + 1) * LANES)
@@ -350,7 +351,7 @@
                 ]
         copies.append(
             pltpu.make_async_copy(
-                ready.at[group],
+                ready.at[group, pl.ds(0, steps)],
                 out.at[pl.ds(block * steps, steps), :, pl.ds(group * LANES, LANES)],
                 sems.at[group],
             )
@@ -451,7 +452,7 @@
             in_specs=[VMEM] * sources + [HBM] * len(last),
             out_specs=HBM,
             scratch_shapes=[
-                pltpu.VMEM((groups, steps, loads, LANES), F32),
+                pltpu.VMEM((groups, steps + 1, loads, LANES), F32),
                 pltpu.SemaphoreType.DMA((groups,)),
             ],
             input_output_aliases={sources: 0} if last else {},
@@ -463,7 +464,7 @@
     own_incident = own_incident.reshape(blocks, steps, share, rows)
     own_incident = own_incident.transpose(0, 2, 1, 3).reshape(blocks, size, rows)
 
-    total_scratch = pltpu.VMEM((groups, steps * loads, LANES), F32)
+    total_scratch = pltpu.VMEM((groups, (steps + 1) * loads, LANES), F32)
     history_scratch = pltpu.VMEM((span + steps, loads, columns), BF16)
 
     *partials, tail = pl.pallas_call(
@@ -524,7 +525,7 @@
                 out_specs=[VMEM] * sources,
                 scratch_shapes=[
                     total_scratch,
-                    pltpu.VMEM((columns // LANES, steps * loads, LANES), F32),
+                    pltpu.VMEM((columns // LANES, (steps + 1) * loads, LANES), F32),
                     history_scratch,
                 ],
                 compiler_params=params(12),

time: 57.8 us -> 58.6 us (1.014)
  starting transfers between devices: 26.5 us -> 25.9 us
  waiting for transfers between devices: 14.2 us -> 14.8 us
  Pallas kernels: 15 us -> 15.6 us
  transfers between devices with their start and end apart: 20 -> 20, of which waited for: 11 -> 9; matrix products, arithmetic and copies ran while one was open for 1% -> 1% of each run, Pallas kernels for 13% -> 13%
where the time goes in v6:
time: 58.6 us; the launch traced here: 58.7 us
  starting transfers between devices  25.9 us (44%)
  Pallas kernels  15.6 us (27%)
  waiting for transfers between devices  14.8 us (25%)
  between operations  1.19 us (2%)
  local copies, waits for them, and re-layouts  0.84 us (1%)
    ppermute x12, starting transfers between devices, trade(): return lax.ppermute(value, 'src', pairs)  19.3 us
    ppermute x12, waiting for transfers between devices, trade(): return lax.ppermute(value, 'src', pairs)  6.09 us
    pallas_call x2, Pallas kernels, solve(): pl.pallas_call(functools.partial(solve_kernel, steps, share, levels, len(...  4.84 us
    pallas_call x1, Pallas kernels, local(): pl.pallas_call(functools.partial(prepare_kernel, levels), out_shape=[jax....  4.36 us
    ppermute x3, starting transfers between devices, local(): arrived.append(lax.ppermute(landed, 'tgt', pairs))  4.23 us
    ppermute x3, waiting for transfers between devices, local(): arrived.append(lax.ppermute(landed, 'tgt', pairs))  3.75 us
    ppermute x1, waiting for transfers between devices, local(): landed = lax.ppermute(rounded, ('tgt', 'src'), moves)  3.74 us
    pallas_call x1, Pallas kernels, local(): pl.pallas_call(functools.partial(far_first_kernel, span, count, share, so...  2.55 us
  transfers between devices with their start and end apart: 20, of which 9 were waited for; matrix products, arithmetic and copies ran while one was open for 1% of the time, Pallas kernels for 13%

profile of v6, /device:TPU:0, one launch (start us, length us, event | category | flops | bytes accessed | tf_op | source)
XLA Modules:
  0.0 58.7 jit_solution(10520237215337556651)
XLA Ops:
  0.7 0.6 %copy-done.4 = s32[1,1,12]{2,1,0:T(1,128)S(1)} copy-done((s32[1,1,12]{2,1,0:T(1,128)S(1)}, s32[1,1,12]{2,1,0:T(1,128)}, u32[]{:S(2)}) %copy-start.4) | copy-done | bytes 72
  1.4 2.5 %far_first.1 = (f32[136,256]{1,0:T(8,128)S(1)}, f32[136,256]{1,0:T(8,128)S(1)}, f32[136,256]{1,0:T(8,128)S(1)}, f32[136,256]{1,0:T(8,128)S(1)}, bf16[12,8,512]{2,1,0:T(8,128)(2,1)S(1)}) custom-call(s32[1,1]{1,0:T(1,128)S(6)} %copy.12.counts, s32[1,1,12]{2,1,0:T(1,128)S(1)} %copy-done.4, bf16[76,8,512]{2,1,0:T(8,128)(2,1)} %past.1, bf16[8,512,256]{2,1,0:T(8,128)(2,1)} %kernels.3), custom_call_target="tpu_custom_call" | custom-call | flops 2000000000 | tf_op jit(solution)/shard_map/far_first/pallas_call | solution.py:470
  4.0 5.1 %collective-permute-start.2 = (f16[136,256]{1,0:T(8,128)(2,1)S(1)}, f16[136,256]{1,0:T(8,128)(2,1)S(1)}, u32[]{:S(2)}, u32[]{:S(2)}) collective-permute-start(f16[136,256]{1,0:T(8,128)(2,1)S(1)} %convert_element_type.68), channel_id=1, source_target_pairs={{0,3},{1,2},{2,1},{3,0},{4,7},{5,6},{6,5},{7,4},{8,11},{9,10},{10,... | collective-permute-start | bytes 208904 | tf_op jit(solution)/shard_map/ppermute | solution.py:405
  9.1 0.1 collective-permute-start.1
  9.2 0.6 %collective-permute-start = (f16[136,256]{1,0:T(8,128)(2,1)S(1)}, f16[136,256]{1,0:T(8,128)(2,1)S(1)}, u32[]{:S(2)}, u32[]{:S(2)}) collective-permute-start(f16[136,256]{1,0:T(8,128)(2,1)S(1)} %convert_element_type.64), channel_id=1, source_target_pairs={{0,1},{1,0},{2,3},{3,2},{4,5},{5,4},{6,7},{7,6},{8,9},{9,8},{10,11... | collective-permute-start | bytes 208904 | tf_op jit(solution)/shard_map/ppermute | solution.py:405
  9.8 0.1 constant_dynamic-slice_fusion
  10.0 4.4 %prepare.1 = (bf16[256,256]{1,0:T(8,128)(2,1)S(1)}, bf16[256,256]{1,0:T(8,128)(2,1)S(1)}, bf16[2,256,256]{2,1,0:T(8,128)(2,1)S(1)}, bf16[2,256,256]{2,1,0:T(8,12...) custom-call(f32[2,256,256]{2,1,0:T(8,128)S(1)} %copy-done.2, ...), custom_call_target="tpu_custom_call" | custom-call | flops 5000000000 | tf_op jit(solution)/shard_map/prepare/pallas_call | solution.py:413
  14.4 0.6 %collective-permute-done.1 = f16[136,256]{1,0:T(8,128)(2,1)S(1)} collective-permute-done((f16[136,256]{1,0:T(8,128)(2,1)S(1)}, f16[136,256]{1,0:T(8,128)(2,1)S(1)}, u32[]{:S(2)}, u32[]{:S(2)}) %collective-permute-start.1) | collective-permute-done | bytes 69664 | tf_op jit(solution)/shard_map/ppermute | solution.py:405
  15.1 2.4 %solve.2 = (f32[128,256]{1,0:T(8,128)S(1)}, f32[136,256]{1,0:T(8,128)S(1)}, bf16[128,256]{1,0:T(8,128)(2,1)S(1)}, f32[8,256]{1,0:T(8,128)S(1)}) custom-call(f32[136,256]{1,0:T(8,128)S(1)} %get-tuple-element.37.refs_0_, f32[136,256]{1,0:T(8,128)S(1)} %convert_element_type.65.refs_1_, f32[136,256]{1,0:T(8,128)S(1)} %convert_element_type.67.refs_2_, ...), custom_call_target="tpu_custom_call" | custom-call | flops 3000000000 | tf_op jit(solution)/shard_map/solve/pallas_call | solution.py:437
  17.5 2.4 %collective-permute-start.3 = (bf16[128,256]{1,0:T(8,128)(2,1)S(1)}, bf16[128,256]{1,0:T(8,128)(2,1)S(1)}, u32[]{:S(2)}, u32[]{:S(2)}) collective-permute-start(bf16[128,256]{1,0:T(8,128)(2,1)S(1)} %get-tuple-element.57), channel_id=1, source_target_pairs={{0,24},{1,16},{2,8},{3,0},{4,28},{5,20},{6,12},{7,4},{8,1},{9,17},... | collective-permute-start | bytes 196616 | tf_op jit(solution)/shard_map/ppermute | solution.py:503
  19.9 3.7 %collective-permute-done.3.refs_0_ = bf16[128,256]{1,0:T(8,128)(2,1)S(1)} collective-permute-done((bf16[128,256]{1,0:T(8,128)(2,1)S(1)}, bf16[128,256]{1,0:T(8,128)(2,1)S(1)}, u32[]{:S(2)}, u32[]{:S(2)}) %collective-permute-start.3) | collective-permute-done | bytes 65568 | tf_op jit(solution)/shard_map/ppermute | solution.py:503
  23.7 2.1 %collective-permute-start.6 = (bf16[128,256]{1,0:T(8,128)(2,1)S(1)}, bf16[128,256]{1,0:T(8,128)(2,1)S(1)}, u32[]{:S(2)}, u32[]{:S(2)}) collective-permute-start(bf16[128,256]{1,0:T(8,128)(2,1)S(1)} %collective-permute-done.3.refs_0_), channel_id=1, source_target_pairs={{0,24},{4,28},{8,16},{12,20},{16,8},{20,12},{24,0},{28,4},{1,25},{... | collective-permute-start | bytes 196616 | tf_op jit(solution)/shard_map/ppermute | solution.py:512
  25.8 1.6 %collective-permute-start.5 = (bf16[128,256]{1,0:T(8,128)(2,1)S(1)}, bf16[128,256]{1,0:T(8,128)(2,1)S(1)}, u32[]{:S(2)}, u32[]{:S(2)}) collective-permute-start(bf16[128,256]{1,0:T(8,128)(2,1)S(1)} %collective-permute-done.3.refs_0_), channel_id=1, source_target_pairs={{0,16},{4,20},{8,24},{12,28},{16,0},{20,4},{24,8},{28,12},{1,17},{... | collective-permute-start | bytes 196616 | tf_op jit(solution)/shard_map/ppermute | solution.py:512
  27.4 0.5 collective-permute-start.4
  27.9 1.0 %collective-permute-done.6.refs_3_ = bf16[128,256]{1,0:T(8,128)(2,1)S(1)} collective-permute-done((bf16[128,256]{1,0:T(8,128)(2,1)S(1)}, bf16[128,256]{1,0:T(8,128)(2,1)S(1)}, u32[]{:S(2)}, u32[]{:S(2)}) %collective-permute-start.6) | collective-permute-done | bytes 65568 | tf_op jit(solution)/shard_map/ppermute | solution.py:512
  28.9 1.1 %collective-permute-done.5.refs_2_ = bf16[128,256]{1,0:T(8,128)(2,1)S(1)} collective-permute-done((bf16[128,256]{1,0:T(8,128)(2,1)S(1)}, bf16[128,256]{1,0:T(8,128)(2,1)S(1)}, u32[]{:S(2)}, u32[]{:S(2)}) %collective-permute-start.5) | collective-permute-done | bytes 65568 | tf_op jit(solution)/shard_map/ppermute | solution.py:512
  30.0 1.6 %collective-permute-done.4.refs_1_ = bf16[128,256]{1,0:T(8,128)(2,1)S(1)} collective-permute-done((bf16[128,256]{1,0:T(8,128)(2,1)S(1)}, bf16[128,256]{1,0:T(8,128)(2,1)S(1)}, u32[]{:S(2)}, u32[]{:S(2)}) %collective-permute-start.4) | collective-permute-done | bytes 65568 | tf_op jit(solution)/shard_map/ppermute | solution.py:512
  31.7 1.2 %collective-permute-done.8.refs_5_ = bf16[128,256]{1,0:T(8,128)(2,1)S(1)} collective-permute-done((bf16[128,256]{1,0:T(8,128)(2,1)S(1)}, bf16[128,256]{1,0:T(8,128)(2,1)S(1)}, u32[]{:S(2)}, u32[]{:S(2)}) %collective-permute-start.8) | collective-permute-done | bytes 65568 | tf_op jit(solution)/shard_map/ppermute | solution.py:520
  32.9 2.1 %far_next.1 = (f32[136,256]{1,0:T(8,128)S(1)}, f32[136,256]{1,0:T(8,128)S(1)}, f32[136,256]{1,0:T(8,128)S(1)}, f32[136,256]{1,0:T(8,128)S(1)}) custom-call(s32[1,1]{1,0:T(1,128)S(6)} %copy.12.counts, s32[1,1,12]{2,1,0:T(1,128)S(1)} %copy-done.5, bf16[12,8,512]{2,1,0:T(8,128)(2,1)S(1)} %get-tuple-element.36.tail, bf16[8,512,256]{2,1,0:T(8,128)(2,1)S(1)} %copy-done.1, ...), custom_call_target="tpu_custom_call" | custom-call | flops 3000000000 | tf_op jit(solution)/shard_map/far_next/pallas_call | solution.py:521
  35.0 3.8 %collective-permute-start.13 = (f16[136,256]{1,0:T(8,128)(2,1)S(1)}, f16[136,256]{1,0:T(8,128)(2,1)S(1)}, u32[]{:S(2)}, u32[]{:S(2)}) collective-permute-start(f16[136,256]{1,0:T(8,128)(2,1)S(1)} %convert_element_type.74), channel_id=1, source_target_pairs={{0,3},{1,2},{2,1},{3,0},{4,7},{5,6},{6,5},{7,4},{8,11},{9,10},{10,... | collective-permute-start | bytes 208904 | tf_op jit(solution)/shard_map/ppermute | solution.py:405
  38.9 0.1 collective-permute-start.12
  39.0 0.7 %collective-permute-start.11 = (f16[136,256]{1,0:T(8,128)(2,1)S(1)}, f16[136,256]{1,0:T(8,128)(2,1)S(1)}, u32[]{:S(2)}, u32[]{:S(2)}) collective-permute-start(f16[136,256]{1,0:T(8,128)(2,1)S(1)} %convert_element_type.70), channel_id=1, source_target_pairs={{0,1},{1,0},{2,3},{3,2},{4,5},{5,4},{6,7},{7,6},{8,9},{9,8},{10,11... | collective-permute-start | bytes 208904 | tf_op jit(solution)/shard_map/ppermute | solution.py:405
  39.7 3.8 %collective-permute-start.19 = (f16[136,256]{1,0:T(8,128)(2,1)S(1)}, f16[136,256]{1,0:T(8,128)(2,1)S(1)}, u32[]{:S(2)}, u32[]{:S(2)}) collective-permute-start(f16[136,256]{1,0:T(8,128)(2,1)S(1)} %convert_element_type.80), channel_id=1, source_target_pairs={{0,3},{1,2},{2,1},{3,0},{4,7},{5,6},{6,5},{7,4},{8,11},{9,10},{10,... | collective-permute-start | bytes 208904 | tf_op jit(solution)/shard_map/ppermute | solution.py:405
  43.5 0.6 %collective-permute-start.17 = (f16[136,256]{1,0:T(8,128)(2,1)S(1)}, f16[136,256]{1,0:T(8,128)(2,1)S(1)}, u32[]{:S(2)}, u32[]{:S(2)}) collective-permute-start(f16[136,256]{1,0:T(8,128)(2,1)S(1)} %convert_element_type.80), channel_id=1, source_target_pairs={{0,1},{1,0},{2,3},{3,2},{4,5},{5,4},{6,7},{7,6},{8,9},{9,8},{10,11... | collective-permute-start | bytes 208904 | tf_op jit(solution)/shard_map/ppermute | solution.py:405
  44.2 2.0 %collective-permute-done.12 = f16[136,256]{1,0:T(8,128)(2,1)S(1)} collective-permute-done((f16[136,256]{1,0:T(8,128)(2,1)S(1)}, f16[136,256]{1,0:T(8,128)(2,1)S(1)}, u32[]{:S(2)}, u32[]{:S(2)}) %collective-permute-start.12) | collective-permute-done | bytes 69664 | tf_op jit(solution)/shard_map/ppermute | solution.py:405
  46.2 2.4 %solve.3 = (f32[128,256]{1,0:T(8,128)S(1)}, f32[136,256]{1,0:T(8,128)S(1)}) custom-call(f32[136,256]{1,0:T(8,128)S(1)} %get-tuple-element.58.refs_0_, f32[136,256]{1,0:T(8,128)S(1)} %convert_element_type.71.refs_1_, f32[136,256]{1,0:T(8,128)S(1)} %convert_element_type.73.refs_2_, f32[136,256]{1,0:T(8,128)S(1)} %convert_element_type.75.refs_3_, ...), custom_call_target="tpu_custom_call" | custom-call | flops 3000000000 | tf_op jit(solution)/shard_map/solve/pallas_call | solution.py:437
  48.7 2.3 %collective-permute-start.16 = (f16[136,256]{1,0:T(8,128)(2,1)S(1)}, f16[136,256]{1,0:T(8,128)(2,1)S(1)}, u32[]{:S(2)}, u32[]{:S(2)}) collective-permute-start(f16[136,256]{1,0:T(8,128)(2,1)S(1)} %convert_element_type.76), channel_id=1, source_target_pairs={{0,3},{1,2},{2,1},{3,0},{4,7},{5,6},{6,5},{7,4},{8,11},{9,10},{10,... | collective-permute-start | bytes 208904 | tf_op jit(solution)/shard_map/ppermute | solution.py:405
  51.0 2.1 %collective-permute-start.14 = (f16[136,256]{1,0:T(8,128)(2,1)S(1)}, f16[136,256]{1,0:T(8,128)(2,1)S(1)}, u32[]{:S(2)}, u32[]{:S(2)}) collective-permute-start(f16[136,256]{1,0:T(8,128)(2,1)S(1)} %convert_element_type.76), channel_id=1, source_target_pairs={{0,1},{1,0},{2,3},{3,2},{4,5},{5,4},{6,7},{7,6},{8,9},{9,8},{10,11... | collective-permute-start | bytes 208904 | tf_op jit(solution)/shard_map/ppermute | solution.py:405
  53.2 0.9 %spread.2.refs_3_ = f32[128,8,256]{2,1,0:T(8,128)} custom-call(f32[128,256]{1,0:T(8,128)S(1)} %get-tuple-element.65.own, f32[136,256]{1,0:T(8,128)S(1)} %convert_element_type.81.refs_0_, f32[136,256]{1,0:T(8,128)S(1)} %convert_element_type.82.refs_1_, f32[136,256]{1,0:T(8,128)S(1)} %convert_element_type.83.refs_2_), custom_call_target="tpu_custom_call" | custom-call | tf_op jit(solution)/shard_map/spread/pallas_call | solution.py:449
  54.1 1.3 %collective-permute-done.16 = f16[136,256]{1,0:T(8,128)(2,1)S(1)} collective-permute-done((f16[136,256]{1,0:T(8,128)(2,1)S(1)}, f16[136,256]{1,0:T(8,128)(2,1)S(1)}, u32[]{:S(2)}, u32[]{:S(2)}) %collective-permute-start.16) | collective-permute-done | bytes 69664 | tf_op jit(solution)/shard_map/ppermute | solution.py:405
  55.4 2.2 %collective-permute-done.15 = f16[136,256]{1,0:T(8,128)(2,1)S(1)} collective-permute-done((f16[136,256]{1,0:T(8,128)(2,1)S(1)}, f16[136,256]{1,0:T(8,128)(2,1)S(1)}, u32[]{:S(2)}, u32[]{:S(2)}) %collective-permute-start.15) | collective-permute-done | bytes 69664 | tf_op jit(solution)/shard_map/ppermute | solution.py:405
  57.6 0.9 %spread.3 = f32[128,8,256]{2,1,0:T(8,128)} custom-call(f32[128,256]{1,0:T(8,128)S(1)} %get-tuple-element.63.own, f32[136,256]{1,0:T(8,128)S(1)} %convert_element_type.77.refs_0_, f32[136,256]{1,0:T(8,128)S(1)} %convert_element_type.78.refs_1_, f32[136,256]{1,0:T(8,128)S(1)} %convert_element_type.79.refs_2_, ...), custom_call_target="tpu_custom_call", output_to_operand_aliasing={{}: (4, {})} | custom-call | tf_op jit(solution)/shard_map/spread/pallas_call | solution.py:449
  (51 shorter events, 0.3 us)
Async XLA Ops:
  0.0 9.8 %copy-start = (bf16[128,8,256]{2,1,0:T(8,128)(2,1)S(1)}, bf16[128,8,256]{2,1,0:T(8,128)(2,1)}, u32[]{:S(2)}) copy-start(bf16[128,8,256]{2,1,0:T(8,128)(2,1)} %param.7) | copy-start | bytes 1572868
  0.7 0.7 %copy-start.4 = (s32[1,1,12]{2,1,0:T(1,128)S(1)}, s32[1,1,12]{2,1,0:T(1,128)}, u32[]{:S(2)}) copy-start(s32[1,1,12]{2,1,0:T(1,128)} %offsets.3) | copy-start | bytes 148
  1.4 8.6 %copy-start.2 = (f32[2,256,256]{2,1,0:T(8,128)S(1)}, f32[2,256,256]{2,1,0:T(8,128)}, u32[]{:S(2)}) copy-start(f32[2,256,256]{2,1,0:T(8,128)} %couplings.1) | copy-start | bytes 1572868
  1.4 8.6 %copy-start.3 = (f32[256,256]{1,0:T(8,128)S(1)}, f32[256,256]{1,0:T(8,128)}, u32[]{:S(2)}) copy-start(f32[256,256]{1,0:T(8,128)} %inverse.1) | copy-start | bytes 786436
  4.0 10.4 %collective-permute-start.2 = (f16[136,256]{1,0:T(8,128)(2,1)S(1)}, f16[136,256]{1,0:T(8,128)(2,1)S(1)}, u32[]{:S(2)}, u32[]{:S(2)}) collective-permute-start(f16[136,256]{1,0:T(8,128)(2,1)S(1)} %convert_element_type.68), channel_id=1, source_target_pairs={{0,3},{1,2},{2,1},{3,0},{4,7},{5,6},{6,5},{7,4},{8,11},{9,10},{10,... | collective-permute-start | bytes 208904 | tf_op jit(solution)/shard_map/ppermute | solution.py:405
  9.1 5.9 %collective-permute-start.1 = (f16[136,256]{1,0:T(8,128)(2,1)S(1)}, f16[136,256]{1,0:T(8,128)(2,1)S(1)}, u32[]{:S(2)}, u32[]{:S(2)}) collective-permute-start(f16[136,256]{1,0:T(8,128)(2,1)S(1)} %convert_element_type.66), channel_id=1, source_target_pairs={{0,2},{1,3},{2,0},{3,1},{4,6},{5,7},{6,4},{7,5},{8,10},{9,11},{10,... | collective-permute-start | bytes 208904 | tf_op jit(solution)/shard_map/ppermute | solution.py:405
  9.2 5.9 %collective-permute-start = (f16[136,256]{1,0:T(8,128)(2,1)S(1)}, f16[136,256]{1,0:T(8,128)(2,1)S(1)}, u32[]{:S(2)}, u32[]{:S(2)}) collective-permute-start(f16[136,256]{1,0:T(8,128)(2,1)S(1)} %convert_element_type.64), channel_id=1, source_target_pairs={{0,1},{1,0},{2,3},{3,2},{4,5},{5,4},{6,7},{7,6},{8,9},{9,8},{10,11... | collective-permute-start | bytes 208904 | tf_op jit(solution)/shard_map/ppermute | solution.py:405
  15.1 17.8 %copy-start.1 = (bf16[8,512,256]{2,1,0:T(8,128)(2,1)S(1)}, bf16[8,512,256]{2,1,0:T(8,128)(2,1)}, u32[]{:S(2)}) copy-start(bf16[8,512,256]{2,1,0:T(8,128)(2,1)} %kernels.3) | copy-start | bytes 6291460
  15.1 17.8 %copy-start.5 = (s32[1,1,12]{2,1,0:T(1,128)S(1)}, s32[1,1,12]{2,1,0:T(1,128)}, u32[]{:S(2)}) copy-start(s32[1,1,12]{2,1,0:T(1,128)} %offsets.3) | copy-start | bytes 148
  17.5 6.1 %collective-permute-start.3 = (bf16[128,256]{1,0:T(8,128)(2,1)S(1)}, bf16[128,256]{1,0:T(8,128)(2,1)S(1)}, u32[]{:S(2)}, u32[]{:S(2)}) collective-permute-start(bf16[128,256]{1,0:T(8,128)(2,1)S(1)} %get-tuple-element.57), channel_id=1, source_target_pairs={{0,24},{1,16},{2,8},{3,0},{4,28},{5,20},{6,12},{7,4},{8,1},{9,17},... | collective-permute-start | bytes 196616 | tf_op jit(solution)/shard_map/ppermute | solution.py:503
  23.7 5.2 %collective-permute-start.6 = (bf16[128,256]{1,0:T(8,128)(2,1)S(1)}, bf16[128,256]{1,0:T(8,128)(2,1)S(1)}, u32[]{:S(2)}, u32[]{:S(2)}) collective-permute-start(bf16[128,256]{1,0:T(8,128)(2,1)S(1)} %collective-permute-done.3.refs_0_), channel_id=1, source_target_pairs={{0,24},{4,28},{8,16},{12,20},{16,8},{20,12},{24,0},{28,4},{1,25},{... | collective-permute-start | bytes 196616 | tf_op jit(solution)/shard_map/ppermute | solution.py:512
  25.8 4.3 %collective-permute-start.5 = (bf16[128,256]{1,0:T(8,128)(2,1)S(1)}, bf16[128,256]{1,0:T(8,128)(2,1)S(1)}, u32[]{:S(2)}, u32[]{:S(2)}) collective-permute-start(bf16[128,256]{1,0:T(8,128)(2,1)S(1)} %collective-permute-done.3.refs_0_), channel_id=1, source_target_pairs={{0,16},{4,20},{8,24},{12,28},{16,0},{20,4},{24,8},{28,12},{1,17},{... | collective-permute-start | bytes 196616 | tf_op jit(solution)/shard_map/ppermute | solution.py:512
  27.4 4.3 %collective-permute-start.4 = (bf16[128,256]{1,0:T(8,128)(2,1)S(1)}, bf16[128,256]{1,0:T(8,128)(2,1)S(1)}, u32[]{:S(2)}, u32[]{:S(2)}) collective-permute-start(bf16[128,256]{1,0:T(8,128)(2,1)S(1)} %collective-permute-done.3.refs_0_), channel_id=1, source_target_pairs={{0,8},{4,12},{8,0},{12,4},{16,24},{20,28},{24,16},{28,20},{1,9},{5... | collective-permute-start | bytes 196616 | tf_op jit(solution)/shard_map/ppermute | solution.py:512
  27.9 3.8 %collective-permute-start.7 = (bf16[128,256]{1,0:T(8,128)(2,1)S(1)}, bf16[128,256]{1,0:T(8,128)(2,1)S(1)}, u32[]{:S(2)}, u32[]{:S(2)}) collective-permute-start(bf16[128,256]{1,0:T(8,128)(2,1)S(1)} %collective-permute-done.3.refs_0_), channel_id=1, source_target_pairs={{0,4},{4,0},{8,12},{12,8},{16,20},{20,16},{24,28},{28,24},{1,5},{5... | collective-permute-start | bytes 196616 | tf_op jit(solution)/shard_map/ppermute | solution.py:520
  28.9 2.8 %collective-permute-start.10 = (bf16[128,256]{1,0:T(8,128)(2,1)S(1)}, bf16[128,256]{1,0:T(8,128)(2,1)S(1)}, u32[]{:S(2)}, u32[]{:S(2)}) collective-permute-start(bf16[128,256]{1,0:T(8,128)(2,1)S(1)} %collective-permute-done.6.refs_3_), channel_id=1, source_target_pairs={{0,4},{4,0},{8,12},{12,8},{16,20},{20,16},{24,28},{28,24},{1,5},{5... | collective-permute-start | bytes 196616 | tf_op jit(solution)/shard_map/ppermute | solution.py:520
  30.0 1.6 %collective-permute-start.9 = (bf16[128,256]{1,0:T(8,128)(2,1)S(1)}, bf16[128,256]{1,0:T(8,128)(2,1)S(1)}, u32[]{:S(2)}, u32[]{:S(2)}) collective-permute-start(bf16[128,256]{1,0:T(8,128)(2,1)S(1)} %collective-permute-done.5.refs_2_), channel_id=1, source_target_pairs={{0,4},{4,0},{8,12},{12,8},{16,20},{20,16},{24,28},{28,24},{1,5},{5... | collective-permute-start | bytes 196616 | tf_op jit(solution)/shard_map/ppermute | solution.py:520
  31.7 1.3 %collective-permute-start.8 = (bf16[128,256]{1,0:T(8,128)(2,1)S(1)}, bf16[128,256]{1,0:T(8,128)(2,1)S(1)}, u32[]{:S(2)}, u32[]{:S(2)}) collective-permute-start(bf16[128,256]{1,0:T(8,128)(2,1)S(1)} %collective-permute-done.4.refs_1_), channel_id=1, source_target_pairs={{0,4},{4,0},{8,12},{12,8},{16,20},{20,16},{24,28},{28,24},{1,5},{5... | collective-permute-start | bytes 196616 | tf_op jit(solution)/shard_map/ppermute | solution.py:520
  35.0 8.5 %collective-permute-start.13 = (f16[136,256]{1,0:T(8,128)(2,1)S(1)}, f16[136,256]{1,0:T(8,128)(2,1)S(1)}, u32[]{:S(2)}, u32[]{:S(2)}) collective-permute-start(f16[136,256]{1,0:T(8,128)(2,1)S(1)} %convert_element_type.74), channel_id=1, source_target_pairs={{0,3},{1,2},{2,1},{3,0},{4,7},{5,6},{6,5},{7,4},{8,11},{9,10},{10,... | collective-permute-start | bytes 208904 | tf_op jit(solution)/shard_map/ppermute | solution.py:405
  38.9 7.3 %collective-permute-start.12 = (f16[136,256]{1,0:T(8,128)(2,1)S(1)}, f16[136,256]{1,0:T(8,128)(2,1)S(1)}, u32[]{:S(2)}, u32[]{:S(2)}) collective-permute-start(f16[136,256]{1,0:T(8,128)(2,1)S(1)} %convert_element_type.72), channel_id=1, source_target_pairs={{0,2},{1,3},{2,0},{3,1},{4,6},{5,7},{6,4},{7,5},{8,10},{9,11},{10,... | collective-permute-start | bytes 208904 | tf_op jit(solution)/shard_map/ppermute | solution.py:405
  39.0 7.2 %collective-permute-start.11 = (f16[136,256]{1,0:T(8,128)(2,1)S(1)}, f16[136,256]{1,0:T(8,128)(2,1)S(1)}, u32[]{:S(2)}, u32[]{:S(2)}) collective-permute-start(f16[136,256]{1,0:T(8,128)(2,1)S(1)} %convert_element_type.70), channel_id=1, source_target_pairs={{0,1},{1,0},{2,3},{3,2},{4,5},{5,4},{6,7},{7,6},{8,9},{9,8},{10,11... | collective-permute-start | bytes 208904 | tf_op jit(solution)/shard_map/ppermute | solution.py:405
  39.7 11.3 %collective-permute-start.19 = (f16[136,256]{1,0:T(8,128)(2,1)S(1)}, f16[136,256]{1,0:T(8,128)(2,1)S(1)}, u32[]{:S(2)}, u32[]{:S(2)}) collective-permute-start(f16[136,256]{1,0:T(8,128)(2,1)S(1)} %convert_element_type.80), channel_id=1, source_target_pairs={{0,3},{1,2},{2,1},{3,0},{4,7},{5,6},{6,5},{7,4},{8,11},{9,10},{10,... | collective-permute-start | bytes 208904 | tf_op jit(solution)/shard_map/ppermute | solution.py:405
  43.5 9.7 %collective-permute-start.18 = (f16[136,256]{1,0:T(8,128)(2,1)S(1)}, f16[136,256]{1,0:T(8,128)(2,1)S(1)}, u32[]{:S(2)}, u32[]{:S(2)}) collective-permute-start(f16[136,256]{1,0:T(8,128)(2,1)S(1)} %convert_element_type.80), channel_id=1, source_target_pairs={{0,2},{1,3},{2,0},{3,1},{4,6},{5,7},{6,4},{7,5},{8,10},{9,11},{10,... | collective-permute-start | bytes 208904 | tf_op jit(solution)/shard_map/ppermute | solution.py:405
  43.5 9.7 %collective-permute-start.17 = (f16[136,256]{1,0:T(8,128)(2,1)S(1)}, f16[136,256]{1,0:T(8,128)(2,1)S(1)}, u32[]{:S(2)}, u32[]{:S(2)}) collective-permute-start(f16[136,256]{1,0:T(8,128)(2,1)S(1)} %convert_element_type.80), channel_id=1, source_target_pairs={{0,1},{1,0},{2,3},{3,2},{4,5},{5,4},{6,7},{7,6},{8,9},{9,8},{10,11... | collective-permute-start | bytes 208904 | tf_op jit(solution)/shard_map/ppermute | solution.py:405
  48.7 6.7 %collective-permute-start.16 = (f16[136,256]{1,0:T(8,128)(2,1)S(1)}, f16[136,256]{1,0:T(8,128)(2,1)S(1)}, u32[]{:S(2)}, u32[]{:S(2)}) collective-permute-start(f16[136,256]{1,0:T(8,128)(2,1)S(1)} %convert_element_type.76), channel_id=1, source_target_pairs={{0,3},{1,2},{2,1},{3,0},{4,7},{5,6},{6,5},{7,4},{8,11},{9,10},{10,... | collective-permute-start | bytes 208904 | tf_op jit(solution)/shard_map/ppermute | solution.py:405
  51.0 6.6 %collective-permute-start.15 = (f16[136,256]{1,0:T(8,128)(2,1)S(1)}, f16[136,256]{1,0:T(8,128)(2,1)S(1)}, u32[]{:S(2)}, u32[]{:S(2)}) collective-permute-start(f16[136,256]{1,0:T(8,128)(2,1)S(1)} %convert_element_type.76), channel_id=1, source_target_pairs={{0,2},{1,3},{2,0},{3,1},{4,6},{5,7},{6,4},{7,5},{8,10},{9,11},{10,... | collective-permute-start | bytes 208904 | tf_op jit(solution)/shard_map/ppermute | solution.py:405
  51.0 6.6 %collective-permute-start.14 = (f16[136,256]{1,0:T(8,128)(2,1)S(1)}, f16[136,256]{1,0:T(8,128)(2,1)S(1)}, u32[]{:S(2)}, u32[]{:S(2)}) collective-permute-start(f16[136,256]{1,0:T(8,128)(2,1)S(1)} %convert_element_type.76), channel_id=1, source_target_pairs={{0,1},{1,0},{2,3},{3,2},{4,5},{5,4},{6,7},{7,6},{8,9},{9,8},{10,11... | collective-permute-start | bytes 208904 | tf_op jit(solution)/shard_map/ppermute | solution.py:405

commit v7 on v6

--- a/solution.py
+++ b/solution.py
@@ -291,14 +291,23 @@
         pieces.append(jnp.zeros((padded - share, rows), F32))
         return jnp.concatenate(pieces, 0)
 
+    nothing = jnp.zeros((padded, rows), F32)
+    reached = [
+        jnp.concatenate(
+            [back(lag - step) if lag > step else nothing for lag in range(1, count + 1)], 1
+        )
+        for step in range(count)
+    ]
+    pull = dot3(
+        jnp.concatenate(reached, 0),
+        coupling_high[...].reshape(count * rows, rows),
+        coupling_low[...].reshape(count * rows, rows),
+    )
     for step in range(count):
-        pull = None
-        for lag in range(step + 1, count + 1):
-            term = dot3(back(lag - step), coupling_high[lag - 1], coupling_low[lag - 1])
-            pull = term if pull is None else pull + term
         for item in range(share):
+            at = step * padded + item
             adjusted = adjusted - jnp.where(
-                row_of == item * steps + step, pull[item : item + 1], 0.0
+                row_of == item * steps + step, pull[at : at + 1], 0.0
             )
     within = row_of % steps
     driven = dot3(adjusted, inverse_high[...], inverse_low[...])

time: 58.6 us -> 58 us (0.990)
  waiting for transfers between devices: 14.8 us -> 13.4 us
  starting transfers between devices: 25.9 us -> 26.8 us
    ppermute x12, waiting for transfers between devices: 6.09 us -> 4.76 us  [trade(): return lax.ppermute(value, 'src', pairs)]
    ppermute x12, starting transfers between devices: 19.3 us -> 20.1 us  [trade(): return lax.ppermute(value, 'src', pairs)]
  transfers between devices with their start and end apart: 20 -> 20, of which waited for: 9 -> 10; matrix products, arithmetic and copies ran while one was open for 1% -> 1% of each run, Pallas kernels for 13% -> 13%
where the time goes in v7:
time: 58 us; the launch traced here: 58.1 us
  starting transfers between devices  26.8 us (46%)
  Pallas kernels  15.6 us (27%)
  waiting for transfers between devices  13.4 us (23%)
  between operations  1.18 us (2%)
  local copies, waits for them, and re-layouts  0.84 us (1%)
    ppermute x12, starting transfers between devices, trade(): return lax.ppermute(value, 'src', pairs)  20.1 us
    pallas_call x2, Pallas kernels, solve(): pl.pallas_call(functools.partial(solve_kernel, steps, share, levels, len(...  4.86 us
    ppermute x12, waiting for transfers between devices, trade(): return lax.ppermute(value, 'src', pairs)  4.76 us
    ppermute x3, starting transfers between devices, local(): arrived.append(lax.ppermute(landed, 'tgt', pairs))  4.44 us
    pallas_call x1, Pallas kernels, local(): pl.pallas_call(functools.partial(prepare_kernel, levels), out_shape=[jax....  4.36 us
    ppermute x1, waiting for transfers between devices, local(): landed = lax.ppermute(rounded, ('tgt', 'src'), moves)  3.99 us
    ppermute x3, waiting for transfers between devices, local(): arrived.append(lax.ppermute(landed, 'tgt', pairs))  3.39 us
    pallas_call x1, Pallas kernels, local(): pl.pallas_call(functools.partial(far_first_kernel, span, count, share, so...  2.49 us
  transfers between devices with their start and end apart: 20, of which 10 were waited for; matrix products, arithmetic and copies ran while one was open for 1% of the time, Pallas kernels for 13%

profile of v7, /device:TPU:0, one launch (start us, length us, event | category | flops | bytes accessed | tf_op | source)
XLA Modules:
  0.0 58.1 jit_solution(888289400137641751)
XLA Ops:
  0.7 0.6 %copy-done.4 = s32[1,1,12]{2,1,0:T(1,128)S(1)} copy-done((s32[1,1,12]{2,1,0:T(1,128)S(1)}, s32[1,1,12]{2,1,0:T(1,128)}, u32[]{:S(2)}) %copy-start.4) | copy-done | bytes 72
  1.4 2.5 %far_first.1 = (f32[136,256]{1,0:T(8,128)S(1)}, f32[136,256]{1,0:T(8,128)S(1)}, f32[136,256]{1,0:T(8,128)S(1)}, f32[136,256]{1,0:T(8,128)S(1)}, bf16[12,8,512]{2,1,0:T(8,128)(2,1)S(1)}) custom-call(s32[1,1]{1,0:T(1,128)S(6)} %copy.12.counts, s32[1,1,12]{2,1,0:T(1,128)S(1)} %copy-done.4, bf16[76,8,512]{2,1,0:T(8,128)(2,1)} %past.1, bf16[8,512,256]{2,1,0:T(8,128)(2,1)} %kernels.3), custom_call_target="tpu_custom_call" | custom-call | flops 2000000000 | tf_op jit(solution)/shard_map/far_first/pallas_call | solution.py:479
  3.9 6.0 %collective-permute-start.2 = (f16[136,256]{1,0:T(8,128)(2,1)S(1)}, f16[136,256]{1,0:T(8,128)(2,1)S(1)}, u32[]{:S(2)}, u32[]{:S(2)}) collective-permute-start(f16[136,256]{1,0:T(8,128)(2,1)S(1)} %convert_element_type.68), channel_id=1, source_target_pairs={{0,3},{1,2},{2,1},{3,0},{4,7},{5,6},{6,5},{7,4},{8,11},{9,10},{10,... | collective-permute-start | bytes 208904 | tf_op jit(solution)/shard_map/ppermute | solution.py:414
  9.9 0.1 collective-permute-start.1
  10.0 0.6 %collective-permute-start = (f16[136,256]{1,0:T(8,128)(2,1)S(1)}, f16[136,256]{1,0:T(8,128)(2,1)S(1)}, u32[]{:S(2)}, u32[]{:S(2)}) collective-permute-start(f16[136,256]{1,0:T(8,128)(2,1)S(1)} %convert_element_type.64), channel_id=1, source_target_pairs={{0,1},{1,0},{2,3},{3,2},{4,5},{5,4},{6,7},{7,6},{8,9},{9,8},{10,11... | collective-permute-start | bytes 208904 | tf_op jit(solution)/shard_map/ppermute | solution.py:414
  10.6 0.1 constant_dynamic-slice_fusion
  10.8 4.4 %prepare.1 = (bf16[256,256]{1,0:T(8,128)(2,1)S(1)}, bf16[256,256]{1,0:T(8,128)(2,1)S(1)}, bf16[2,256,256]{2,1,0:T(8,128)(2,1)S(1)}, bf16[2,256,256]{2,1,0:T(8,12...) custom-call(f32[2,256,256]{2,1,0:T(8,128)S(1)} %copy-done.2, ...), custom_call_target="tpu_custom_call" | custom-call | flops 5000000000 | tf_op jit(solution)/shard_map/prepare/pallas_call | solution.py:422
  15.2 0.2 collective-permute-done.1
  15.4 0.3 collective-permute-done
  15.8 2.4 %solve.2 = (f32[128,256]{1,0:T(8,128)S(1)}, f32[136,256]{1,0:T(8,128)S(1)}, bf16[128,256]{1,0:T(8,128)(2,1)S(1)}, f32[8,256]{1,0:T(8,128)S(1)}) custom-call(f32[136,256]{1,0:T(8,128)S(1)} %get-tuple-element.37.refs_0_, f32[136,256]{1,0:T(8,128)S(1)} %convert_element_type.65.refs_1_, f32[136,256]{1,0:T(8,128)S(1)} %convert_element_type.67.refs_2_, ...), custom_call_target="tpu_custom_call" | custom-call | flops 3000000000 | tf_op jit(solution)/shard_map/solve/pallas_call | solution.py:446
  18.2 2.2 %collective-permute-start.3 = (bf16[128,256]{1,0:T(8,128)(2,1)S(1)}, bf16[128,256]{1,0:T(8,128)(2,1)S(1)}, u32[]{:S(2)}, u32[]{:S(2)}) collective-permute-start(bf16[128,256]{1,0:T(8,128)(2,1)S(1)} %get-tuple-element.57), channel_id=1, source_target_pairs={{0,24},{1,16},{2,8},{3,0},{4,28},{5,20},{6,12},{7,4},{8,1},{9,17},... | collective-permute-start | bytes 196616 | tf_op jit(solution)/shard_map/ppermute | solution.py:512
  20.5 4.0 %collective-permute-done.3.refs_0_ = bf16[128,256]{1,0:T(8,128)(2,1)S(1)} collective-permute-done((bf16[128,256]{1,0:T(8,128)(2,1)S(1)}, bf16[128,256]{1,0:T(8,128)(2,1)S(1)}, u32[]{:S(2)}, u32[]{:S(2)}) %collective-permute-start.3) | collective-permute-done | bytes 65568 | tf_op jit(solution)/shard_map/ppermute | solution.py:512
  24.4 2.1 %collective-permute-start.6 = (bf16[128,256]{1,0:T(8,128)(2,1)S(1)}, bf16[128,256]{1,0:T(8,128)(2,1)S(1)}, u32[]{:S(2)}, u32[]{:S(2)}) collective-permute-start(bf16[128,256]{1,0:T(8,128)(2,1)S(1)} %collective-permute-done.3.refs_0_), channel_id=1, source_target_pairs={{0,24},{4,28},{8,16},{12,20},{16,8},{20,12},{24,0},{28,4},{1,25},{... | collective-permute-start | bytes 196616 | tf_op jit(solution)/shard_map/ppermute | solution.py:521
  26.5 1.3 %collective-permute-start.5 = (bf16[128,256]{1,0:T(8,128)(2,1)S(1)}, bf16[128,256]{1,0:T(8,128)(2,1)S(1)}, u32[]{:S(2)}, u32[]{:S(2)}) collective-permute-start(bf16[128,256]{1,0:T(8,128)(2,1)S(1)} %collective-permute-done.3.refs_0_), channel_id=1, source_target_pairs={{0,16},{4,20},{8,24},{12,28},{16,0},{20,4},{24,8},{28,12},{1,17},{... | collective-permute-start | bytes 196616 | tf_op jit(solution)/shard_map/ppermute | solution.py:521
  27.8 1.1 %collective-permute-start.4 = (bf16[128,256]{1,0:T(8,128)(2,1)S(1)}, bf16[128,256]{1,0:T(8,128)(2,1)S(1)}, u32[]{:S(2)}, u32[]{:S(2)}) collective-permute-start(bf16[128,256]{1,0:T(8,128)(2,1)S(1)} %collective-permute-done.3.refs_0_), channel_id=1, source_target_pairs={{0,8},{4,12},{8,0},{12,4},{16,24},{20,28},{24,16},{28,20},{1,9},{5... | collective-permute-start | bytes 196616 | tf_op jit(solution)/shard_map/ppermute | solution.py:521
  28.9 0.8 %collective-permute-done.6.refs_3_ = bf16[128,256]{1,0:T(8,128)(2,1)S(1)} collective-permute-done((bf16[128,256]{1,0:T(8,128)(2,1)S(1)}, bf16[128,256]{1,0:T(8,128)(2,1)S(1)}, u32[]{:S(2)}, u32[]{:S(2)}) %collective-permute-start.6) | collective-permute-done | bytes 65568 | tf_op jit(solution)/shard_map/ppermute | solution.py:521
  29.7 1.1 %collective-permute-done.5.refs_2_ = bf16[128,256]{1,0:T(8,128)(2,1)S(1)} collective-permute-done((bf16[128,256]{1,0:T(8,128)(2,1)S(1)}, bf16[128,256]{1,0:T(8,128)(2,1)S(1)}, u32[]{:S(2)}, u32[]{:S(2)}) %collective-permute-start.5) | collective-permute-done | bytes 65568 | tf_op jit(solution)/shard_map/ppermute | solution.py:521
  30.8 1.5 %collective-permute-done.4.refs_1_ = bf16[128,256]{1,0:T(8,128)(2,1)S(1)} collective-permute-done((bf16[128,256]{1,0:T(8,128)(2,1)S(1)}, bf16[128,256]{1,0:T(8,128)(2,1)S(1)}, u32[]{:S(2)}, u32[]{:S(2)}) %collective-permute-start.4) | collective-permute-done | bytes 65568 | tf_op jit(solution)/shard_map/ppermute | solution.py:521
  32.3 1.2 %collective-permute-done.8.refs_5_ = bf16[128,256]{1,0:T(8,128)(2,1)S(1)} collective-permute-done((bf16[128,256]{1,0:T(8,128)(2,1)S(1)}, bf16[128,256]{1,0:T(8,128)(2,1)S(1)}, u32[]{:S(2)}, u32[]{:S(2)}) %collective-permute-start.8) | collective-permute-done | bytes 65568 | tf_op jit(solution)/shard_map/ppermute | solution.py:529
  33.5 2.1 %far_next.1 = (f32[136,256]{1,0:T(8,128)S(1)}, f32[136,256]{1,0:T(8,128)S(1)}, f32[136,256]{1,0:T(8,128)S(1)}, f32[136,256]{1,0:T(8,128)S(1)}) custom-call(s32[1,1]{1,0:T(1,128)S(6)} %copy.12.counts, s32[1,1,12]{2,1,0:T(1,128)S(1)} %copy-done.5, bf16[12,8,512]{2,1,0:T(8,128)(2,1)S(1)} %get-tuple-element.36.tail, bf16[8,512,256]{2,1,0:T(8,128)(2,1)S(1)} %copy-done.1, ...), custom_call_target="tpu_custom_call" | custom-call | flops 3000000000 | tf_op jit(solution)/shard_map/far_next/pallas_call | solution.py:530
  35.7 2.6 %collective-permute-start.13 = (f16[136,256]{1,0:T(8,128)(2,1)S(1)}, f16[136,256]{1,0:T(8,128)(2,1)S(1)}, u32[]{:S(2)}, u32[]{:S(2)}) collective-permute-start(f16[136,256]{1,0:T(8,128)(2,1)S(1)} %convert_element_type.74), channel_id=1, source_target_pairs={{0,3},{1,2},{2,1},{3,0},{4,7},{5,6},{6,5},{7,4},{8,11},{9,10},{10,... | collective-permute-start | bytes 208904 | tf_op jit(solution)/shard_map/ppermute | solution.py:414
  38.4 1.9 %collective-permute-start.11 = (f16[136,256]{1,0:T(8,128)(2,1)S(1)}, f16[136,256]{1,0:T(8,128)(2,1)S(1)}, u32[]{:S(2)}, u32[]{:S(2)}) collective-permute-start(f16[136,256]{1,0:T(8,128)(2,1)S(1)} %convert_element_type.70), channel_id=1, source_target_pairs={{0,1},{1,0},{2,3},{3,2},{4,5},{5,4},{6,7},{7,6},{8,9},{9,8},{10,11... | collective-permute-start | bytes 208904 | tf_op jit(solution)/shard_map/ppermute | solution.py:414
  40.3 2.6 %collective-permute-start.19 = (f16[136,256]{1,0:T(8,128)(2,1)S(1)}, f16[136,256]{1,0:T(8,128)(2,1)S(1)}, u32[]{:S(2)}, u32[]{:S(2)}) collective-permute-start(f16[136,256]{1,0:T(8,128)(2,1)S(1)} %convert_element_type.80), channel_id=1, source_target_pairs={{0,3},{1,2},{2,1},{3,0},{4,7},{5,6},{6,5},{7,4},{8,11},{9,10},{10,... | collective-permute-start | bytes 208904 | tf_op jit(solution)/shard_map/ppermute | solution.py:414
  42.9 1.9 %collective-permute-start.17 = (f16[136,256]{1,0:T(8,128)(2,1)S(1)}, f16[136,256]{1,0:T(8,128)(2,1)S(1)}, u32[]{:S(2)}, u32[]{:S(2)}) collective-permute-start(f16[136,256]{1,0:T(8,128)(2,1)S(1)} %convert_element_type.80), channel_id=1, source_target_pairs={{0,1},{1,0},{2,3},{3,2},{4,5},{5,4},{6,7},{7,6},{8,9},{9,8},{10,11... | collective-permute-start | bytes 208904 | tf_op jit(solution)/shard_map/ppermute | solution.py:414
  44.8 2.0 %collective-permute-done.12 = f16[136,256]{1,0:T(8,128)(2,1)S(1)} collective-permute-done((f16[136,256]{1,0:T(8,128)(2,1)S(1)}, f16[136,256]{1,0:T(8,128)(2,1)S(1)}, u32[]{:S(2)}, u32[]{:S(2)}) %collective-permute-start.12) | collective-permute-done | bytes 69664 | tf_op jit(solution)/shard_map/ppermute | solution.py:414
  46.8 2.4 %solve.3 = (f32[128,256]{1,0:T(8,128)S(1)}, f32[136,256]{1,0:T(8,128)S(1)}) custom-call(f32[136,256]{1,0:T(8,128)S(1)} %get-tuple-element.58.refs_0_, f32[136,256]{1,0:T(8,128)S(1)} %convert_element_type.71.refs_1_, f32[136,256]{1,0:T(8,128)S(1)} %convert_element_type.73.refs_2_, f32[136,256]{1,0:T(8,128)S(1)} %convert_element_type.75.refs_3_, ...), custom_call_target="tpu_custom_call" | custom-call | flops 3000000000 | tf_op jit(solution)/shard_map/solve/pallas_call | solution.py:446
  49.3 1.5 %collective-permute-start.16 = (f16[136,256]{1,0:T(8,128)(2,1)S(1)}, f16[136,256]{1,0:T(8,128)(2,1)S(1)}, u32[]{:S(2)}, u32[]{:S(2)}) collective-permute-start(f16[136,256]{1,0:T(8,128)(2,1)S(1)} %convert_element_type.76), channel_id=1, source_target_pairs={{0,3},{1,2},{2,1},{3,0},{4,7},{5,6},{6,5},{7,4},{8,11},{9,10},{10,... | collective-permute-start | bytes 208904 | tf_op jit(solution)/shard_map/ppermute | solution.py:414
  50.8 3.0 %collective-permute-start.14 = (f16[136,256]{1,0:T(8,128)(2,1)S(1)}, f16[136,256]{1,0:T(8,128)(2,1)S(1)}, u32[]{:S(2)}, u32[]{:S(2)}) collective-permute-start(f16[136,256]{1,0:T(8,128)(2,1)S(1)} %convert_element_type.76), channel_id=1, source_target_pairs={{0,1},{1,0},{2,3},{3,2},{4,5},{5,4},{6,7},{7,6},{8,9},{9,8},{10,11... | collective-permute-start | bytes 208904 | tf_op jit(solution)/shard_map/ppermute | solution.py:414
  53.8 0.9 %spread.2.refs_3_ = f32[128,8,256]{2,1,0:T(8,128)} custom-call(f32[128,256]{1,0:T(8,128)S(1)} %get-tuple-element.65.own, f32[136,256]{1,0:T(8,128)S(1)} %convert_element_type.81.refs_0_, f32[136,256]{1,0:T(8,128)S(1)} %convert_element_type.82.refs_1_, f32[136,256]{1,0:T(8,128)S(1)} %convert_element_type.83.refs_2_), custom_call_target="tpu_custom_call" | custom-call | tf_op jit(solution)/shard_map/spread/pallas_call | solution.py:458
  54.7 0.8 %collective-permute-done.16 = f16[136,256]{1,0:T(8,128)(2,1)S(1)} collective-permute-done((f16[136,256]{1,0:T(8,128)(2,1)S(1)}, f16[136,256]{1,0:T(8,128)(2,1)S(1)}, u32[]{:S(2)}, u32[]{:S(2)}) %collective-permute-start.16) | collective-permute-done | bytes 69664 | tf_op jit(solution)/shard_map/ppermute | solution.py:414
  55.5 1.4 %collective-permute-done.15 = f16[136,256]{1,0:T(8,128)(2,1)S(1)} collective-permute-done((f16[136,256]{1,0:T(8,128)(2,1)S(1)}, f16[136,256]{1,0:T(8,128)(2,1)S(1)}, u32[]{:S(2)}, u32[]{:S(2)}) %collective-permute-start.15) | collective-permute-done | bytes 69664 | tf_op jit(solution)/shard_map/ppermute | solution.py:414
  57.0 0.9 %spread.3 = f32[128,8,256]{2,1,0:T(8,128)} custom-call(f32[128,256]{1,0:T(8,128)S(1)} %get-tuple-element.63.own, f32[136,256]{1,0:T(8,128)S(1)} %convert_element_type.77.refs_0_, f32[136,256]{1,0:T(8,128)S(1)} %convert_element_type.78.refs_1_, f32[136,256]{1,0:T(8,128)S(1)} %convert_element_type.79.refs_2_, ...), custom_call_target="tpu_custom_call", output_to_operand_aliasing={{}: (4, {})} | custom-call | tf_op jit(solution)/shard_map/spread/pallas_call | solution.py:458
  (51 shorter events, 0.4 us)
Async XLA Ops:
  0.0 10.6 %copy-start = (bf16[128,8,256]{2,1,0:T(8,128)(2,1)S(1)}, bf16[128,8,256]{2,1,0:T(8,128)(2,1)}, u32[]{:S(2)}) copy-start(bf16[128,8,256]{2,1,0:T(8,128)(2,1)} %param.7) | copy-start | bytes 1572868
  0.7 0.7 %copy-start.4 = (s32[1,1,12]{2,1,0:T(1,128)S(1)}, s32[1,1,12]{2,1,0:T(1,128)}, u32[]{:S(2)}) copy-start(s32[1,1,12]{2,1,0:T(1,128)} %offsets.3) | copy-start | bytes 148
  1.4 9.4 %copy-start.2 = (f32[2,256,256]{2,1,0:T(8,128)S(1)}, f32[2,256,256]{2,1,0:T(8,128)}, u32[]{:S(2)}) copy-start(f32[2,256,256]{2,1,0:T(8,128)} %couplings.1) | copy-start | bytes 1572868
  1.4 9.4 %copy-start.3 = (f32[256,256]{1,0:T(8,128)S(1)}, f32[256,256]{1,0:T(8,128)}, u32[]{:S(2)}) copy-start(f32[256,256]{1,0:T(8,128)} %inverse.1) | copy-start | bytes 786436
  3.9 11.3 %collective-permute-start.2 = (f16[136,256]{1,0:T(8,128)(2,1)S(1)}, f16[136,256]{1,0:T(8,128)(2,1)S(1)}, u32[]{:S(2)}, u32[]{:S(2)}) collective-permute-start(f16[136,256]{1,0:T(8,128)(2,1)S(1)} %convert_element_type.68), channel_id=1, source_target_pairs={{0,3},{1,2},{2,1},{3,0},{4,7},{5,6},{6,5},{7,4},{8,11},{9,10},{10,... | collective-permute-start | bytes 208904 | tf_op jit(solution)/shard_map/ppermute | solution.py:414
  9.9 5.5 %collective-permute-start.1 = (f16[136,256]{1,0:T(8,128)(2,1)S(1)}, f16[136,256]{1,0:T(8,128)(2,1)S(1)}, u32[]{:S(2)}, u32[]{:S(2)}) collective-permute-start(f16[136,256]{1,0:T(8,128)(2,1)S(1)} %convert_element_type.66), channel_id=1, source_target_pairs={{0,2},{1,3},{2,0},{3,1},{4,6},{5,7},{6,4},{7,5},{8,10},{9,11},{10,... | collective-permute-start | bytes 208904 | tf_op jit(solution)/shard_map/ppermute | solution.py:414
  10.0 5.8 %collective-permute-start = (f16[136,256]{1,0:T(8,128)(2,1)S(1)}, f16[136,256]{1,0:T(8,128)(2,1)S(1)}, u32[]{:S(2)}, u32[]{:S(2)}) collective-permute-start(f16[136,256]{1,0:T(8,128)(2,1)S(1)} %convert_element_type.64), channel_id=1, source_target_pairs={{0,1},{1,0},{2,3},{3,2},{4,5},{5,4},{6,7},{7,6},{8,9},{9,8},{10,11... | collective-permute-start | bytes 208904 | tf_op jit(solution)/shard_map/ppermute | solution.py:414
  15.8 17.8 %copy-start.1 = (bf16[8,512,256]{2,1,0:T(8,128)(2,1)S(1)}, bf16[8,512,256]{2,1,0:T(8,128)(2,1)}, u32[]{:S(2)}) copy-start(bf16[8,512,256]{2,1,0:T(8,128)(2,1)} %kernels.3) | copy-start | bytes 6291460
  15.8 17.8 %copy-start.5 = (s32[1,1,12]{2,1,0:T(1,128)S(1)}, s32[1,1,12]{2,1,0:T(1,128)}, u32[]{:S(2)}) copy-start(s32[1,1,12]{2,1,0:T(1,128)} %offsets.3) | copy-start | bytes 148
  18.2 6.2 %collective-permute-start.3 = (bf16[128,256]{1,0:T(8,128)(2,1)S(1)}, bf16[128,256]{1,0:T(8,128)(2,1)S(1)}, u32[]{:S(2)}, u32[]{:S(2)}) collective-permute-start(bf16[128,256]{1,0:T(8,128)(2,1)S(1)} %get-tuple-element.57), channel_id=1, source_target_pairs={{0,24},{1,16},{2,8},{3,0},{4,28},{5,20},{6,12},{7,4},{8,1},{9,17},... | collective-permute-start | bytes 196616 | tf_op jit(solution)/shard_map/ppermute | solution.py:512
  24.4 5.3 %collective-permute-start.6 = (bf16[128,256]{1,0:T(8,128)(2,1)S(1)}, bf16[128,256]{1,0:T(8,128)(2,1)S(1)}, u32[]{:S(2)}, u32[]{:S(2)}) collective-permute-start(bf16[128,256]{1,0:T(8,128)(2,1)S(1)} %collective-permute-done.3.refs_0_), channel_id=1, source_target_pairs={{0,24},{4,28},{8,16},{12,20},{16,8},{20,12},{24,0},{28,4},{1,25},{... | collective-permute-start | bytes 196616 | tf_op jit(solution)/shard_map/ppermute | solution.py:521
  26.5 4.3 %collective-permute-start.5 = (bf16[128,256]{1,0:T(8,128)(2,1)S(1)}, bf16[128,256]{1,0:T(8,128)(2,1)S(1)}, u32[]{:S(2)}, u32[]{:S(2)}) collective-permute-start(bf16[128,256]{1,0:T(8,128)(2,1)S(1)} %collective-permute-done.3.refs_0_), channel_id=1, source_target_pairs={{0,16},{4,20},{8,24},{12,28},{16,0},{20,4},{24,8},{28,12},{1,17},{... | collective-permute-start | bytes 196616 | tf_op jit(solution)/shard_map/ppermute | solution.py:521
  27.8 4.5 %collective-permute-start.4 = (bf16[128,256]{1,0:T(8,128)(2,1)S(1)}, bf16[128,256]{1,0:T(8,128)(2,1)S(1)}, u32[]{:S(2)}, u32[]{:S(2)}) collective-permute-start(bf16[128,256]{1,0:T(8,128)(2,1)S(1)} %collective-permute-done.3.refs_0_), channel_id=1, source_target_pairs={{0,8},{4,12},{8,0},{12,4},{16,24},{20,28},{24,16},{28,20},{1,9},{5... | collective-permute-start | bytes 196616 | tf_op jit(solution)/shard_map/ppermute | solution.py:521
  28.9 3.4 %collective-permute-start.7 = (bf16[128,256]{1,0:T(8,128)(2,1)S(1)}, bf16[128,256]{1,0:T(8,128)(2,1)S(1)}, u32[]{:S(2)}, u32[]{:S(2)}) collective-permute-start(bf16[128,256]{1,0:T(8,128)(2,1)S(1)} %collective-permute-done.3.refs_0_), channel_id=1, source_target_pairs={{0,4},{4,0},{8,12},{12,8},{16,20},{20,16},{24,28},{28,24},{1,5},{5... | collective-permute-start | bytes 196616 | tf_op jit(solution)/shard_map/ppermute | solution.py:529
  29.7 2.6 %collective-permute-start.10 = (bf16[128,256]{1,0:T(8,128)(2,1)S(1)}, bf16[128,256]{1,0:T(8,128)(2,1)S(1)}, u32[]{:S(2)}, u32[]{:S(2)}) collective-permute-start(bf16[128,256]{1,0:T(8,128)(2,1)S(1)} %collective-permute-done.6.refs_3_), channel_id=1, source_target_pairs={{0,4},{4,0},{8,12},{12,8},{16,20},{20,16},{24,28},{28,24},{1,5},{5... | collective-permute-start | bytes 196616 | tf_op jit(solution)/shard_map/ppermute | solution.py:529
  30.8 1.5 %collective-permute-start.9 = (bf16[128,256]{1,0:T(8,128)(2,1)S(1)}, bf16[128,256]{1,0:T(8,128)(2,1)S(1)}, u32[]{:S(2)}, u32[]{:S(2)}) collective-permute-start(bf16[128,256]{1,0:T(8,128)(2,1)S(1)} %collective-permute-done.5.refs_2_), channel_id=1, source_target_pairs={{0,4},{4,0},{8,12},{12,8},{16,20},{20,16},{24,28},{28,24},{1,5},{5... | collective-permute-start | bytes 196616 | tf_op jit(solution)/shard_map/ppermute | solution.py:529
  32.3 1.3 %collective-permute-start.8 = (bf16[128,256]{1,0:T(8,128)(2,1)S(1)}, bf16[128,256]{1,0:T(8,128)(2,1)S(1)}, u32[]{:S(2)}, u32[]{:S(2)}) collective-permute-start(bf16[128,256]{1,0:T(8,128)(2,1)S(1)} %collective-permute-done.4.refs_1_), channel_id=1, source_target_pairs={{0,4},{4,0},{8,12},{12,8},{16,20},{20,16},{24,28},{28,24},{1,5},{5... | collective-permute-start | bytes 196616 | tf_op jit(solution)/shard_map/ppermute | solution.py:529
  35.7 7.2 %collective-permute-start.13 = (f16[136,256]{1,0:T(8,128)(2,1)S(1)}, f16[136,256]{1,0:T(8,128)(2,1)S(1)}, u32[]{:S(2)}, u32[]{:S(2)}) collective-permute-start(f16[136,256]{1,0:T(8,128)(2,1)S(1)} %convert_element_type.74), channel_id=1, source_target_pairs={{0,3},{1,2},{2,1},{3,0},{4,7},{5,6},{6,5},{7,4},{8,11},{9,10},{10,... | collective-permute-start | bytes 208904 | tf_op jit(solution)/shard_map/ppermute | solution.py:414
  38.3 8.5 %collective-permute-start.12 = (f16[136,256]{1,0:T(8,128)(2,1)S(1)}, f16[136,256]{1,0:T(8,128)(2,1)S(1)}, u32[]{:S(2)}, u32[]{:S(2)}) collective-permute-start(f16[136,256]{1,0:T(8,128)(2,1)S(1)} %convert_element_type.72), channel_id=1, source_target_pairs={{0,2},{1,3},{2,0},{3,1},{4,6},{5,7},{6,4},{7,5},{8,10},{9,11},{10,... | collective-permute-start | bytes 208904 | tf_op jit(solution)/shard_map/ppermute | solution.py:414
  38.4 8.4 %collective-permute-start.11 = (f16[136,256]{1,0:T(8,128)(2,1)S(1)}, f16[136,256]{1,0:T(8,128)(2,1)S(1)}, u32[]{:S(2)}, u32[]{:S(2)}) collective-permute-start(f16[136,256]{1,0:T(8,128)(2,1)S(1)} %convert_element_type.70), channel_id=1, source_target_pairs={{0,1},{1,0},{2,3},{3,2},{4,5},{5,4},{6,7},{7,6},{8,9},{9,8},{10,11... | collective-permute-start | bytes 208904 | tf_op jit(solution)/shard_map/ppermute | solution.py:414
  40.3 10.5 %collective-permute-start.19 = (f16[136,256]{1,0:T(8,128)(2,1)S(1)}, f16[136,256]{1,0:T(8,128)(2,1)S(1)}, u32[]{:S(2)}, u32[]{:S(2)}) collective-permute-start(f16[136,256]{1,0:T(8,128)(2,1)S(1)} %convert_element_type.80), channel_id=1, source_target_pairs={{0,3},{1,2},{2,1},{3,0},{4,7},{5,6},{6,5},{7,4},{8,11},{9,10},{10,... | collective-permute-start | bytes 208904 | tf_op jit(solution)/shard_map/ppermute | solution.py:414
  42.9 10.9 %collective-permute-start.18 = (f16[136,256]{1,0:T(8,128)(2,1)S(1)}, f16[136,256]{1,0:T(8,128)(2,1)S(1)}, u32[]{:S(2)}, u32[]{:S(2)}) collective-permute-start(f16[136,256]{1,0:T(8,128)(2,1)S(1)} %convert_element_type.80), channel_id=1, source_target_pairs={{0,2},{1,3},{2,0},{3,1},{4,6},{5,7},{6,4},{7,5},{8,10},{9,11},{10,... | collective-permute-start | bytes 208904 | tf_op jit(solution)/shard_map/ppermute | solution.py:414
  42.9 10.9 %collective-permute-start.17 = (f16[136,256]{1,0:T(8,128)(2,1)S(1)}, f16[136,256]{1,0:T(8,128)(2,1)S(1)}, u32[]{:S(2)}, u32[]{:S(2)}) collective-permute-start(f16[136,256]{1,0:T(8,128)(2,1)S(1)} %convert_element_type.80), channel_id=1, source_target_pairs={{0,1},{1,0},{2,3},{3,2},{4,5},{5,4},{6,7},{7,6},{8,9},{9,8},{10,11... | collective-permute-start | bytes 208904 | tf_op jit(solution)/shard_map/ppermute | solution.py:414
  49.3 6.2 %collective-permute-start.16 = (f16[136,256]{1,0:T(8,128)(2,1)S(1)}, f16[136,256]{1,0:T(8,128)(2,1)S(1)}, u32[]{:S(2)}, u32[]{:S(2)}) collective-permute-start(f16[136,256]{1,0:T(8,128)(2,1)S(1)} %convert_element_type.76), channel_id=1, source_target_pairs={{0,3},{1,2},{2,1},{3,0},{4,7},{5,6},{6,5},{7,4},{8,11},{9,10},{10,... | collective-permute-start | bytes 208904 | tf_op jit(solution)/shard_map/ppermute | solution.py:414
  50.8 6.2 %collective-permute-start.15 = (f16[136,256]{1,0:T(8,128)(2,1)S(1)}, f16[136,256]{1,0:T(8,128)(2,1)S(1)}, u32[]{:S(2)}, u32[]{:S(2)}) collective-permute-start(f16[136,256]{1,0:T(8,128)(2,1)S(1)} %convert_element_type.76), channel_id=1, source_target_pairs={{0,2},{1,3},{2,0},{3,1},{4,6},{5,7},{6,4},{7,5},{8,10},{9,11},{10,... | collective-permute-start | bytes 208904 | tf_op jit(solution)/shard_map/ppermute | solution.py:414
  50.8 6.2 %collective-permute-start.14 = (f16[136,256]{1,0:T(8,128)(2,1)S(1)}, f16[136,256]{1,0:T(8,128)(2,1)S(1)}, u32[]{:S(2)}, u32[]{:S(2)}) collective-permute-start(f16[136,256]{1,0:T(8,128)(2,1)S(1)} %convert_element_type.76), channel_id=1, source_target_pairs={{0,1},{1,0},{2,3},{3,2},{4,5},{5,4},{6,7},{7,6},{8,9},{9,8},{10,11... | collective-permute-start | bytes 208904 | tf_op jit(solution)/shard_map/ppermute | solution.py:414

commit v8 on v6

--- a/solution.py
+++ b/solution.py
@@ -144,15 +144,8 @@
     fetched.wait()
     tail[...] = history[steps:]
 
-    def arrived(slot):
-        pltpu.make_async_copy(
-            kernels.at[slot], kernel_buffer.at[slot], sems.at[slot]
-        ).wait()
-
-    sum_slots(counts, scalars, history, kernel_buffer, total, span, arrived)
     for out in outs:
         out[size:] = jnp.zeros_like(out[size:])
-    write_chunks(total, outs, share, loads, size + share * couplings)
     target, source = lax.axis_index("tgt"), lax.axis_index("src")
     holds = source == target // ratio
     at = pl.multiple_of(target % ratio * rows, LANES)
@@ -169,6 +162,14 @@
                     out[row : row + 1, group * LANES : (group + 1) * LANES] = total[
                         group, pl.ds(step * loads + first + item, 1), :
                     ]
+
+    def arrived(slot):
+        pltpu.make_async_copy(
+            kernels.at[slot], kernel_buffer.at[slot], sems.at[slot]
+        ).wait()
+
+    sum_slots(counts, scalars, history, kernel_buffer, total, span, arrived)
+    write_chunks(total, outs, share, loads, size + share * couplings)
 
 
 def far_next_kernel(table, span, share, ratio, counts, offsets, tail, kernels, *refs):

time: 58.6 us -> 58.3 us (level); the launches traced: 58.7 us -> 57.6 us
  waiting for transfers between devices: 14.8 us -> 14.2 us
    ppermute x12, waiting for transfers between devices: 6.09 us -> 5.38 us  [trade(): return lax.ppermute(value, 'src', pairs)]
  transfers between devices with their start and end apart: 20 -> 20, of which waited for: 9 -> 10; matrix products, arithmetic and copies ran while one was open for 1% -> 1% of each run, Pallas kernels for 13% -> 13%
where the time goes in v8:
time: 58.3 us; the launch traced here: 57.6 us
  starting transfers between devices  25.5 us (44%)
  Pallas kernels  15.6 us (27%)
  waiting for transfers between devices  14.2 us (24%)
  between operations  1.19 us (2%)
  local copies, waits for them, and re-layouts  0.84 us (1%)
    ppermute x12, starting transfers between devices, trade(): return lax.ppermute(value, 'src', pairs)  19.2 us
    ppermute x12, waiting for transfers between devices, trade(): return lax.ppermute(value, 'src', pairs)  5.38 us
    pallas_call x2, Pallas kernels, solve(): pl.pallas_call(functools.partial(solve_kernel, steps, share, levels, len(...  4.85 us
    pallas_call x1, Pallas kernels, local(): pl.pallas_call(functools.partial(prepare_kernel, levels), out_shape=[jax....  4.36 us
    ppermute x3, starting transfers between devices, local(): arrived.append(lax.ppermute(landed, 'tgt', pairs))  4.34 us
    ppermute x1, waiting for transfers between devices, local(): landed = lax.ppermute(rounded, ('tgt', 'src'), moves)  4.19 us
    ppermute x3, waiting for transfers between devices, local(): arrived.append(lax.ppermute(landed, 'tgt', pairs))  3.4 us
    pallas_call x1, Pallas kernels, local(): pl.pallas_call(functools.partial(far_first_kernel, span, count, share, so...  2.52 us
  transfers between devices with their start and end apart: 20, of which 10 were waited for; matrix products, arithmetic and copies ran while one was open for 1% of the time, Pallas kernels for 13%

profile of v8, /device:TPU:0, one launch (start us, length us, event | category | flops | bytes accessed | tf_op | source)
XLA Modules:
  0.0 57.6 jit_solution(15362255761021113909)
XLA Ops:
  0.7 0.6 %copy-done.4 = s32[1,1,12]{2,1,0:T(1,128)S(1)} copy-done((s32[1,1,12]{2,1,0:T(1,128)S(1)}, s32[1,1,12]{2,1,0:T(1,128)}, u32[]{:S(2)}) %copy-start.4) | copy-done | bytes 72
  1.4 2.5 %far_first.1 = (f32[136,256]{1,0:T(8,128)S(1)}, f32[136,256]{1,0:T(8,128)S(1)}, f32[136,256]{1,0:T(8,128)S(1)}, f32[136,256]{1,0:T(8,128)S(1)}, bf16[12,8,512]{2,1,0:T(8,128)(2,1)S(1)}) custom-call(s32[1,1]{1,0:T(1,128)S(6)} %copy.12.counts, s32[1,1,12]{2,1,0:T(1,128)S(1)} %copy-done.4, bf16[76,8,512]{2,1,0:T(8,128)(2,1)} %past.1, bf16[8,512,256]{2,1,0:T(8,128)(2,1)} %kernels.3), custom_call_target="tpu_custom_call" | custom-call | flops 2000000000 | tf_op jit(solution)/shard_map/far_first/pallas_call | solution.py:471
  3.9 5.1 %collective-permute-start.2 = (f16[136,256]{1,0:T(8,128)(2,1)S(1)}, f16[136,256]{1,0:T(8,128)(2,1)S(1)}, u32[]{:S(2)}, u32[]{:S(2)}) collective-permute-start(f16[136,256]{1,0:T(8,128)(2,1)S(1)} %convert_element_type.68), channel_id=1, source_target_pairs={{0,3},{1,2},{2,1},{3,0},{4,7},{5,6},{6,5},{7,4},{8,11},{9,10},{10,... | collective-permute-start | bytes 208904 | tf_op jit(solution)/shard_map/ppermute | solution.py:406
  9.1 0.1 collective-permute-start.1
  9.2 0.7 %collective-permute-start = (f16[136,256]{1,0:T(8,128)(2,1)S(1)}, f16[136,256]{1,0:T(8,128)(2,1)S(1)}, u32[]{:S(2)}, u32[]{:S(2)}) collective-permute-start(f16[136,256]{1,0:T(8,128)(2,1)S(1)} %convert_element_type.64), channel_id=1, source_target_pairs={{0,1},{1,0},{2,3},{3,2},{4,5},{5,4},{6,7},{7,6},{8,9},{9,8},{10,11... | collective-permute-start | bytes 208904 | tf_op jit(solution)/shard_map/ppermute | solution.py:406
  9.8 0.1 constant_dynamic-slice_fusion
  10.0 4.4 %prepare.1 = (bf16[256,256]{1,0:T(8,128)(2,1)S(1)}, bf16[256,256]{1,0:T(8,128)(2,1)S(1)}, bf16[2,256,256]{2,1,0:T(8,128)(2,1)S(1)}, bf16[2,256,256]{2,1,0:T(8,12...) custom-call(f32[2,256,256]{2,1,0:T(8,128)S(1)} %copy-done.2, ...), custom_call_target="tpu_custom_call" | custom-call | flops 5000000000 | tf_op jit(solution)/shard_map/prepare/pallas_call | solution.py:414
  14.4 1.1 %collective-permute-done.1 = f16[136,256]{1,0:T(8,128)(2,1)S(1)} collective-permute-done((f16[136,256]{1,0:T(8,128)(2,1)S(1)}, f16[136,256]{1,0:T(8,128)(2,1)S(1)}, u32[]{:S(2)}, u32[]{:S(2)}) %collective-permute-start.1) | collective-permute-done | bytes 69664 | tf_op jit(solution)/shard_map/ppermute | solution.py:406
  15.6 2.4 %solve.2 = (f32[128,256]{1,0:T(8,128)S(1)}, f32[136,256]{1,0:T(8,128)S(1)}, bf16[128,256]{1,0:T(8,128)(2,1)S(1)}, f32[8,256]{1,0:T(8,128)S(1)}) custom-call(f32[136,256]{1,0:T(8,128)S(1)} %get-tuple-element.37.refs_0_, f32[136,256]{1,0:T(8,128)S(1)} %convert_element_type.65.refs_1_, f32[136,256]{1,0:T(8,128)S(1)} %convert_element_type.67.refs_2_, ...), custom_call_target="tpu_custom_call" | custom-call | flops 3000000000 | tf_op jit(solution)/shard_map/solve/pallas_call | solution.py:438
  18.0 2.0 %collective-permute-start.3 = (bf16[128,256]{1,0:T(8,128)(2,1)S(1)}, bf16[128,256]{1,0:T(8,128)(2,1)S(1)}, u32[]{:S(2)}, u32[]{:S(2)}) collective-permute-start(bf16[128,256]{1,0:T(8,128)(2,1)S(1)} %get-tuple-element.57), channel_id=1, source_target_pairs={{0,24},{1,16},{2,8},{3,0},{4,28},{5,20},{6,12},{7,4},{8,1},{9,17},... | collective-permute-start | bytes 196616 | tf_op jit(solution)/shard_map/ppermute | solution.py:504
  20.1 4.2 %collective-permute-done.3.refs_0_ = bf16[128,256]{1,0:T(8,128)(2,1)S(1)} collective-permute-done((bf16[128,256]{1,0:T(8,128)(2,1)S(1)}, bf16[128,256]{1,0:T(8,128)(2,1)S(1)}, u32[]{:S(2)}, u32[]{:S(2)}) %collective-permute-start.3) | collective-permute-done | bytes 65568 | tf_op jit(solution)/shard_map/ppermute | solution.py:504
  24.3 1.3 %collective-permute-start.6 = (bf16[128,256]{1,0:T(8,128)(2,1)S(1)}, bf16[128,256]{1,0:T(8,128)(2,1)S(1)}, u32[]{:S(2)}, u32[]{:S(2)}) collective-permute-start(bf16[128,256]{1,0:T(8,128)(2,1)S(1)} %collective-permute-done.3.refs_0_), channel_id=1, source_target_pairs={{0,24},{4,28},{8,16},{12,20},{16,8},{20,12},{24,0},{28,4},{1,25},{... | collective-permute-start | bytes 196616 | tf_op jit(solution)/shard_map/ppermute | solution.py:513
  25.6 2.2 %collective-permute-start.5 = (bf16[128,256]{1,0:T(8,128)(2,1)S(1)}, bf16[128,256]{1,0:T(8,128)(2,1)S(1)}, u32[]{:S(2)}, u32[]{:S(2)}) collective-permute-start(bf16[128,256]{1,0:T(8,128)(2,1)S(1)} %collective-permute-done.3.refs_0_), channel_id=1, source_target_pairs={{0,16},{4,20},{8,24},{12,28},{16,0},{20,4},{24,8},{28,12},{1,17},{... | collective-permute-start | bytes 196616 | tf_op jit(solution)/shard_map/ppermute | solution.py:513
  27.8 0.9 %collective-permute-start.4 = (bf16[128,256]{1,0:T(8,128)(2,1)S(1)}, bf16[128,256]{1,0:T(8,128)(2,1)S(1)}, u32[]{:S(2)}, u32[]{:S(2)}) collective-permute-start(bf16[128,256]{1,0:T(8,128)(2,1)S(1)} %collective-permute-done.3.refs_0_), channel_id=1, source_target_pairs={{0,8},{4,12},{8,0},{12,4},{16,24},{20,28},{24,16},{28,20},{1,9},{5... | collective-permute-start | bytes 196616 | tf_op jit(solution)/shard_map/ppermute | solution.py:513
  28.6 0.8 %collective-permute-done.6.refs_3_ = bf16[128,256]{1,0:T(8,128)(2,1)S(1)} collective-permute-done((bf16[128,256]{1,0:T(8,128)(2,1)S(1)}, bf16[128,256]{1,0:T(8,128)(2,1)S(1)}, u32[]{:S(2)}, u32[]{:S(2)}) %collective-permute-start.6) | collective-permute-done | bytes 65568 | tf_op jit(solution)/shard_map/ppermute | solution.py:513
  29.4 0.8 %collective-permute-done.5.refs_2_ = bf16[128,256]{1,0:T(8,128)(2,1)S(1)} collective-permute-done((bf16[128,256]{1,0:T(8,128)(2,1)S(1)}, bf16[128,256]{1,0:T(8,128)(2,1)S(1)}, u32[]{:S(2)}, u32[]{:S(2)}) %collective-permute-start.5) | collective-permute-done | bytes 65568 | tf_op jit(solution)/shard_map/ppermute | solution.py:513
  30.3 1.7 %collective-permute-done.4.refs_1_ = bf16[128,256]{1,0:T(8,128)(2,1)S(1)} collective-permute-done((bf16[128,256]{1,0:T(8,128)(2,1)S(1)}, bf16[128,256]{1,0:T(8,128)(2,1)S(1)}, u32[]{:S(2)}, u32[]{:S(2)}) %collective-permute-start.4) | collective-permute-done | bytes 65568 | tf_op jit(solution)/shard_map/ppermute | solution.py:513
  32.0 1.2 %collective-permute-done.8.refs_5_ = bf16[128,256]{1,0:T(8,128)(2,1)S(1)} collective-permute-done((bf16[128,256]{1,0:T(8,128)(2,1)S(1)}, bf16[128,256]{1,0:T(8,128)(2,1)S(1)}, u32[]{:S(2)}, u32[]{:S(2)}) %collective-permute-start.8) | collective-permute-done | bytes 65568 | tf_op jit(solution)/shard_map/ppermute | solution.py:521
  33.3 2.1 %far_next.1 = (f32[136,256]{1,0:T(8,128)S(1)}, f32[136,256]{1,0:T(8,128)S(1)}, f32[136,256]{1,0:T(8,128)S(1)}, f32[136,256]{1,0:T(8,128)S(1)}) custom-call(s32[1,1]{1,0:T(1,128)S(6)} %copy.12.counts, s32[1,1,12]{2,1,0:T(1,128)S(1)} %copy-done.5, bf16[12,8,512]{2,1,0:T(8,128)(2,1)S(1)} %get-tuple-element.36.tail, bf16[8,512,256]{2,1,0:T(8,128)(2,1)S(1)} %copy-done.1, ...), custom_call_target="tpu_custom_call" | custom-call | flops 3000000000 | tf_op jit(solution)/shard_map/far_next/pallas_call | solution.py:522
  35.4 2.1 %collective-permute-start.13 = (f16[136,256]{1,0:T(8,128)(2,1)S(1)}, f16[136,256]{1,0:T(8,128)(2,1)S(1)}, u32[]{:S(2)}, u32[]{:S(2)}) collective-permute-start(f16[136,256]{1,0:T(8,128)(2,1)S(1)} %convert_element_type.74), channel_id=1, source_target_pairs={{0,3},{1,2},{2,1},{3,0},{4,7},{5,6},{6,5},{7,4},{8,11},{9,10},{10,... | collective-permute-start | bytes 208904 | tf_op jit(solution)/shard_map/ppermute | solution.py:406
  37.7 2.4 %collective-permute-start.11 = (f16[136,256]{1,0:T(8,128)(2,1)S(1)}, f16[136,256]{1,0:T(8,128)(2,1)S(1)}, u32[]{:S(2)}, u32[]{:S(2)}) collective-permute-start(f16[136,256]{1,0:T(8,128)(2,1)S(1)} %convert_element_type.70), channel_id=1, source_target_pairs={{0,1},{1,0},{2,3},{3,2},{4,5},{5,4},{6,7},{7,6},{8,9},{9,8},{10,11... | collective-permute-start | bytes 208904 | tf_op jit(solution)/shard_map/ppermute | solution.py:406
  40.0 2.2 %collective-permute-start.19 = (f16[136,256]{1,0:T(8,128)(2,1)S(1)}, f16[136,256]{1,0:T(8,128)(2,1)S(1)}, u32[]{:S(2)}, u32[]{:S(2)}) collective-permute-start(f16[136,256]{1,0:T(8,128)(2,1)S(1)} %convert_element_type.80), channel_id=1, source_target_pairs={{0,3},{1,2},{2,1},{3,0},{4,7},{5,6},{6,5},{7,4},{8,11},{9,10},{10,... | collective-permute-start | bytes 208904 | tf_op jit(solution)/shard_map/ppermute | solution.py:406
  42.2 0.2 collective-permute-done.13
  42.4 2.1 %collective-permute-start.17 = (f16[136,256]{1,0:T(8,128)(2,1)S(1)}, f16[136,256]{1,0:T(8,128)(2,1)S(1)}, u32[]{:S(2)}, u32[]{:S(2)}) collective-permute-start(f16[136,256]{1,0:T(8,128)(2,1)S(1)} %convert_element_type.80), channel_id=1, source_target_pairs={{0,1},{1,0},{2,3},{3,2},{4,5},{5,4},{6,7},{7,6},{8,9},{9,8},{10,11... | collective-permute-start | bytes 208904 | tf_op jit(solution)/shard_map/ppermute | solution.py:406
  44.5 0.7 %collective-permute-done.12 = f16[136,256]{1,0:T(8,128)(2,1)S(1)} collective-permute-done((f16[136,256]{1,0:T(8,128)(2,1)S(1)}, f16[136,256]{1,0:T(8,128)(2,1)S(1)}, u32[]{:S(2)}, u32[]{:S(2)}) %collective-permute-start.12) | collective-permute-done | bytes 69664 | tf_op jit(solution)/shard_map/ppermute | solution.py:406
  45.3 2.4 %solve.3 = (f32[128,256]{1,0:T(8,128)S(1)}, f32[136,256]{1,0:T(8,128)S(1)}) custom-call(f32[136,256]{1,0:T(8,128)S(1)} %get-tuple-element.58.refs_0_, f32[136,256]{1,0:T(8,128)S(1)} %convert_element_type.71.refs_1_, f32[136,256]{1,0:T(8,128)S(1)} %convert_element_type.73.refs_2_, f32[136,256]{1,0:T(8,128)S(1)} %convert_element_type.75.refs_3_, ...), custom_call_target="tpu_custom_call" | custom-call | flops 3000000000 | tf_op jit(solution)/shard_map/solve/pallas_call | solution.py:438
  47.7 2.3 %collective-permute-start.16 = (f16[136,256]{1,0:T(8,128)(2,1)S(1)}, f16[136,256]{1,0:T(8,128)(2,1)S(1)}, u32[]{:S(2)}, u32[]{:S(2)}) collective-permute-start(f16[136,256]{1,0:T(8,128)(2,1)S(1)} %convert_element_type.76), channel_id=1, source_target_pairs={{0,3},{1,2},{2,1},{3,0},{4,7},{5,6},{6,5},{7,4},{8,11},{9,10},{10,... | collective-permute-start | bytes 208904 | tf_op jit(solution)/shard_map/ppermute | solution.py:406
  50.0 2.1 %collective-permute-start.14 = (f16[136,256]{1,0:T(8,128)(2,1)S(1)}, f16[136,256]{1,0:T(8,128)(2,1)S(1)}, u32[]{:S(2)}, u32[]{:S(2)}) collective-permute-start(f16[136,256]{1,0:T(8,128)(2,1)S(1)} %convert_element_type.76), channel_id=1, source_target_pairs={{0,1},{1,0},{2,3},{3,2},{4,5},{5,4},{6,7},{7,6},{8,9},{9,8},{10,11... | collective-permute-start | bytes 208904 | tf_op jit(solution)/shard_map/ppermute | solution.py:406
  52.2 0.9 %spread.2.refs_3_ = f32[128,8,256]{2,1,0:T(8,128)} custom-call(f32[128,256]{1,0:T(8,128)S(1)} %get-tuple-element.65.own, f32[136,256]{1,0:T(8,128)S(1)} %convert_element_type.81.refs_0_, f32[136,256]{1,0:T(8,128)S(1)} %convert_element_type.82.refs_1_, f32[136,256]{1,0:T(8,128)S(1)} %convert_element_type.83.refs_2_), custom_call_target="tpu_custom_call" | custom-call | tf_op jit(solution)/shard_map/spread/pallas_call | solution.py:450
  53.1 1.3 %collective-permute-done.16 = f16[136,256]{1,0:T(8,128)(2,1)S(1)} collective-permute-done((f16[136,256]{1,0:T(8,128)(2,1)S(1)}, f16[136,256]{1,0:T(8,128)(2,1)S(1)}, u32[]{:S(2)}, u32[]{:S(2)}) %collective-permute-start.16) | collective-permute-done | bytes 69664 | tf_op jit(solution)/shard_map/ppermute | solution.py:406
  54.5 2.1 %collective-permute-done.15 = f16[136,256]{1,0:T(8,128)(2,1)S(1)} collective-permute-done((f16[136,256]{1,0:T(8,128)(2,1)S(1)}, f16[136,256]{1,0:T(8,128)(2,1)S(1)}, u32[]{:S(2)}, u32[]{:S(2)}) %collective-permute-start.15) | collective-permute-done | bytes 69664 | tf_op jit(solution)/shard_map/ppermute | solution.py:406
  56.6 0.9 %spread.3 = f32[128,8,256]{2,1,0:T(8,128)} custom-call(f32[128,256]{1,0:T(8,128)S(1)} %get-tuple-element.63.own, f32[136,256]{1,0:T(8,128)S(1)} %convert_element_type.77.refs_0_, f32[136,256]{1,0:T(8,128)S(1)} %convert_element_type.78.refs_1_, f32[136,256]{1,0:T(8,128)S(1)} %convert_element_type.79.refs_2_, ...), custom_call_target="tpu_custom_call", output_to_operand_aliasing={{}: (4, {})} | custom-call | tf_op jit(solution)/shard_map/spread/pallas_call | solution.py:450
  (51 shorter events, 0.4 us)
Async XLA Ops:
  0.0 9.8 %copy-start = (bf16[128,8,256]{2,1,0:T(8,128)(2,1)S(1)}, bf16[128,8,256]{2,1,0:T(8,128)(2,1)}, u32[]{:S(2)}) copy-start(bf16[128,8,256]{2,1,0:T(8,128)(2,1)} %param.7) | copy-start | bytes 1572868
  0.7 0.7 %copy-start.4 = (s32[1,1,12]{2,1,0:T(1,128)S(1)}, s32[1,1,12]{2,1,0:T(1,128)}, u32[]{:S(2)}) copy-start(s32[1,1,12]{2,1,0:T(1,128)} %offsets.3) | copy-start | bytes 148
  1.4 8.6 %copy-start.2 = (f32[2,256,256]{2,1,0:T(8,128)S(1)}, f32[2,256,256]{2,1,0:T(8,128)}, u32[]{:S(2)}) copy-start(f32[2,256,256]{2,1,0:T(8,128)} %couplings.1) | copy-start | bytes 1572868
  1.4 8.6 %copy-start.3 = (f32[256,256]{1,0:T(8,128)S(1)}, f32[256,256]{1,0:T(8,128)}, u32[]{:S(2)}) copy-start(f32[256,256]{1,0:T(8,128)} %inverse.1) | copy-start | bytes 786436
  3.9 10.5 %collective-permute-start.2 = (f16[136,256]{1,0:T(8,128)(2,1)S(1)}, f16[136,256]{1,0:T(8,128)(2,1)S(1)}, u32[]{:S(2)}, u32[]{:S(2)}) collective-permute-start(f16[136,256]{1,0:T(8,128)(2,1)S(1)} %convert_element_type.68), channel_id=1, source_target_pairs={{0,3},{1,2},{2,1},{3,0},{4,7},{5,6},{6,5},{7,4},{8,11},{9,10},{10,... | collective-permute-start | bytes 208904 | tf_op jit(solution)/shard_map/ppermute | solution.py:406
  9.1 6.5 %collective-permute-start.1 = (f16[136,256]{1,0:T(8,128)(2,1)S(1)}, f16[136,256]{1,0:T(8,128)(2,1)S(1)}, u32[]{:S(2)}, u32[]{:S(2)}) collective-permute-start(f16[136,256]{1,0:T(8,128)(2,1)S(1)} %convert_element_type.66), channel_id=1, source_target_pairs={{0,2},{1,3},{2,0},{3,1},{4,6},{5,7},{6,4},{7,5},{8,10},{9,11},{10,... | collective-permute-start | bytes 208904 | tf_op jit(solution)/shard_map/ppermute | solution.py:406
  9.2 6.4 %collective-permute-start = (f16[136,256]{1,0:T(8,128)(2,1)S(1)}, f16[136,256]{1,0:T(8,128)(2,1)S(1)}, u32[]{:S(2)}, u32[]{:S(2)}) collective-permute-start(f16[136,256]{1,0:T(8,128)(2,1)S(1)} %convert_element_type.64), channel_id=1, source_target_pairs={{0,1},{1,0},{2,3},{3,2},{4,5},{5,4},{6,7},{7,6},{8,9},{9,8},{10,11... | collective-permute-start | bytes 208904 | tf_op jit(solution)/shard_map/ppermute | solution.py:406
  15.6 17.7 %copy-start.1 = (bf16[8,512,256]{2,1,0:T(8,128)(2,1)S(1)}, bf16[8,512,256]{2,1,0:T(8,128)(2,1)}, u32[]{:S(2)}) copy-start(bf16[8,512,256]{2,1,0:T(8,128)(2,1)} %kernels.3) | copy-start | bytes 6291460
  15.6 17.7 %copy-start.5 = (s32[1,1,12]{2,1,0:T(1,128)S(1)}, s32[1,1,12]{2,1,0:T(1,128)}, u32[]{:S(2)}) copy-start(s32[1,1,12]{2,1,0:T(1,128)} %offsets.3) | copy-start | bytes 148
  18.0 6.2 %collective-permute-start.3 = (bf16[128,256]{1,0:T(8,128)(2,1)S(1)}, bf16[128,256]{1,0:T(8,128)(2,1)S(1)}, u32[]{:S(2)}, u32[]{:S(2)}) collective-permute-start(bf16[128,256]{1,0:T(8,128)(2,1)S(1)} %get-tuple-element.57), channel_id=1, source_target_pairs={{0,24},{1,16},{2,8},{3,0},{4,28},{5,20},{6,12},{7,4},{8,1},{9,17},... | collective-permute-start | bytes 196616 | tf_op jit(solution)/shard_map/ppermute | solution.py:504
  24.3 5.2 %collective-permute-start.6 = (bf16[128,256]{1,0:T(8,128)(2,1)S(1)}, bf16[128,256]{1,0:T(8,128)(2,1)S(1)}, u32[]{:S(2)}, u32[]{:S(2)}) collective-permute-start(bf16[128,256]{1,0:T(8,128)(2,1)S(1)} %collective-permute-done.3.refs_0_), channel_id=1, source_target_pairs={{0,24},{4,28},{8,16},{12,20},{16,8},{20,12},{24,0},{28,4},{1,25},{... | collective-permute-start | bytes 196616 | tf_op jit(solution)/shard_map/ppermute | solution.py:513
  25.6 4.7 %collective-permute-start.5 = (bf16[128,256]{1,0:T(8,128)(2,1)S(1)}, bf16[128,256]{1,0:T(8,128)(2,1)S(1)}, u32[]{:S(2)}, u32[]{:S(2)}) collective-permute-start(bf16[128,256]{1,0:T(8,128)(2,1)S(1)} %collective-permute-done.3.refs_0_), channel_id=1, source_target_pairs={{0,16},{4,20},{8,24},{12,28},{16,0},{20,4},{24,8},{28,12},{1,17},{... | collective-permute-start | bytes 196616 | tf_op jit(solution)/shard_map/ppermute | solution.py:513
  27.8 4.3 %collective-permute-start.4 = (bf16[128,256]{1,0:T(8,128)(2,1)S(1)}, bf16[128,256]{1,0:T(8,128)(2,1)S(1)}, u32[]{:S(2)}, u32[]{:S(2)}) collective-permute-start(bf16[128,256]{1,0:T(8,128)(2,1)S(1)} %collective-permute-done.3.refs_0_), channel_id=1, source_target_pairs={{0,8},{4,12},{8,0},{12,4},{16,24},{20,28},{24,16},{28,20},{1,9},{5... | collective-permute-start | bytes 196616 | tf_op jit(solution)/shard_map/ppermute | solution.py:513
  28.6 3.4 %collective-permute-start.7 = (bf16[128,256]{1,0:T(8,128)(2,1)S(1)}, bf16[128,256]{1,0:T(8,128)(2,1)S(1)}, u32[]{:S(2)}, u32[]{:S(2)}) collective-permute-start(bf16[128,256]{1,0:T(8,128)(2,1)S(1)} %collective-permute-done.3.refs_0_), channel_id=1, source_target_pairs={{0,4},{4,0},{8,12},{12,8},{16,20},{20,16},{24,28},{28,24},{1,5},{5... | collective-permute-start | bytes 196616 | tf_op jit(solution)/shard_map/ppermute | solution.py:521
  29.4 2.6 %collective-permute-start.10 = (bf16[128,256]{1,0:T(8,128)(2,1)S(1)}, bf16[128,256]{1,0:T(8,128)(2,1)S(1)}, u32[]{:S(2)}, u32[]{:S(2)}) collective-permute-start(bf16[128,256]{1,0:T(8,128)(2,1)S(1)} %collective-permute-done.6.refs_3_), channel_id=1, source_target_pairs={{0,4},{4,0},{8,12},{12,8},{16,20},{20,16},{24,28},{28,24},{1,5},{5... | collective-permute-start | bytes 196616 | tf_op jit(solution)/shard_map/ppermute | solution.py:521
  30.3 1.8 %collective-permute-start.9 = (bf16[128,256]{1,0:T(8,128)(2,1)S(1)}, bf16[128,256]{1,0:T(8,128)(2,1)S(1)}, u32[]{:S(2)}, u32[]{:S(2)}) collective-permute-start(bf16[128,256]{1,0:T(8,128)(2,1)S(1)} %collective-permute-done.5.refs_2_), channel_id=1, source_target_pairs={{0,4},{4,0},{8,12},{12,8},{16,20},{20,16},{24,28},{28,24},{1,5},{5... | collective-permute-start | bytes 196616 | tf_op jit(solution)/shard_map/ppermute | solution.py:521
  32.0 1.3 %collective-permute-start.8 = (bf16[128,256]{1,0:T(8,128)(2,1)S(1)}, bf16[128,256]{1,0:T(8,128)(2,1)S(1)}, u32[]{:S(2)}, u32[]{:S(2)}) collective-permute-start(bf16[128,256]{1,0:T(8,128)(2,1)S(1)} %collective-permute-done.4.refs_1_), channel_id=1, source_target_pairs={{0,4},{4,0},{8,12},{12,8},{16,20},{20,16},{24,28},{28,24},{1,5},{5... | collective-permute-start | bytes 196616 | tf_op jit(solution)/shard_map/ppermute | solution.py:521
  35.4 6.9 %collective-permute-start.13 = (f16[136,256]{1,0:T(8,128)(2,1)S(1)}, f16[136,256]{1,0:T(8,128)(2,1)S(1)}, u32[]{:S(2)}, u32[]{:S(2)}) collective-permute-start(f16[136,256]{1,0:T(8,128)(2,1)S(1)} %convert_element_type.74), channel_id=1, source_target_pairs={{0,3},{1,2},{2,1},{3,0},{4,7},{5,6},{6,5},{7,4},{8,11},{9,10},{10,... | collective-permute-start | bytes 208904 | tf_op jit(solution)/shard_map/ppermute | solution.py:406
  37.6 7.7 %collective-permute-start.12 = (f16[136,256]{1,0:T(8,128)(2,1)S(1)}, f16[136,256]{1,0:T(8,128)(2,1)S(1)}, u32[]{:S(2)}, u32[]{:S(2)}) collective-permute-start(f16[136,256]{1,0:T(8,128)(2,1)S(1)} %convert_element_type.72), channel_id=1, source_target_pairs={{0,2},{1,3},{2,0},{3,1},{4,6},{5,7},{6,4},{7,5},{8,10},{9,11},{10,... | collective-permute-start | bytes 208904 | tf_op jit(solution)/shard_map/ppermute | solution.py:406
  37.7 7.6 %collective-permute-start.11 = (f16[136,256]{1,0:T(8,128)(2,1)S(1)}, f16[136,256]{1,0:T(8,128)(2,1)S(1)}, u32[]{:S(2)}, u32[]{:S(2)}) collective-permute-start(f16[136,256]{1,0:T(8,128)(2,1)S(1)} %convert_element_type.70), channel_id=1, source_target_pairs={{0,1},{1,0},{2,3},{3,2},{4,5},{5,4},{6,7},{7,6},{8,9},{9,8},{10,11... | collective-permute-start | bytes 208904 | tf_op jit(solution)/shard_map/ppermute | solution.py:406
  40.0 10.0 %collective-permute-start.19 = (f16[136,256]{1,0:T(8,128)(2,1)S(1)}, f16[136,256]{1,0:T(8,128)(2,1)S(1)}, u32[]{:S(2)}, u32[]{:S(2)}) collective-permute-start(f16[136,256]{1,0:T(8,128)(2,1)S(1)} %convert_element_type.80), channel_id=1, source_target_pairs={{0,3},{1,2},{2,1},{3,0},{4,7},{5,6},{6,5},{7,4},{8,11},{9,10},{10,... | collective-permute-start | bytes 208904 | tf_op jit(solution)/shard_map/ppermute | solution.py:406
  42.2 10.0 %collective-permute-start.18 = (f16[136,256]{1,0:T(8,128)(2,1)S(1)}, f16[136,256]{1,0:T(8,128)(2,1)S(1)}, u32[]{:S(2)}, u32[]{:S(2)}) collective-permute-start(f16[136,256]{1,0:T(8,128)(2,1)S(1)} %convert_element_type.80), channel_id=1, source_target_pairs={{0,2},{1,3},{2,0},{3,1},{4,6},{5,7},{6,4},{7,5},{8,10},{9,11},{10,... | collective-permute-start | bytes 208904 | tf_op jit(solution)/shard_map/ppermute | solution.py:406
  42.4 9.9 %collective-permute-start.17 = (f16[136,256]{1,0:T(8,128)(2,1)S(1)}, f16[136,256]{1,0:T(8,128)(2,1)S(1)}, u32[]{:S(2)}, u32[]{:S(2)}) collective-permute-start(f16[136,256]{1,0:T(8,128)(2,1)S(1)} %convert_element_type.80), channel_id=1, source_target_pairs={{0,1},{1,0},{2,3},{3,2},{4,5},{5,4},{6,7},{7,6},{8,9},{9,8},{10,11... | collective-permute-start | bytes 208904 | tf_op jit(solution)/shard_map/ppermute | solution.py:406
  47.7 6.7 %collective-permute-start.16 = (f16[136,256]{1,0:T(8,128)(2,1)S(1)}, f16[136,256]{1,0:T(8,128)(2,1)S(1)}, u32[]{:S(2)}, u32[]{:S(2)}) collective-permute-start(f16[136,256]{1,0:T(8,128)(2,1)S(1)} %convert_element_type.76), channel_id=1, source_target_pairs={{0,3},{1,2},{2,1},{3,0},{4,7},{5,6},{6,5},{7,4},{8,11},{9,10},{10,... | collective-permute-start | bytes 208904 | tf_op jit(solution)/shard_map/ppermute | solution.py:406
  50.0 6.5 %collective-permute-start.15 = (f16[136,256]{1,0:T(8,128)(2,1)S(1)}, f16[136,256]{1,0:T(8,128)(2,1)S(1)}, u32[]{:S(2)}, u32[]{:S(2)}) collective-permute-start(f16[136,256]{1,0:T(8,128)(2,1)S(1)} %convert_element_type.76), channel_id=1, source_target_pairs={{0,2},{1,3},{2,0},{3,1},{4,6},{5,7},{6,4},{7,5},{8,10},{9,11},{10,... | collective-permute-start | bytes 208904 | tf_op jit(solution)/shard_map/ppermute | solution.py:406
  50.0 6.5 %collective-permute-start.14 = (f16[136,256]{1,0:T(8,128)(2,1)S(1)}, f16[136,256]{1,0:T(8,128)(2,1)S(1)}, u32[]{:S(2)}, u32[]{:S(2)}) collective-permute-start(f16[136,256]{1,0:T(8,128)(2,1)S(1)} %convert_element_type.76), channel_id=1, source_target_pairs={{0,1},{1,0},{2,3},{3,2},{4,5},{5,4},{6,7},{7,6},{8,9},{9,8},{10,11... | collective-permute-start | bytes 208904 | tf_op jit(solution)/shard_map/ppermute | solution.py:406
